TPU v7x, 512 devices: a whole 4x8x8 slice. The times are simulated.
512 devices in a mesh: snap: 64 (over y, z_lo, core), space: 8 (over x, z_hi).
Axes of the slice: x: 4, y: 8, z: 8 (z_hi: 2, z_lo: 4; z = z_hi * 4 + z_lo), core: 2. Of those that a mesh axis runs over, the one named last changes fastest.
Arguments:
- snapshots: bfloat16 [8192, 12288], P('snap', 'space'), may hold values from -6 to 6
- counts: int32 [64], P('snap'), may hold values from 1 to 128, 6144 in all
- weights: float32 [12288], P('space'), may hold values from 0.2 to 5
Outputs:
- gram: float32 [64, 33, 128, 128], P('snap', None, 'space')
Inputs may be any that keep to these rules, and one draw needn't show every extreme that they name: The counts of all blocks sum to 6144, and some block is full.
All inputs are finite; a program needn't handle non-finite values.
Results may differ from a plain program's by a relative error of at most 0.0016.
Values may be sent and summed in bfloat16 or wider, within the bound.
No kernel may reach another device: no remote copies, remote signals or barrier semaphores. Data moves between devices by JAX's collectives and lax.ppermute only.
A program may use at most 64 MiB of HBM per device.

v0:
```python
import math

import jax
import jax.numpy as jnp
from jax import lax
from jax.sharding import PartitionSpec as P


def from_behind(x, axis, by):
    peers = lax.axis_size(axis)
    return lax.ppermute(x, axis, [(i, (i + by) % peers) for i in range(peers)])


def product(left_rows, right_rows):
    return lax.dot_general(
        left_rows, right_rows, (((1,), (1,)), ((), ())), preferred_element_type=jnp.float32
    )


def on_device(snapshots, counts, weights):
    slot_index = lax.broadcasted_iota(jnp.int32, (snapshots.shape[0], 1), 0)
    masked = jnp.where(slot_index < counts[0], snapshots, jnp.zeros_like(snapshots))
    weighted = (masked.astype(jnp.float32) * weights[None, :]).astype(jnp.bfloat16)
    offsets = lax.axis_size("snap") // 2 + 1

    def advance(current, unused):
        tile_now = product(weighted, current)
        following = from_behind(current, "snap", -1)
        return (following, tile_now)

    last_block, tile_list = lax.scan(advance, masked, None, length=offsets - 1)
    tile_set = jnp.concatenate([tile_list, product(weighted, last_block)[None]], axis=0)
    parts_count = lax.axis_size("space")
    factor = 1.0 / math.sqrt(snapshots.shape[1] * parts_count)
    summed = lax.psum(tile_set, "space")
    share = tile_set.shape[1] // parts_count
    position = lax.axis_index("space")
    own_rows = lax.dynamic_slice_in_dim(summed, position * share, share, 1)
    return (own_rows * factor)[None]


def solution(mesh):
    in_specs = (P("snap", "space"), P("snap"), P("space"))
    out_specs = P("snap", None, "space", None)
    return jax.shard_map(
        on_device, mesh=mesh, in_specs=in_specs, out_specs=out_specs, check_vma=False
    )
```

profile of v0, /device:TPU:56, one launch (start us, length us, event | category | flops | bytes accessed | tf_op | source)
XLA Modules:
  0.0 643.8 jit_solution(12296832418475375419)
XLA Ops:
  8.4 380.0 %while.12 = (s32[]{:T(128)}, bf16[128,1536]{1,0:T(8,128)(2,1)S(1)}, f32[32,128,128]{2,1,0:T(8,128)S(1)}, bf16[128,1536]{1,0:T(8,128)(2,1)S(1)}, s32[]{:T(128)}) while((s32[]{:T(128)}, bf16[128,1536]{1,0:T(8,128)(2,1)S(1)}, f32[32,128,128]{2,1,0:T(8,128)S(1)}, bf16[128,1536]{1,0:T(8,128)(2,1)S(1)}, s32[]{:T(128)}) %tuple.19), condition=%wide.region_1.2_spmd, body=%wide.region_0.1_spmd.sunk | while | flops 50331648 | bytes 3211377 | solution.py:31
  8.4 8.1 %collective-permute-start = (bf16[128,1536]{1,0:T(8,128)(2,1)S(1)}, bf16[128,1536]{1,0:T(8,128)(2,1)S(1)}, u32[]{:S(2)}, u32[]{:S(2)}) collective-permute-start(bf16[128,1536]{1,0:T(8,128)(2,1)S(1)} %copy.9), channel_id=1, source_target_pairs={{0,504},{8,0},{16,8},{24,16},{32,24},{40,32},{48,40},{56,48},{64,5... | collective-permute-start | bytes 1179656 | tf_op jit(solution)/shard_map/while/body/eval_jaxpr/ppermute | solution.py:11
  16.8 5.0 collective-permute-done
  21.9 6.5 %collective-permute-start = (bf16[128,1536]{1,0:T(8,128)(2,1)S(1)}, bf16[128,1536]{1,0:T(8,128)(2,1)S(1)}, u32[]{:S(2)}, u32[]{:S(2)}) collective-permute-start(bf16[128,1536]{1,0:T(8,128)(2,1)S(1)} %copy.9), channel_id=1, source_target_pairs={{0,504},{8,0},{16,8},{24,16},{32,24},{40,32},{48,40},{56,48},{64,5... | collective-permute-start | bytes 1179656 | tf_op jit(solution)/shard_map/while/body/eval_jaxpr/ppermute | solution.py:11
  28.7 5.0 collective-permute-done
  33.7 6.5 %collective-permute-start = (bf16[128,1536]{1,0:T(8,128)(2,1)S(1)}, bf16[128,1536]{1,0:T(8,128)(2,1)S(1)}, u32[]{:S(2)}, u32[]{:S(2)}) collective-permute-start(bf16[128,1536]{1,0:T(8,128)(2,1)S(1)} %copy.9), channel_id=1, source_target_pairs={{0,504},{8,0},{16,8},{24,16},{32,24},{40,32},{48,40},{56,48},{64,5... | collective-permute-start | bytes 1179656 | tf_op jit(solution)/shard_map/while/body/eval_jaxpr/ppermute | solution.py:11
  40.5 5.0 collective-permute-done
  45.5 6.5 %collective-permute-start = (bf16[128,1536]{1,0:T(8,128)(2,1)S(1)}, bf16[128,1536]{1,0:T(8,128)(2,1)S(1)}, u32[]{:S(2)}, u32[]{:S(2)}) collective-permute-start(bf16[128,1536]{1,0:T(8,128)(2,1)S(1)} %copy.9), channel_id=1, source_target_pairs={{0,504},{8,0},{16,8},{24,16},{32,24},{40,32},{48,40},{56,48},{64,5... | collective-permute-start | bytes 1179656 | tf_op jit(solution)/shard_map/while/body/eval_jaxpr/ppermute | solution.py:11
  52.3 5.0 collective-permute-done
  57.3 6.5 %collective-permute-start = (bf16[128,1536]{1,0:T(8,128)(2,1)S(1)}, bf16[128,1536]{1,0:T(8,128)(2,1)S(1)}, u32[]{:S(2)}, u32[]{:S(2)}) collective-permute-start(bf16[128,1536]{1,0:T(8,128)(2,1)S(1)} %copy.9), channel_id=1, source_target_pairs={{0,504},{8,0},{16,8},{24,16},{32,24},{40,32},{48,40},{56,48},{64,5... | collective-permute-start | bytes 1179656 | tf_op jit(solution)/shard_map/while/body/eval_jaxpr/ppermute | solution.py:11
  64.1 5.0 collective-permute-done
  69.2 6.5 %collective-permute-start = (bf16[128,1536]{1,0:T(8,128)(2,1)S(1)}, bf16[128,1536]{1,0:T(8,128)(2,1)S(1)}, u32[]{:S(2)}, u32[]{:S(2)}) collective-permute-start(bf16[128,1536]{1,0:T(8,128)(2,1)S(1)} %copy.9), channel_id=1, source_target_pairs={{0,504},{8,0},{16,8},{24,16},{32,24},{40,32},{48,40},{56,48},{64,5... | collective-permute-start | bytes 1179656 | tf_op jit(solution)/shard_map/while/body/eval_jaxpr/ppermute | solution.py:11
  76.0 5.0 collective-permute-done
  81.0 6.5 %collective-permute-start = (bf16[128,1536]{1,0:T(8,128)(2,1)S(1)}, bf16[128,1536]{1,0:T(8,128)(2,1)S(1)}, u32[]{:S(2)}, u32[]{:S(2)}) collective-permute-start(bf16[128,1536]{1,0:T(8,128)(2,1)S(1)} %copy.9), channel_id=1, source_target_pairs={{0,504},{8,0},{16,8},{24,16},{32,24},{40,32},{48,40},{56,48},{64,5... | collective-permute-start | bytes 1179656 | tf_op jit(solution)/shard_map/while/body/eval_jaxpr/ppermute | solution.py:11
  87.8 5.0 collective-permute-done
  92.8 6.5 %collective-permute-start = (bf16[128,1536]{1,0:T(8,128)(2,1)S(1)}, bf16[128,1536]{1,0:T(8,128)(2,1)S(1)}, u32[]{:S(2)}, u32[]{:S(2)}) collective-permute-start(bf16[128,1536]{1,0:T(8,128)(2,1)S(1)} %copy.9), channel_id=1, source_target_pairs={{0,504},{8,0},{16,8},{24,16},{32,24},{40,32},{48,40},{56,48},{64,5... | collective-permute-start | bytes 1179656 | tf_op jit(solution)/shard_map/while/body/eval_jaxpr/ppermute | solution.py:11
  99.6 5.0 collective-permute-done
  104.6 6.5 %collective-permute-start = (bf16[128,1536]{1,0:T(8,128)(2,1)S(1)}, bf16[128,1536]{1,0:T(8,128)(2,1)S(1)}, u32[]{:S(2)}, u32[]{:S(2)}) collective-permute-start(bf16[128,1536]{1,0:T(8,128)(2,1)S(1)} %copy.9), channel_id=1, source_target_pairs={{0,504},{8,0},{16,8},{24,16},{32,24},{40,32},{48,40},{56,48},{64,5... | collective-permute-start | bytes 1179656 | tf_op jit(solution)/shard_map/while/body/eval_jaxpr/ppermute | solution.py:11
  111.4 5.0 collective-permute-done
  116.5 6.5 %collective-permute-start = (bf16[128,1536]{1,0:T(8,128)(2,1)S(1)}, bf16[128,1536]{1,0:T(8,128)(2,1)S(1)}, u32[]{:S(2)}, u32[]{:S(2)}) collective-permute-start(bf16[128,1536]{1,0:T(8,128)(2,1)S(1)} %copy.9), channel_id=1, source_target_pairs={{0,504},{8,0},{16,8},{24,16},{32,24},{40,32},{48,40},{56,48},{64,5... | collective-permute-start | bytes 1179656 | tf_op jit(solution)/shard_map/while/body/eval_jaxpr/ppermute | solution.py:11
  123.3 5.0 collective-permute-done
  128.3 6.5 %collective-permute-start = (bf16[128,1536]{1,0:T(8,128)(2,1)S(1)}, bf16[128,1536]{1,0:T(8,128)(2,1)S(1)}, u32[]{:S(2)}, u32[]{:S(2)}) collective-permute-start(bf16[128,1536]{1,0:T(8,128)(2,1)S(1)} %copy.9), channel_id=1, source_target_pairs={{0,504},{8,0},{16,8},{24,16},{32,24},{40,32},{48,40},{56,48},{64,5... | collective-permute-start | bytes 1179656 | tf_op jit(solution)/shard_map/while/body/eval_jaxpr/ppermute | solution.py:11
  135.1 5.0 collective-permute-done
  140.1 6.5 %collective-permute-start = (bf16[128,1536]{1,0:T(8,128)(2,1)S(1)}, bf16[128,1536]{1,0:T(8,128)(2,1)S(1)}, u32[]{:S(2)}, u32[]{:S(2)}) collective-permute-start(bf16[128,1536]{1,0:T(8,128)(2,1)S(1)} %copy.9), channel_id=1, source_target_pairs={{0,504},{8,0},{16,8},{24,16},{32,24},{40,32},{48,40},{56,48},{64,5... | collective-permute-start | bytes 1179656 | tf_op jit(solution)/shard_map/while/body/eval_jaxpr/ppermute | solution.py:11
  146.9 5.0 collective-permute-done
  151.9 6.5 %collective-permute-start = (bf16[128,1536]{1,0:T(8,128)(2,1)S(1)}, bf16[128,1536]{1,0:T(8,128)(2,1)S(1)}, u32[]{:S(2)}, u32[]{:S(2)}) collective-permute-start(bf16[128,1536]{1,0:T(8,128)(2,1)S(1)} %copy.9), channel_id=1, source_target_pairs={{0,504},{8,0},{16,8},{24,16},{32,24},{40,32},{48,40},{56,48},{64,5... | collective-permute-start | bytes 1179656 | tf_op jit(solution)/shard_map/while/body/eval_jaxpr/ppermute | solution.py:11
  158.7 5.0 collective-permute-done
  163.8 6.5 %collective-permute-start = (bf16[128,1536]{1,0:T(8,128)(2,1)S(1)}, bf16[128,1536]{1,0:T(8,128)(2,1)S(1)}, u32[]{:S(2)}, u32[]{:S(2)}) collective-permute-start(bf16[128,1536]{1,0:T(8,128)(2,1)S(1)} %copy.9), channel_id=1, source_target_pairs={{0,504},{8,0},{16,8},{24,16},{32,24},{40,32},{48,40},{56,48},{64,5... | collective-permute-start | bytes 1179656 | tf_op jit(solution)/shard_map/while/body/eval_jaxpr/ppermute | solution.py:11
  170.5 5.0 collective-permute-done
  175.6 6.5 %collective-permute-start = (bf16[128,1536]{1,0:T(8,128)(2,1)S(1)}, bf16[128,1536]{1,0:T(8,128)(2,1)S(1)}, u32[]{:S(2)}, u32[]{:S(2)}) collective-permute-start(bf16[128,1536]{1,0:T(8,128)(2,1)S(1)} %copy.9), channel_id=1, source_target_pairs={{0,504},{8,0},{16,8},{24,16},{32,24},{40,32},{48,40},{56,48},{64,5... | collective-permute-start | bytes 1179656 | tf_op jit(solution)/shard_map/while/body/eval_jaxpr/ppermute | solution.py:11
  182.4 5.0 collective-permute-done
  187.4 6.5 %collective-permute-start = (bf16[128,1536]{1,0:T(8,128)(2,1)S(1)}, bf16[128,1536]{1,0:T(8,128)(2,1)S(1)}, u32[]{:S(2)}, u32[]{:S(2)}) collective-permute-start(bf16[128,1536]{1,0:T(8,128)(2,1)S(1)} %copy.9), channel_id=1, source_target_pairs={{0,504},{8,0},{16,8},{24,16},{32,24},{40,32},{48,40},{56,48},{64,5... | collective-permute-start | bytes 1179656 | tf_op jit(solution)/shard_map/while/body/eval_jaxpr/ppermute | solution.py:11
  194.2 5.0 collective-permute-done
  199.2 6.5 %collective-permute-start = (bf16[128,1536]{1,0:T(8,128)(2,1)S(1)}, bf16[128,1536]{1,0:T(8,128)(2,1)S(1)}, u32[]{:S(2)}, u32[]{:S(2)}) collective-permute-start(bf16[128,1536]{1,0:T(8,128)(2,1)S(1)} %copy.9), channel_id=1, source_target_pairs={{0,504},{8,0},{16,8},{24,16},{32,24},{40,32},{48,40},{56,48},{64,5... | collective-permute-start | bytes 1179656 | tf_op jit(solution)/shard_map/while/body/eval_jaxpr/ppermute | solution.py:11
  206.0 5.0 collective-permute-done
  211.0 6.5 %collective-permute-start = (bf16[128,1536]{1,0:T(8,128)(2,1)S(1)}, bf16[128,1536]{1,0:T(8,128)(2,1)S(1)}, u32[]{:S(2)}, u32[]{:S(2)}) collective-permute-start(bf16[128,1536]{1,0:T(8,128)(2,1)S(1)} %copy.9), channel_id=1, source_target_pairs={{0,504},{8,0},{16,8},{24,16},{32,24},{40,32},{48,40},{56,48},{64,5... | collective-permute-start | bytes 1179656 | tf_op jit(solution)/shard_map/while/body/eval_jaxpr/ppermute | solution.py:11
  217.8 5.0 collective-permute-done
  222.9 6.5 %collective-permute-start = (bf16[128,1536]{1,0:T(8,128)(2,1)S(1)}, bf16[128,1536]{1,0:T(8,128)(2,1)S(1)}, u32[]{:S(2)}, u32[]{:S(2)}) collective-permute-start(bf16[128,1536]{1,0:T(8,128)(2,1)S(1)} %copy.9), channel_id=1, source_target_pairs={{0,504},{8,0},{16,8},{24,16},{32,24},{40,32},{48,40},{56,48},{64,5... | collective-permute-start | bytes 1179656 | tf_op jit(solution)/shard_map/while/body/eval_jaxpr/ppermute | solution.py:11
  229.7 5.0 collective-permute-done
  234.7 6.5 %collective-permute-start = (bf16[128,1536]{1,0:T(8,128)(2,1)S(1)}, bf16[128,1536]{1,0:T(8,128)(2,1)S(1)}, u32[]{:S(2)}, u32[]{:S(2)}) collective-permute-start(bf16[128,1536]{1,0:T(8,128)(2,1)S(1)} %copy.9), channel_id=1, source_target_pairs={{0,504},{8,0},{16,8},{24,16},{32,24},{40,32},{48,40},{56,48},{64,5... | collective-permute-start | bytes 1179656 | tf_op jit(solution)/shard_map/while/body/eval_jaxpr/ppermute | solution.py:11
  241.5 5.0 collective-permute-done
  246.5 6.5 %collective-permute-start = (bf16[128,1536]{1,0:T(8,128)(2,1)S(1)}, bf16[128,1536]{1,0:T(8,128)(2,1)S(1)}, u32[]{:S(2)}, u32[]{:S(2)}) collective-permute-start(bf16[128,1536]{1,0:T(8,128)(2,1)S(1)} %copy.9), channel_id=1, source_target_pairs={{0,504},{8,0},{16,8},{24,16},{32,24},{40,32},{48,40},{56,48},{64,5... | collective-permute-start | bytes 1179656 | tf_op jit(solution)/shard_map/while/body/eval_jaxpr/ppermute | solution.py:11
  253.3 5.0 collective-permute-done
  258.3 6.5 %collective-permute-start = (bf16[128,1536]{1,0:T(8,128)(2,1)S(1)}, bf16[128,1536]{1,0:T(8,128)(2,1)S(1)}, u32[]{:S(2)}, u32[]{:S(2)}) collective-permute-start(bf16[128,1536]{1,0:T(8,128)(2,1)S(1)} %copy.9), channel_id=1, source_target_pairs={{0,504},{8,0},{16,8},{24,16},{32,24},{40,32},{48,40},{56,48},{64,5... | collective-permute-start | bytes 1179656 | tf_op jit(solution)/shard_map/while/body/eval_jaxpr/ppermute | solution.py:11
  265.1 5.0 collective-permute-done
  270.2 6.5 %collective-permute-start = (bf16[128,1536]{1,0:T(8,128)(2,1)S(1)}, bf16[128,1536]{1,0:T(8,128)(2,1)S(1)}, u32[]{:S(2)}, u32[]{:S(2)}) collective-permute-start(bf16[128,1536]{1,0:T(8,128)(2,1)S(1)} %copy.9), channel_id=1, source_target_pairs={{0,504},{8,0},{16,8},{24,16},{32,24},{40,32},{48,40},{56,48},{64,5... | collective-permute-start | bytes 1179656 | tf_op jit(solution)/shard_map/while/body/eval_jaxpr/ppermute | solution.py:11
  277.0 5.0 collective-permute-done
  282.0 6.5 %collective-permute-start = (bf16[128,1536]{1,0:T(8,128)(2,1)S(1)}, bf16[128,1536]{1,0:T(8,128)(2,1)S(1)}, u32[]{:S(2)}, u32[]{:S(2)}) collective-permute-start(bf16[128,1536]{1,0:T(8,128)(2,1)S(1)} %copy.9), channel_id=1, source_target_pairs={{0,504},{8,0},{16,8},{24,16},{32,24},{40,32},{48,40},{56,48},{64,5... | collective-permute-start | bytes 1179656 | tf_op jit(solution)/shard_map/while/body/eval_jaxpr/ppermute | solution.py:11
  288.8 5.0 collective-permute-done
  293.8 6.5 %collective-permute-start = (bf16[128,1536]{1,0:T(8,128)(2,1)S(1)}, bf16[128,1536]{1,0:T(8,128)(2,1)S(1)}, u32[]{:S(2)}, u32[]{:S(2)}) collective-permute-start(bf16[128,1536]{1,0:T(8,128)(2,1)S(1)} %copy.9), channel_id=1, source_target_pairs={{0,504},{8,0},{16,8},{24,16},{32,24},{40,32},{48,40},{56,48},{64,5... | collective-permute-start | bytes 1179656 | tf_op jit(solution)/shard_map/while/body/eval_jaxpr/ppermute | solution.py:11
  305.6 6.5 %collective-permute-start = (bf16[128,1536]{1,0:T(8,128)(2,1)S(1)}, bf16[128,1536]{1,0:T(8,128)(2,1)S(1)}, u32[]{:S(2)}, u32[]{:S(2)}) collective-permute-start(bf16[128,1536]{1,0:T(8,128)(2,1)S(1)} %copy.9), channel_id=1, source_target_pairs={{0,504},{8,0},{16,8},{24,16},{32,24},{40,32},{48,40},{56,48},{64,5... | collective-permute-start | bytes 1179656 | tf_op jit(solution)/shard_map/while/body/eval_jaxpr/ppermute | solution.py:11
  317.5 6.5 %collective-permute-start = (bf16[128,1536]{1,0:T(8,128)(2,1)S(1)}, bf16[128,1536]{1,0:T(8,128)(2,1)S(1)}, u32[]{:S(2)}, u32[]{:S(2)}) collective-permute-start(bf16[128,1536]{1,0:T(8,128)(2,1)S(1)} %copy.9), channel_id=1, source_target_pairs={{0,504},{8,0},{16,8},{24,16},{32,24},{40,32},{48,40},{56,48},{64,5... | collective-permute-start | bytes 1179656 | tf_op jit(solution)/shard_map/while/body/eval_jaxpr/ppermute | solution.py:11
  324.2 5.0 collective-permute-done
  329.3 6.5 %collective-permute-start = (bf16[128,1536]{1,0:T(8,128)(2,1)S(1)}, bf16[128,1536]{1,0:T(8,128)(2,1)S(1)}, u32[]{:S(2)}, u32[]{:S(2)}) collective-permute-start(bf16[128,1536]{1,0:T(8,128)(2,1)S(1)} %copy.9), channel_id=1, source_target_pairs={{0,504},{8,0},{16,8},{24,16},{32,24},{40,32},{48,40},{56,48},{64,5... | collective-permute-start | bytes 1179656 | tf_op jit(solution)/shard_map/while/body/eval_jaxpr/ppermute | solution.py:11
  336.1 5.0 collective-permute-done
  341.1 6.5 %collective-permute-start = (bf16[128,1536]{1,0:T(8,128)(2,1)S(1)}, bf16[128,1536]{1,0:T(8,128)(2,1)S(1)}, u32[]{:S(2)}, u32[]{:S(2)}) collective-permute-start(bf16[128,1536]{1,0:T(8,128)(2,1)S(1)} %copy.9), channel_id=1, source_target_pairs={{0,504},{8,0},{16,8},{24,16},{32,24},{40,32},{48,40},{56,48},{64,5... | collective-permute-start | bytes 1179656 | tf_op jit(solution)/shard_map/while/body/eval_jaxpr/ppermute | solution.py:11
  347.9 5.0 collective-permute-done
  352.9 6.5 %collective-permute-start = (bf16[128,1536]{1,0:T(8,128)(2,1)S(1)}, bf16[128,1536]{1,0:T(8,128)(2,1)S(1)}, u32[]{:S(2)}, u32[]{:S(2)}) collective-permute-start(bf16[128,1536]{1,0:T(8,128)(2,1)S(1)} %copy.9), channel_id=1, source_target_pairs={{0,504},{8,0},{16,8},{24,16},{32,24},{40,32},{48,40},{56,48},{64,5... | collective-permute-start | bytes 1179656 | tf_op jit(solution)/shard_map/while/body/eval_jaxpr/ppermute | solution.py:11
  359.7 5.0 collective-permute-done
  364.8 6.5 %collective-permute-start = (bf16[128,1536]{1,0:T(8,128)(2,1)S(1)}, bf16[128,1536]{1,0:T(8,128)(2,1)S(1)}, u32[]{:S(2)}, u32[]{:S(2)}) collective-permute-start(bf16[128,1536]{1,0:T(8,128)(2,1)S(1)} %copy.9), channel_id=1, source_target_pairs={{0,504},{8,0},{16,8},{24,16},{32,24},{40,32},{48,40},{56,48},{64,5... | collective-permute-start | bytes 1179656 | tf_op jit(solution)/shard_map/while/body/eval_jaxpr/ppermute | solution.py:11
  371.5 5.0 collective-permute-done
  376.6 6.5 %collective-permute-start = (bf16[128,1536]{1,0:T(8,128)(2,1)S(1)}, bf16[128,1536]{1,0:T(8,128)(2,1)S(1)}, u32[]{:S(2)}, u32[]{:S(2)}) collective-permute-start(bf16[128,1536]{1,0:T(8,128)(2,1)S(1)} %copy.9), channel_id=1, source_target_pairs={{0,504},{8,0},{16,8},{24,16},{32,24},{40,32},{48,40},{56,48},{64,5... | collective-permute-start | bytes 1179656 | tf_op jit(solution)/shard_map/while/body/eval_jaxpr/ppermute | solution.py:11
  383.4 5.0 collective-permute-done
  390.2 245.0 %all-reduce.2.cloned.1.call-done = f32[33,128,128]{2,1,0:T(8,128)} async-done(((f32[33,128,128]{2,1,0:T(8,128)}), f32[33,128,128]{2,1,0:T(8,128)}) %all-reduce.2.cloned.1.call-update) | async-done | bytes 2162704 | tf_op jit(solution)/shard_map/psum | solution.py:35
  (74 shorter events, 23.9 us)
Async XLA Ops:
  6.5 628.7 %all-reduce.2.cloned.1.call-start = ((), (), s32[]{:S(2)}) async-start(), calls=%async_computation | async-start | bytes 4325376 | tf_op jit(solution)/shard_map/psum | solution.py:35
  8.4 13.4 %collective-permute-start = (bf16[128,1536]{1,0:T(8,128)(2,1)S(1)}, bf16[128,1536]{1,0:T(8,128)(2,1)S(1)}, u32[]{:S(2)}, u32[]{:S(2)}) collective-permute-start(bf16[128,1536]{1,0:T(8,128)(2,1)S(1)} %copy.9), channel_id=1, source_target_pairs={{0,504},{8,0},{16,8},{24,16},{32,24},{40,32},{48,40},{56,48},{64,5... | collective-permute-start | bytes 1179656 | tf_op jit(solution)/shard_map/while/body/eval_jaxpr/ppermute | solution.py:11
  21.9 11.8 %collective-permute-start = (bf16[128,1536]{1,0:T(8,128)(2,1)S(1)}, bf16[128,1536]{1,0:T(8,128)(2,1)S(1)}, u32[]{:S(2)}, u32[]{:S(2)}) collective-permute-start(bf16[128,1536]{1,0:T(8,128)(2,1)S(1)} %copy.9), channel_id=1, source_target_pairs={{0,504},{8,0},{16,8},{24,16},{32,24},{40,32},{48,40},{56,48},{64,5... | collective-permute-start | bytes 1179656 | tf_op jit(solution)/shard_map/while/body/eval_jaxpr/ppermute | solution.py:11
  33.7 11.8 %collective-permute-start = (bf16[128,1536]{1,0:T(8,128)(2,1)S(1)}, bf16[128,1536]{1,0:T(8,128)(2,1)S(1)}, u32[]{:S(2)}, u32[]{:S(2)}) collective-permute-start(bf16[128,1536]{1,0:T(8,128)(2,1)S(1)} %copy.9), channel_id=1, source_target_pairs={{0,504},{8,0},{16,8},{24,16},{32,24},{40,32},{48,40},{56,48},{64,5... | collective-permute-start | bytes 1179656 | tf_op jit(solution)/shard_map/while/body/eval_jaxpr/ppermute | solution.py:11
  45.5 11.8 %collective-permute-start = (bf16[128,1536]{1,0:T(8,128)(2,1)S(1)}, bf16[128,1536]{1,0:T(8,128)(2,1)S(1)}, u32[]{:S(2)}, u32[]{:S(2)}) collective-permute-start(bf16[128,1536]{1,0:T(8,128)(2,1)S(1)} %copy.9), channel_id=1, source_target_pairs={{0,504},{8,0},{16,8},{24,16},{32,24},{40,32},{48,40},{56,48},{64,5... | collective-permute-start | bytes 1179656 | tf_op jit(solution)/shard_map/while/body/eval_jaxpr/ppermute | solution.py:11
  57.3 11.8 %collective-permute-start = (bf16[128,1536]{1,0:T(8,128)(2,1)S(1)}, bf16[128,1536]{1,0:T(8,128)(2,1)S(1)}, u32[]{:S(2)}, u32[]{:S(2)}) collective-permute-start(bf16[128,1536]{1,0:T(8,128)(2,1)S(1)} %copy.9), channel_id=1, source_target_pairs={{0,504},{8,0},{16,8},{24,16},{32,24},{40,32},{48,40},{56,48},{64,5... | collective-permute-start | bytes 1179656 | tf_op jit(solution)/shard_map/while/body/eval_jaxpr/ppermute | solution.py:11
  69.2 11.8 %collective-permute-start = (bf16[128,1536]{1,0:T(8,128)(2,1)S(1)}, bf16[128,1536]{1,0:T(8,128)(2,1)S(1)}, u32[]{:S(2)}, u32[]{:S(2)}) collective-permute-start(bf16[128,1536]{1,0:T(8,128)(2,1)S(1)} %copy.9), channel_id=1, source_target_pairs={{0,504},{8,0},{16,8},{24,16},{32,24},{40,32},{48,40},{56,48},{64,5... | collective-permute-start | bytes 1179656 | tf_op jit(solution)/shard_map/while/body/eval_jaxpr/ppermute | solution.py:11
  81.0 11.8 %collective-permute-start = (bf16[128,1536]{1,0:T(8,128)(2,1)S(1)}, bf16[128,1536]{1,0:T(8,128)(2,1)S(1)}, u32[]{:S(2)}, u32[]{:S(2)}) collective-permute-start(bf16[128,1536]{1,0:T(8,128)(2,1)S(1)} %copy.9), channel_id=1, source_target_pairs={{0,504},{8,0},{16,8},{24,16},{32,24},{40,32},{48,40},{56,48},{64,5... | collective-permute-start | bytes 1179656 | tf_op jit(solution)/shard_map/while/body/eval_jaxpr/ppermute | solution.py:11
  92.8 11.8 %collective-permute-start = (bf16[128,1536]{1,0:T(8,128)(2,1)S(1)}, bf16[128,1536]{1,0:T(8,128)(2,1)S(1)}, u32[]{:S(2)}, u32[]{:S(2)}) collective-permute-start(bf16[128,1536]{1,0:T(8,128)(2,1)S(1)} %copy.9), channel_id=1, source_target_pairs={{0,504},{8,0},{16,8},{24,16},{32,24},{40,32},{48,40},{56,48},{64,5... | collective-permute-start | bytes 1179656 | tf_op jit(solution)/shard_map/while/body/eval_jaxpr/ppermute | solution.py:11
  104.6 11.8 %collective-permute-start = (bf16[128,1536]{1,0:T(8,128)(2,1)S(1)}, bf16[128,1536]{1,0:T(8,128)(2,1)S(1)}, u32[]{:S(2)}, u32[]{:S(2)}) collective-permute-start(bf16[128,1536]{1,0:T(8,128)(2,1)S(1)} %copy.9), channel_id=1, source_target_pairs={{0,504},{8,0},{16,8},{24,16},{32,24},{40,32},{48,40},{56,48},{64,5... | collective-permute-start | bytes 1179656 | tf_op jit(solution)/shard_map/while/body/eval_jaxpr/ppermute | solution.py:11
  116.5 11.8 %collective-permute-start = (bf16[128,1536]{1,0:T(8,128)(2,1)S(1)}, bf16[128,1536]{1,0:T(8,128)(2,1)S(1)}, u32[]{:S(2)}, u32[]{:S(2)}) collective-permute-start(bf16[128,1536]{1,0:T(8,128)(2,1)S(1)} %copy.9), channel_id=1, source_target_pairs={{0,504},{8,0},{16,8},{24,16},{32,24},{40,32},{48,40},{56,48},{64,5... | collective-permute-start | bytes 1179656 | tf_op jit(solution)/shard_map/while/body/eval_jaxpr/ppermute | solution.py:11
  128.3 11.8 %collective-permute-start = (bf16[128,1536]{1,0:T(8,128)(2,1)S(1)}, bf16[128,1536]{1,0:T(8,128)(2,1)S(1)}, u32[]{:S(2)}, u32[]{:S(2)}) collective-permute-start(bf16[128,1536]{1,0:T(8,128)(2,1)S(1)} %copy.9), channel_id=1, source_target_pairs={{0,504},{8,0},{16,8},{24,16},{32,24},{40,32},{48,40},{56,48},{64,5... | collective-permute-start | bytes 1179656 | tf_op jit(solution)/shard_map/while/body/eval_jaxpr/ppermute | solution.py:11
  140.1 11.8 %collective-permute-start = (bf16[128,1536]{1,0:T(8,128)(2,1)S(1)}, bf16[128,1536]{1,0:T(8,128)(2,1)S(1)}, u32[]{:S(2)}, u32[]{:S(2)}) collective-permute-start(bf16[128,1536]{1,0:T(8,128)(2,1)S(1)} %copy.9), channel_id=1, source_target_pairs={{0,504},{8,0},{16,8},{24,16},{32,24},{40,32},{48,40},{56,48},{64,5... | collective-permute-start | bytes 1179656 | tf_op jit(solution)/shard_map/while/body/eval_jaxpr/ppermute | solution.py:11
  151.9 11.8 %collective-permute-start = (bf16[128,1536]{1,0:T(8,128)(2,1)S(1)}, bf16[128,1536]{1,0:T(8,128)(2,1)S(1)}, u32[]{:S(2)}, u32[]{:S(2)}) collective-permute-start(bf16[128,1536]{1,0:T(8,128)(2,1)S(1)} %copy.9), channel_id=1, source_target_pairs={{0,504},{8,0},{16,8},{24,16},{32,24},{40,32},{48,40},{56,48},{64,5... | collective-permute-start | bytes 1179656 | tf_op jit(solution)/shard_map/while/body/eval_jaxpr/ppermute | solution.py:11
  163.8 11.8 %collective-permute-start = (bf16[128,1536]{1,0:T(8,128)(2,1)S(1)}, bf16[128,1536]{1,0:T(8,128)(2,1)S(1)}, u32[]{:S(2)}, u32[]{:S(2)}) collective-permute-start(bf16[128,1536]{1,0:T(8,128)(2,1)S(1)} %copy.9), channel_id=1, source_target_pairs={{0,504},{8,0},{16,8},{24,16},{32,24},{40,32},{48,40},{56,48},{64,5... | collective-permute-start | bytes 1179656 | tf_op jit(solution)/shard_map/while/body/eval_jaxpr/ppermute | solution.py:11
  175.6 11.8 %collective-permute-start = (bf16[128,1536]{1,0:T(8,128)(2,1)S(1)}, bf16[128,1536]{1,0:T(8,128)(2,1)S(1)}, u32[]{:S(2)}, u32[]{:S(2)}) collective-permute-start(bf16[128,1536]{1,0:T(8,128)(2,1)S(1)} %copy.9), channel_id=1, source_target_pairs={{0,504},{8,0},{16,8},{24,16},{32,24},{40,32},{48,40},{56,48},{64,5... | collective-permute-start | bytes 1179656 | tf_op jit(solution)/shard_map/while/body/eval_jaxpr/ppermute | solution.py:11
  187.4 11.8 %collective-permute-start = (bf16[128,1536]{1,0:T(8,128)(2,1)S(1)}, bf16[128,1536]{1,0:T(8,128)(2,1)S(1)}, u32[]{:S(2)}, u32[]{:S(2)}) collective-permute-start(bf16[128,1536]{1,0:T(8,128)(2,1)S(1)} %copy.9), channel_id=1, source_target_pairs={{0,504},{8,0},{16,8},{24,16},{32,24},{40,32},{48,40},{56,48},{64,5... | collective-permute-start | bytes 1179656 | tf_op jit(solution)/shard_map/while/body/eval_jaxpr/ppermute | solution.py:11
  199.2 11.8 %collective-permute-start = (bf16[128,1536]{1,0:T(8,128)(2,1)S(1)}, bf16[128,1536]{1,0:T(8,128)(2,1)S(1)}, u32[]{:S(2)}, u32[]{:S(2)}) collective-permute-start(bf16[128,1536]{1,0:T(8,128)(2,1)S(1)} %copy.9), channel_id=1, source_target_pairs={{0,504},{8,0},{16,8},{24,16},{32,24},{40,32},{48,40},{56,48},{64,5... | collective-permute-start | bytes 1179656 | tf_op jit(solution)/shard_map/while/body/eval_jaxpr/ppermute | solution.py:11
  211.0 11.8 %collective-permute-start = (bf16[128,1536]{1,0:T(8,128)(2,1)S(1)}, bf16[128,1536]{1,0:T(8,128)(2,1)S(1)}, u32[]{:S(2)}, u32[]{:S(2)}) collective-permute-start(bf16[128,1536]{1,0:T(8,128)(2,1)S(1)} %copy.9), channel_id=1, source_target_pairs={{0,504},{8,0},{16,8},{24,16},{32,24},{40,32},{48,40},{56,48},{64,5... | collective-permute-start | bytes 1179656 | tf_op jit(solution)/shard_map/while/body/eval_jaxpr/ppermute | solution.py:11
  222.9 11.8 %collective-permute-start = (bf16[128,1536]{1,0:T(8,128)(2,1)S(1)}, bf16[128,1536]{1,0:T(8,128)(2,1)S(1)}, u32[]{:S(2)}, u32[]{:S(2)}) collective-permute-start(bf16[128,1536]{1,0:T(8,128)(2,1)S(1)} %copy.9), channel_id=1, source_target_pairs={{0,504},{8,0},{16,8},{24,16},{32,24},{40,32},{48,40},{56,48},{64,5... | collective-permute-start | bytes 1179656 | tf_op jit(solution)/shard_map/while/body/eval_jaxpr/ppermute | solution.py:11
  234.7 11.8 %collective-permute-start = (bf16[128,1536]{1,0:T(8,128)(2,1)S(1)}, bf16[128,1536]{1,0:T(8,128)(2,1)S(1)}, u32[]{:S(2)}, u32[]{:S(2)}) collective-permute-start(bf16[128,1536]{1,0:T(8,128)(2,1)S(1)} %copy.9), channel_id=1, source_target_pairs={{0,504},{8,0},{16,8},{24,16},{32,24},{40,32},{48,40},{56,48},{64,5... | collective-permute-start | bytes 1179656 | tf_op jit(solution)/shard_map/while/body/eval_jaxpr/ppermute | solution.py:11
  246.5 11.8 %collective-permute-start = (bf16[128,1536]{1,0:T(8,128)(2,1)S(1)}, bf16[128,1536]{1,0:T(8,128)(2,1)S(1)}, u32[]{:S(2)}, u32[]{:S(2)}) collective-permute-start(bf16[128,1536]{1,0:T(8,128)(2,1)S(1)} %copy.9), channel_id=1, source_target_pairs={{0,504},{8,0},{16,8},{24,16},{32,24},{40,32},{48,40},{56,48},{64,5... | collective-permute-start | bytes 1179656 | tf_op jit(solution)/shard_map/while/body/eval_jaxpr/ppermute | solution.py:11
  258.3 11.8 %collective-permute-start = (bf16[128,1536]{1,0:T(8,128)(2,1)S(1)}, bf16[128,1536]{1,0:T(8,128)(2,1)S(1)}, u32[]{:S(2)}, u32[]{:S(2)}) collective-permute-start(bf16[128,1536]{1,0:T(8,128)(2,1)S(1)} %copy.9), channel_id=1, source_target_pairs={{0,504},{8,0},{16,8},{24,16},{32,24},{40,32},{48,40},{56,48},{64,5... | collective-permute-start | bytes 1179656 | tf_op jit(solution)/shard_map/while/body/eval_jaxpr/ppermute | solution.py:11
  270.2 11.8 %collective-permute-start = (bf16[128,1536]{1,0:T(8,128)(2,1)S(1)}, bf16[128,1536]{1,0:T(8,128)(2,1)S(1)}, u32[]{:S(2)}, u32[]{:S(2)}) collective-permute-start(bf16[128,1536]{1,0:T(8,128)(2,1)S(1)} %copy.9), channel_id=1, source_target_pairs={{0,504},{8,0},{16,8},{24,16},{32,24},{40,32},{48,40},{56,48},{64,5... | collective-permute-start | bytes 1179656 | tf_op jit(solution)/shard_map/while/body/eval_jaxpr/ppermute | solution.py:11
  282.0 11.8 %collective-permute-start = (bf16[128,1536]{1,0:T(8,128)(2,1)S(1)}, bf16[128,1536]{1,0:T(8,128)(2,1)S(1)}, u32[]{:S(2)}, u32[]{:S(2)}) collective-permute-start(bf16[128,1536]{1,0:T(8,128)(2,1)S(1)} %copy.9), channel_id=1, source_target_pairs={{0,504},{8,0},{16,8},{24,16},{32,24},{40,32},{48,40},{56,48},{64,5... | collective-permute-start | bytes 1179656 | tf_op jit(solution)/shard_map/while/body/eval_jaxpr/ppermute | solution.py:11
  293.8 11.8 %collective-permute-start = (bf16[128,1536]{1,0:T(8,128)(2,1)S(1)}, bf16[128,1536]{1,0:T(8,128)(2,1)S(1)}, u32[]{:S(2)}, u32[]{:S(2)}) collective-permute-start(bf16[128,1536]{1,0:T(8,128)(2,1)S(1)} %copy.9), channel_id=1, source_target_pairs={{0,504},{8,0},{16,8},{24,16},{32,24},{40,32},{48,40},{56,48},{64,5... | collective-permute-start | bytes 1179656 | tf_op jit(solution)/shard_map/while/body/eval_jaxpr/ppermute | solution.py:11
  305.6 11.8 %collective-permute-start = (bf16[128,1536]{1,0:T(8,128)(2,1)S(1)}, bf16[128,1536]{1,0:T(8,128)(2,1)S(1)}, u32[]{:S(2)}, u32[]{:S(2)}) collective-permute-start(bf16[128,1536]{1,0:T(8,128)(2,1)S(1)} %copy.9), channel_id=1, source_target_pairs={{0,504},{8,0},{16,8},{24,16},{32,24},{40,32},{48,40},{56,48},{64,5... | collective-permute-start | bytes 1179656 | tf_op jit(solution)/shard_map/while/body/eval_jaxpr/ppermute | solution.py:11
  317.5 11.8 %collective-permute-start = (bf16[128,1536]{1,0:T(8,128)(2,1)S(1)}, bf16[128,1536]{1,0:T(8,128)(2,1)S(1)}, u32[]{:S(2)}, u32[]{:S(2)}) collective-permute-start(bf16[128,1536]{1,0:T(8,128)(2,1)S(1)} %copy.9), channel_id=1, source_target_pairs={{0,504},{8,0},{16,8},{24,16},{32,24},{40,32},{48,40},{56,48},{64,5... | collective-permute-start | bytes 1179656 | tf_op jit(solution)/shard_map/while/body/eval_jaxpr/ppermute | solution.py:11
  329.3 11.8 %collective-permute-start = (bf16[128,1536]{1,0:T(8,128)(2,1)S(1)}, bf16[128,1536]{1,0:T(8,128)(2,1)S(1)}, u32[]{:S(2)}, u32[]{:S(2)}) collective-permute-start(bf16[128,1536]{1,0:T(8,128)(2,1)S(1)} %copy.9), channel_id=1, source_target_pairs={{0,504},{8,0},{16,8},{24,16},{32,24},{40,32},{48,40},{56,48},{64,5... | collective-permute-start | bytes 1179656 | tf_op jit(solution)/shard_map/while/body/eval_jaxpr/ppermute | solution.py:11
  341.1 11.8 %collective-permute-start = (bf16[128,1536]{1,0:T(8,128)(2,1)S(1)}, bf16[128,1536]{1,0:T(8,128)(2,1)S(1)}, u32[]{:S(2)}, u32[]{:S(2)}) collective-permute-start(bf16[128,1536]{1,0:T(8,128)(2,1)S(1)} %copy.9), channel_id=1, source_target_pairs={{0,504},{8,0},{16,8},{24,16},{32,24},{40,32},{48,40},{56,48},{64,5... | collective-permute-start | bytes 1179656 | tf_op jit(solution)/shard_map/while/body/eval_jaxpr/ppermute | solution.py:11
  352.9 11.8 %collective-permute-start = (bf16[128,1536]{1,0:T(8,128)(2,1)S(1)}, bf16[128,1536]{1,0:T(8,128)(2,1)S(1)}, u32[]{:S(2)}, u32[]{:S(2)}) collective-permute-start(bf16[128,1536]{1,0:T(8,128)(2,1)S(1)} %copy.9), channel_id=1, source_target_pairs={{0,504},{8,0},{16,8},{24,16},{32,24},{40,32},{48,40},{56,48},{64,5... | collective-permute-start | bytes 1179656 | tf_op jit(solution)/shard_map/while/body/eval_jaxpr/ppermute | solution.py:11
  364.8 11.8 %collective-permute-start = (bf16[128,1536]{1,0:T(8,128)(2,1)S(1)}, bf16[128,1536]{1,0:T(8,128)(2,1)S(1)}, u32[]{:S(2)}, u32[]{:S(2)}) collective-permute-start(bf16[128,1536]{1,0:T(8,128)(2,1)S(1)} %copy.9), channel_id=1, source_target_pairs={{0,504},{8,0},{16,8},{24,16},{32,24},{40,32},{48,40},{56,48},{64,5... | collective-permute-start | bytes 1179656 | tf_op jit(solution)/shard_map/while/body/eval_jaxpr/ppermute | solution.py:11
  376.6 11.8 %collective-permute-start = (bf16[128,1536]{1,0:T(8,128)(2,1)S(1)}, bf16[128,1536]{1,0:T(8,128)(2,1)S(1)}, u32[]{:S(2)}, u32[]{:S(2)}) collective-permute-start(bf16[128,1536]{1,0:T(8,128)(2,1)S(1)} %copy.9), channel_id=1, source_target_pairs={{0,504},{8,0},{16,8},{24,16},{32,24},{40,32},{48,40},{56,48},{64,5... | collective-permute-start | bytes 1179656 | tf_op jit(solution)/shard_map/while/body/eval_jaxpr/ppermute | solution.py:11
Sparse Core Ops, SparseCore 0:
  390.4 244.8 all-reduce.1
where the time goes:
time: 646 us; the launch traced here: 644 us
  waiting for transfers between devices  405 us (63%)
  starting transfers between devices  210 us (33%)
  between operations  14.1 us (2%)
  matrix products  8.56 us (1%)
    psum x1, waiting for transfers between devices, on_device(): summed = lax.psum(tile_set, 'space')  245 us
    ppermute x32, starting transfers between devices, from_behind(): return lax.ppermute(x, axis, [(i, (i + by) % peers) for i in range(peers)])  210 us
    ppermute x32, waiting for transfers between devices, from_behind(): return lax.ppermute(x, axis, [(i, (i + by) % peers) for i in range(peers)])  160 us
  transfers between devices with their start and end apart: 33, of which 33 were waited for; matrix products, arithmetic and copies ran while one was open for 1% of the time, Pallas kernels for 0%

commit v1 on v0

v1 whole, which is shorter than its diff:
```python
import functools
import math

import jax
import jax.numpy as jnp
from jax import lax
from jax.experimental import pallas as pl
from jax.experimental.pallas import tpu as pltpu
from jax.sharding import Mesh
from jax.sharding import PartitionSpec as P

SIZES = {"y": 8, "zl": 4, "core": 2, "x": 4, "zh": 2}
ROW = 8
FAR = 4
VMEM = pl.BlockSpec(memory_space=pltpu.VMEM)
SMEM = pl.BlockSpec(memory_space=pltpu.SMEM)
PARAMS = pltpu.CompilerParams(vmem_limit_bytes=24 * 1024 * 1024)


def ahead(block, by):
    return lax.ppermute(block, "y", [(i, (i - by) % SIZES["y"]) for i in range(SIZES["y"])])


def across(block, flip):
    return lax.ppermute(block, "zl", [(i, i ^ flip) for i in range(SIZES["zl"])])


def swapped(block):
    return lax.ppermute(block, "core", [(0, 1), (1, 0)])


def tiles_kernel(place_ref, *refs):
    lefts, rights, out_ref, all_rights = refs[:8], refs[8:13], refs[13], refs[14]
    rows = rights[0].shape[0]
    share = rows // SIZES["x"]
    zl, core = place_ref[0], place_ref[1]
    mine = zl * 2 + core
    for d in range(FAR + 1):
        all_rights[pl.ds(d * rows, rows), :] = rights[d][...]
    contract = (((1,), (1,)), ((), ()))
    for n in range(ROW):
        flip, other = n % 4, n // 4
        zl_n = jnp.bitwise_xor(zl, flip)
        core_n = jnp.bitwise_xor(core, other)
        target = zl_n * 2 + core_n
        first = jnp.where(target < mine, 0, 1)
        right = all_rights[pl.ds(pl.multiple_of(first * rows, rows), FAR * rows), :]
        tile = lax.dot_general(
            lefts[n][...], right, contract, preferred_element_type=jnp.float32
        ).astype(jnp.bfloat16)
        for t in range(FAR):
            for x in range(SIZES["x"]):
                out_ref[x, target * FAR + t] = tile[
                    x * share : (x + 1) * share, t * rows : (t + 1) * rows
                ]
    own = lax.dot_general(
        lefts[0][...], rights[0][...], contract, preferred_element_type=jnp.float32
    )
    high = own.astype(jnp.bfloat16)
    low = (own - high.astype(jnp.float32)).astype(jnp.bfloat16)
    for x in range(SIZES["x"]):
        out_ref[x, ROW * FAR] = high[x * share : (x + 1) * share]
        out_ref[x, ROW * FAR + 1] = low[x * share : (x + 1) * share]


def first_sum_kernel(place_ref, parts_ref, out_ref, keep_ref, give_ref):
    half = out_ref.shape[2]
    zh = place_ref[2]

    def total(tile):
        acc = parts_ref[0, tile].astype(jnp.float32)
        for x in range(1, SIZES["x"]):
            acc = acc + parts_ref[x, tile].astype(jnp.float32)
        return acc

    for target in range(ROW):
        for t in range(FAR):
            acc = total(target * FAR + t).astype(jnp.bfloat16)
            for h in range(SIZES["zh"]):
                out_ref[target * SIZES["zh"] + h, t] = acc[h * half : (h + 1) * half]
    own = total(ROW * FAR) + total(ROW * FAR + 1)
    upper, lower = own[:half], own[half:]
    keep_ref[...] = jnp.where(zh == 0, upper, lower)
    give_ref[...] = jnp.where(zh == 0, lower, upper)


def last_sum_kernel(factor, place_ref, parts_ref, keep_ref, got_ref, out_ref):
    mine = place_ref[0] * 2 + place_ref[1]
    out_ref[0, 0] = (keep_ref[...] + got_ref[...]) * factor
    for j in range(1, ROW + 1):
        source = lax.rem(mine + j, ROW)
        for t in range(FAR):
            a = parts_ref[source * 2, t].astype(jnp.float32)
            b = parts_ref[source * 2 + 1, t].astype(jnp.float32)
            out_ref[0, ROW * t + j] = (a + b) * factor


def on_device(snapshots, counts, weights):
    rows, points = snapshots.shape
    slot_index = lax.broadcasted_iota(jnp.int32, (rows, 1), 0)
    masked = jnp.where(slot_index < counts[0], snapshots, jnp.zeros_like(snapshots))
    weighted = (masked.astype(jnp.float32) * weights[None, :]).astype(jnp.bfloat16)
    place = jnp.stack(
        [lax.axis_index("zl"), lax.axis_index("core"), lax.axis_index("zh")]
    ).astype(jnp.int32)

    z2, z3 = across(weighted, 2), across(weighted, 3)
    r4, r1 = ahead(masked, 4), ahead(masked, 1)
    z1 = across(weighted, 1)
    r3, r2 = ahead(r4, -1), ahead(r1, 1)
    lefts = [weighted, z1, z2, z3]
    lefts = lefts + [swapped(b) for b in lefts]
    rights = [masked, r1, r2, r3, r4]

    share, half = rows // SIZES["x"], rows // (SIZES["x"] * SIZES["zh"])
    tiles = pl.pallas_call(
        tiles_kernel,
        out_shape=jax.ShapeDtypeStruct(
            (SIZES["x"], ROW * FAR + 2, share, rows), jnp.bfloat16
        ),
        in_specs=[SMEM] + [VMEM] * 13,
        out_specs=VMEM,
        scratch_shapes=[pltpu.VMEM(((FAR + 1) * rows, points), jnp.bfloat16)],
        compiler_params=PARAMS,
    )(place, *lefts, *rights)
    parts = lax.all_to_all(tiles, "x", 0, 0, tiled=True)
    sums, keep, give = pl.pallas_call(
        first_sum_kernel,
        out_shape=(
            jax.ShapeDtypeStruct((ROW * SIZES["zh"], FAR, half, rows), jnp.bfloat16),
            jax.ShapeDtypeStruct((half, rows), jnp.float32),
            jax.ShapeDtypeStruct((half, rows), jnp.float32),
        ),
        in_specs=[SMEM, VMEM],
        out_specs=(VMEM, VMEM, VMEM),
        compiler_params=PARAMS,
    )(place, parts)
    got = lax.ppermute(give, "zh", [(0, 1), (1, 0)])
    shares = lax.all_to_all(sums, ("zl", "core", "zh"), 0, 0, tiled=True)
    factor = 1.0 / math.sqrt(points * SIZES["x"] * SIZES["zh"])
    return pl.pallas_call(
        functools.partial(last_sum_kernel, factor),
        out_shape=jax.ShapeDtypeStruct((1, ROW * FAR + 1, half, rows), jnp.float32),
        in_specs=[SMEM, VMEM, VMEM, VMEM],
        out_specs=VMEM,
        compiler_params=PARAMS,
    )(place, shares, keep, got)


def solution(mesh):
    fine = Mesh(mesh.devices.reshape(tuple(SIZES.values())), tuple(SIZES))
    snap, space = ("y", "zl", "core"), ("x", "zh")
    return jax.shard_map(
        on_device,
        mesh=fine,
        in_specs=(P(snap, space), P(snap), P(space)),
        out_specs=P(snap, None, space, None),
        check_vma=False,
    )
```

time: 646 us -> 112 us (0.17)
  the two profiles are of different devices: /device:TPU:56 before, /device:TPU:8 now
where the time goes in v1:
time: 112 us; the launch traced here: 111 us
  starting transfers between devices  54.7 us (49%)
  waiting for transfers between devices  25.9 us (23%)
  blocking collectives  20.4 us (18%)
  Pallas kernels  8.23 us (7%)
  other arithmetic  1.27 us (1%)
    all_to_all x1, blocking collectives, on_device(): parts = lax.all_to_all(tiles, 'x', 0, 0, tiled=True)  20.4 us
    ppermute x4, starting transfers between devices, ahead(): lax.ppermute(block, 'y', [(i, (i - by) % SIZES['y']) for i in range(SIZES...  15.9 us
    ppermute x3, starting transfers between devices, across(): lax.ppermute(block, 'zl', [(i, i ^ flip) for i in range(SIZES['zl'])])  14.1 us
    ppermute x3, waiting for transfers between devices, across(): lax.ppermute(block, 'zl', [(i, i ^ flip) for i in range(SIZES['zl'])])  12.1 us
    all_to_all x1, starting transfers between devices, on_device(): shares = lax.all_to_all(sums, ('zl', 'core', 'zh'), 0, 0, tiled=True)  8.84 us
    ppermute x4, starting transfers between devices, swapped(): return lax.ppermute(block, 'core', [(0, 1), (1, 0)])  8.16 us
    ppermute x1, starting transfers between devices, on_device(): got = lax.ppermute(give, 'zh', [(0, 1), (1, 0)])  7.73 us
    ppermute x4, waiting for transfers between devices, ahead(): lax.ppermute(block, 'y', [(i, (i - by) % SIZES['y']) for i in range(SIZES...  7.15 us
  transfers between devices with their start and end apart: 13, of which 5 were waited for; matrix products, arithmetic and copies ran while one was open for 0% of the time, Pallas kernels for 0%

profile of v1, /device:TPU:8, one launch (start us, length us, event | category | flops | bytes accessed | tf_op | source)
XLA Modules:
  0.0 111.4 jit_solution(14133018591389884111)
XLA Ops:
  0.7 1.2 %multiply_convert_fusion = (bf16[128,1536]{1,0:T(8,128)(2,1)S(1)}, bf16[128,1536]{1,0:T(8,128)(2,1)S(1)}) fusion(f32[1536]{0:T(1024)} %param.5, bf16[128,1536]{1,0:T(8,128)(2,1)} %param.3, pred[128]{0:T(512)(128)(4,1)S(1)} %iota_compare_fusion), kind=kLoop, calls=%fused_computation | loop fusion | flops 786432 | bytes 1185920 | tf_op jit(solution)/shard_map/convert_element_type | solution.py:102
  1.9 6.8 %collective-permute-start.9 = (bf16[128,1536]{1,0:T(8,128)(2,1)S(1)}, bf16[128,1536]{1,0:T(8,128)(2,1)S(1)}, u32[]{:S(2)}, u32[]{:S(2)}) collective-permute-start(bf16[128,1536]{1,0:T(8,128)(2,1)S(1)} %get-tuple-element.12.refs_8_), channel_id=1, source_target_pairs={{0,256},{64,320},{128,384},{192,448},{256,0},{320,64},{384,128},{4... | collective-permute-start | bytes 1179656 | tf_op jit(solution)/shard_map/ppermute | solution.py:21
  8.7 3.3 %collective-permute-start.7 = (bf16[128,1536]{1,0:T(8,128)(2,1)S(1)}, bf16[128,1536]{1,0:T(8,128)(2,1)S(1)}, u32[]{:S(2)}, u32[]{:S(2)}) collective-permute-start(bf16[128,1536]{1,0:T(8,128)(2,1)S(1)} %get-tuple-element.12.refs_8_), channel_id=1, source_target_pairs={{0,448},{64,0},{128,64},{192,128},{256,192},{320,256},{384,320},{4... | collective-permute-start | bytes 1179656 | tf_op jit(solution)/shard_map/ppermute | solution.py:21
  12.0 1.9 %collective-permute-start.3 = (bf16[128,1536]{1,0:T(8,128)(2,1)S(1)}, bf16[128,1536]{1,0:T(8,128)(2,1)S(1)}, u32[]{:S(2)}, u32[]{:S(2)}) collective-permute-start(bf16[128,1536]{1,0:T(8,128)(2,1)S(1)} %get-tuple-element.11.refs_0_), channel_id=1, source_target_pairs={{0,8},{8,0},{1,9},{9,1},{2,10},{10,2},{3,11},{11,3},{4,12},{12,4},... | collective-permute-start | bytes 1179656 | tf_op jit(solution)/shard_map/ppermute | solution.py:29
  13.9 7.9 %collective-permute-start.2 = (bf16[128,1536]{1,0:T(8,128)(2,1)S(1)}, bf16[128,1536]{1,0:T(8,128)(2,1)S(1)}, u32[]{:S(2)}, u32[]{:S(2)}) collective-permute-start(bf16[128,1536]{1,0:T(8,128)(2,1)S(1)} %get-tuple-element.11.refs_0_), channel_id=1, source_target_pairs={{0,48},{16,32},{32,16},{48,0},{1,49},{17,33},{33,17},{49,1},{2,50}... | collective-permute-start | bytes 1179656 | tf_op jit(solution)/shard_map/ppermute | solution.py:25
  21.8 1.9 %collective-permute-start.1 = (bf16[128,1536]{1,0:T(8,128)(2,1)S(1)}, bf16[128,1536]{1,0:T(8,128)(2,1)S(1)}, u32[]{:S(2)}, u32[]{:S(2)}) collective-permute-start(bf16[128,1536]{1,0:T(8,128)(2,1)S(1)} %get-tuple-element.11.refs_0_), channel_id=1, source_target_pairs={{0,32},{16,48},{32,0},{48,16},{1,33},{17,49},{33,1},{49,17},{2,34}... | collective-permute-start | bytes 1179656 | tf_op jit(solution)/shard_map/ppermute | solution.py:25
  23.7 3.6 %collective-permute-done.9.refs_12_ = bf16[128,1536]{1,0:T(8,128)(2,1)S(1)} collective-permute-done((bf16[128,1536]{1,0:T(8,128)(2,1)S(1)}, bf16[128,1536]{1,0:T(8,128)(2,1)S(1)}, u32[]{:S(2)}, u32[]{:S(2)}) %collective-permute-start.9) | collective-permute-done | bytes 393248 | tf_op jit(solution)/shard_map/ppermute | solution.py:21
  27.3 4.3 %collective-permute-start = (bf16[128,1536]{1,0:T(8,128)(2,1)S(1)}, bf16[128,1536]{1,0:T(8,128)(2,1)S(1)}, u32[]{:S(2)}, u32[]{:S(2)}) collective-permute-start(bf16[128,1536]{1,0:T(8,128)(2,1)S(1)} %get-tuple-element.11.refs_0_), channel_id=1, source_target_pairs={{0,16},{16,0},{32,48},{48,32},{1,17},{17,1},{33,49},{49,33},{2,18}... | collective-permute-start | bytes 1179656 | tf_op jit(solution)/shard_map/ppermute | solution.py:25
  31.6 3.6 %collective-permute-done.7.refs_9_ = bf16[128,1536]{1,0:T(8,128)(2,1)S(1)} collective-permute-done((bf16[128,1536]{1,0:T(8,128)(2,1)S(1)}, bf16[128,1536]{1,0:T(8,128)(2,1)S(1)}, u32[]{:S(2)}, u32[]{:S(2)}) %collective-permute-start.7) | collective-permute-done | bytes 393248 | tf_op jit(solution)/shard_map/ppermute | solution.py:21
  35.2 2.6 %collective-permute-start.10 = (bf16[128,1536]{1,0:T(8,128)(2,1)S(1)}, bf16[128,1536]{1,0:T(8,128)(2,1)S(1)}, u32[]{:S(2)}, u32[]{:S(2)}) collective-permute-start(bf16[128,1536]{1,0:T(8,128)(2,1)S(1)} %collective-permute-done.9.refs_12_), channel_id=1, source_target_pairs={{0,64},{64,128},{128,192},{192,256},{256,320},{320,384},{384,448},... | collective-permute-start | bytes 1179656 | tf_op jit(solution)/shard_map/ppermute | solution.py:21
  37.8 0.0 collective-permute-done.3.refs_4_
  37.8 3.2 %collective-permute-start.8 = (bf16[128,1536]{1,0:T(8,128)(2,1)S(1)}, bf16[128,1536]{1,0:T(8,128)(2,1)}, u32[]{:S(2)}, u32[]{:S(2)}) collective-permute-start(bf16[128,1536]{1,0:T(8,128)(2,1)S(1)} %collective-permute-done.7.refs_9_), channel_id=1, source_target_pairs={{0,448},{64,0},{128,64},{192,128},{256,192},{320,256},{384,320},{4... | collective-permute-start | bytes 1179656 | tf_op jit(solution)/shard_map/ppermute | solution.py:21
  41.0 0.0 collective-permute-done.2.refs_3_
  41.0 1.9 %collective-permute-start.6 = (bf16[128,1536]{1,0:T(8,128)(2,1)S(1)}, bf16[128,1536]{1,0:T(8,128)(2,1)}, u32[]{:S(2)}, u32[]{:S(2)}) collective-permute-start(bf16[128,1536]{1,0:T(8,128)(2,1)S(1)} %collective-permute-done.2.refs_3_), channel_id=1, source_target_pairs={{0,8},{8,0},{1,9},{9,1},{2,10},{10,2},{3,11},{11,3},{4,12},{12,4},... | collective-permute-start | bytes 1179656 | tf_op jit(solution)/shard_map/ppermute | solution.py:29
  43.0 12.1 %collective-permute-done.1.refs_2_ = bf16[128,1536]{1,0:T(8,128)(2,1)S(1)} collective-permute-done((bf16[128,1536]{1,0:T(8,128)(2,1)S(1)}, bf16[128,1536]{1,0:T(8,128)(2,1)S(1)}, u32[]{:S(2)}, u32[]{:S(2)}) %collective-permute-start.1) | collective-permute-done | bytes 393248 | tf_op jit(solution)/shard_map/ppermute | solution.py:25
  55.0 1.9 %collective-permute-start.5 = (bf16[128,1536]{1,0:T(8,128)(2,1)S(1)}, bf16[128,1536]{1,0:T(8,128)(2,1)}, u32[]{:S(2)}, u32[]{:S(2)}) collective-permute-start(bf16[128,1536]{1,0:T(8,128)(2,1)S(1)} %collective-permute-done.1.refs_2_), channel_id=1, source_target_pairs={{0,8},{8,0},{1,9},{9,1},{2,10},{10,2},{3,11},{11,3},{4,12},{12,4},... | collective-permute-start | bytes 1179656 | tf_op jit(solution)/shard_map/ppermute | solution.py:29
  57.0 0.0 collective-permute-done.refs_1_
  57.0 2.4 %collective-permute-start.4 = (bf16[128,1536]{1,0:T(8,128)(2,1)S(1)}, bf16[128,1536]{1,0:T(8,128)(2,1)}, u32[]{:S(2)}, u32[]{:S(2)}) collective-permute-start(bf16[128,1536]{1,0:T(8,128)(2,1)S(1)} %collective-permute-done.refs_1_), channel_id=1, source_target_pairs={{0,8},{8,0},{1,9},{9,1},{2,10},{10,2},{3,11},{11,3},{4,12},{12,4},... | collective-permute-start | bytes 1179656 | tf_op jit(solution)/shard_map/ppermute | solution.py:29
  59.4 0.1 pad_add_fusion.place_ref
  59.5 0.0 collective-permute-done.10.refs_11_
  59.5 0.0 collective-permute-done.8.refs_10_
  59.5 0.0 collective-permute-done.6.refs_7_
  59.5 0.0 collective-permute-done.5.refs_6_
  59.5 1.4 %collective-permute-done.4.refs_5_ = bf16[128,1536]{1,0:T(8,128)(2,1)} collective-permute-done((bf16[128,1536]{1,0:T(8,128)(2,1)S(1)}, bf16[128,1536]{1,0:T(8,128)(2,1)}, u32[]{:S(2)}, u32[]{:S(2)}) %collective-permute-start.4) | collective-permute-done | bytes 393248 | tf_op jit(solution)/shard_map/ppermute | solution.py:29
  60.8 5.6 %shard_map.37 = bf16[4,34,32,128]{3,2,1,0:T(8,128)(2,1)S(1)} custom-call(s32[3]{0:T(128)S(1)} %pad_add_fusion.place_ref, bf16[128,1536]{1,0:T(8,128)(2,1)S(1)} %get-tuple-element.11.refs_0_, bf16[128,1536]{1,0:T(8,128)(2,1)S(1)} %collective-permute-done.refs_1_, bf16[128,1536]{1,0:T(8,128)(2,1)S(1)} %collective-permute-done.1.refs_2_, ...), custom_call_target="tpu_custom_call" | custom-call | tf_op jit(solution)/shard_map/pallas_call | solution.py:116
  66.4 20.4 %all_to_all.10.parts_ref = bf16[4,34,32,128]{3,2,1,0:T(8,128)(2,1)S(1)} all-to-all(bf16[4,34,32,128]{3,2,1,0:T(8,128)(2,1)S(1)} %shard_map.37), channel_id=1, replica_groups=mesh['y'=8,'zl'=4,'core'=2,'x'=4,'zh'=2] {'x'}, dimensions={0} | all-to-all | bytes 2228224 | tf_op jit(solution)/shard_map/all_to_all | solution.py:126
  86.8 1.4 %shard_map.38 = (bf16[16,4,16,128]{3,2,1,0:T(8,128)(2,1)}, f32[16,128]{1,0:T(8,128)S(1)}, f32[16,128]{1,0:T(8,128)S(1)}) custom-call(s32[3]{0:T(128)S(1)} %pad_add_fusion.place_ref, bf16[4,34,32,128]{3,2,1,0:T(8,128)(2,1)S(1)} %all_to_all.10.parts_ref), custom_call_target="tpu_custom_call" | custom-call | tf_op jit(solution)/shard_map/pallas_call | solution.py:127
  88.2 8.8 %all-to-all-start.1 = ((bf16[16,4,16,128]{3,2,1,0:T(8,128)(2,1)}), bf16[16,4,16,128]{3,2,1,0:T(8,128)(2,1)S(1)}, u32[]{:S(2)}, u32[]{:S(2)}) async-start(bf16[16,4,16,128]{3,2,1,0:T(8,128)(2,1)} %get-tuple-element.8), calls=%async_computation.1 | async-start | bytes 524288 | tf_op jit(solution)/shard_map/all_to_all | solution.py:139
  97.1 7.7 %collective-permute-start.11 = (f32[16,128]{1,0:T(8,128)S(1)}, f32[16,128]{1,0:T(8,128)S(1)}, u32[]{:S(2)}, u32[]{:S(2)}) collective-permute-start(f32[16,128]{1,0:T(8,128)S(1)} %get-tuple-element.10), channel_id=1, source_target_pairs={{0,1},{1,0},{2,3},{3,2},{4,5},{5,4},{6,7},{7,6},{8,9},{9,8},{10,11... | collective-permute-start | bytes 24584 | tf_op jit(solution)/shard_map/ppermute | solution.py:138
  104.8 5.3 %collective-permute-done.11.got_ref = f32[16,128]{1,0:T(8,128)S(1)} collective-permute-done((f32[16,128]{1,0:T(8,128)S(1)}, f32[16,128]{1,0:T(8,128)S(1)}, u32[]{:S(2)}, u32[]{:S(2)}) %collective-permute-start.11) | collective-permute-done | bytes 8224 | tf_op jit(solution)/shard_map/ppermute | solution.py:138
  110.1 0.0 all-to-all-done.1.parts_ref
  110.1 1.3 %shard_map.39 = f32[1,33,16,128]{3,2,1,0:T(8,128)} custom-call(s32[3]{0:T(128)S(1)} %pad_add_fusion.place_ref, bf16[16,4,16,128]{3,2,1,0:T(8,128)(2,1)S(1)} %all-to-all-done.1.parts_ref, f32[16,128]{1,0:T(8,128)S(1)} %get-tuple-element.9.keep_ref, f32[16,128]{1,0:T(8,128)S(1)} %collective-permute-done.11.got_ref), custom_call_target="tpu_custom_call" | custom-call | tf_op jit(solution)/shard_map/pallas_call | solution.py:141
  (1 shorter events, 0.0 us)
Async XLA Ops:
  1.9 25.4 %collective-permute-start.9 = (bf16[128,1536]{1,0:T(8,128)(2,1)S(1)}, bf16[128,1536]{1,0:T(8,128)(2,1)S(1)}, u32[]{:S(2)}, u32[]{:S(2)}) collective-permute-start(bf16[128,1536]{1,0:T(8,128)(2,1)S(1)} %get-tuple-element.12.refs_8_), channel_id=1, source_target_pairs={{0,256},{64,320},{128,384},{192,448},{256,0},{320,64},{384,128},{4... | collective-permute-start | bytes 1179656 | tf_op jit(solution)/shard_map/ppermute | solution.py:21
  8.7 26.5 %collective-permute-start.7 = (bf16[128,1536]{1,0:T(8,128)(2,1)S(1)}, bf16[128,1536]{1,0:T(8,128)(2,1)S(1)}, u32[]{:S(2)}, u32[]{:S(2)}) collective-permute-start(bf16[128,1536]{1,0:T(8,128)(2,1)S(1)} %get-tuple-element.12.refs_8_), channel_id=1, source_target_pairs={{0,448},{64,0},{128,64},{192,128},{256,192},{320,256},{384,320},{4... | collective-permute-start | bytes 1179656 | tf_op jit(solution)/shard_map/ppermute | solution.py:21
  12.0 25.8 %collective-permute-start.3 = (bf16[128,1536]{1,0:T(8,128)(2,1)S(1)}, bf16[128,1536]{1,0:T(8,128)(2,1)S(1)}, u32[]{:S(2)}, u32[]{:S(2)}) collective-permute-start(bf16[128,1536]{1,0:T(8,128)(2,1)S(1)} %get-tuple-element.11.refs_0_), channel_id=1, source_target_pairs={{0,8},{8,0},{1,9},{9,1},{2,10},{10,2},{3,11},{11,3},{4,12},{12,4},... | collective-permute-start | bytes 1179656 | tf_op jit(solution)/shard_map/ppermute | solution.py:29
  13.9 27.1 %collective-permute-start.2 = (bf16[128,1536]{1,0:T(8,128)(2,1)S(1)}, bf16[128,1536]{1,0:T(8,128)(2,1)S(1)}, u32[]{:S(2)}, u32[]{:S(2)}) collective-permute-start(bf16[128,1536]{1,0:T(8,128)(2,1)S(1)} %get-tuple-element.11.refs_0_), channel_id=1, source_target_pairs={{0,48},{16,32},{32,16},{48,0},{1,49},{17,33},{33,17},{49,1},{2,50}... | collective-permute-start | bytes 1179656 | tf_op jit(solution)/shard_map/ppermute | solution.py:25
  21.8 33.2 %collective-permute-start.1 = (bf16[128,1536]{1,0:T(8,128)(2,1)S(1)}, bf16[128,1536]{1,0:T(8,128)(2,1)S(1)}, u32[]{:S(2)}, u32[]{:S(2)}) collective-permute-start(bf16[128,1536]{1,0:T(8,128)(2,1)S(1)} %get-tuple-element.11.refs_0_), channel_id=1, source_target_pairs={{0,32},{16,48},{32,0},{48,16},{1,33},{17,49},{33,1},{49,17},{2,34}... | collective-permute-start | bytes 1179656 | tf_op jit(solution)/shard_map/ppermute | solution.py:25
  27.3 29.7 %collective-permute-start = (bf16[128,1536]{1,0:T(8,128)(2,1)S(1)}, bf16[128,1536]{1,0:T(8,128)(2,1)S(1)}, u32[]{:S(2)}, u32[]{:S(2)}) collective-permute-start(bf16[128,1536]{1,0:T(8,128)(2,1)S(1)} %get-tuple-element.11.refs_0_), channel_id=1, source_target_pairs={{0,16},{16,0},{32,48},{48,32},{1,17},{17,1},{33,49},{49,33},{2,18}... | collective-permute-start | bytes 1179656 | tf_op jit(solution)/shard_map/ppermute | solution.py:25
  35.2 24.3 %collective-permute-start.10 = (bf16[128,1536]{1,0:T(8,128)(2,1)S(1)}, bf16[128,1536]{1,0:T(8,128)(2,1)S(1)}, u32[]{:S(2)}, u32[]{:S(2)}) collective-permute-start(bf16[128,1536]{1,0:T(8,128)(2,1)S(1)} %collective-permute-done.9.refs_12_), channel_id=1, source_target_pairs={{0,64},{64,128},{128,192},{192,256},{256,320},{320,384},{384,448},... | collective-permute-start | bytes 1179656 | tf_op jit(solution)/shard_map/ppermute | solution.py:21
  37.8 21.7 %collective-permute-start.8 = (bf16[128,1536]{1,0:T(8,128)(2,1)S(1)}, bf16[128,1536]{1,0:T(8,128)(2,1)}, u32[]{:S(2)}, u32[]{:S(2)}) collective-permute-start(bf16[128,1536]{1,0:T(8,128)(2,1)S(1)} %collective-permute-done.7.refs_9_), channel_id=1, source_target_pairs={{0,448},{64,0},{128,64},{192,128},{256,192},{320,256},{384,320},{4... | collective-permute-start | bytes 1179656 | tf_op jit(solution)/shard_map/ppermute | solution.py:21
  41.0 18.4 %collective-permute-start.6 = (bf16[128,1536]{1,0:T(8,128)(2,1)S(1)}, bf16[128,1536]{1,0:T(8,128)(2,1)}, u32[]{:S(2)}, u32[]{:S(2)}) collective-permute-start(bf16[128,1536]{1,0:T(8,128)(2,1)S(1)} %collective-permute-done.2.refs_3_), channel_id=1, source_target_pairs={{0,8},{8,0},{1,9},{9,1},{2,10},{10,2},{3,11},{11,3},{4,12},{12,4},... | collective-permute-start | bytes 1179656 | tf_op jit(solution)/shard_map/ppermute | solution.py:29
  55.0 4.4 %collective-permute-start.5 = (bf16[128,1536]{1,0:T(8,128)(2,1)S(1)}, bf16[128,1536]{1,0:T(8,128)(2,1)}, u32[]{:S(2)}, u32[]{:S(2)}) collective-permute-start(bf16[128,1536]{1,0:T(8,128)(2,1)S(1)} %collective-permute-done.1.refs_2_), channel_id=1, source_target_pairs={{0,8},{8,0},{1,9},{9,1},{2,10},{10,2},{3,11},{11,3},{4,12},{12,4},... | collective-permute-start | bytes 1179656 | tf_op jit(solution)/shard_map/ppermute | solution.py:29
  57.0 3.9 %collective-permute-start.4 = (bf16[128,1536]{1,0:T(8,128)(2,1)S(1)}, bf16[128,1536]{1,0:T(8,128)(2,1)}, u32[]{:S(2)}, u32[]{:S(2)}) collective-permute-start(bf16[128,1536]{1,0:T(8,128)(2,1)S(1)} %collective-permute-done.refs_1_), channel_id=1, source_target_pairs={{0,8},{8,0},{1,9},{9,1},{2,10},{10,2},{3,11},{11,3},{4,12},{12,4},... | collective-permute-start | bytes 1179656 | tf_op jit(solution)/shard_map/ppermute | solution.py:29
  88.2 21.9 %all-to-all-start.1 = ((bf16[16,4,16,128]{3,2,1,0:T(8,128)(2,1)}), bf16[16,4,16,128]{3,2,1,0:T(8,128)(2,1)S(1)}, u32[]{:S(2)}, u32[]{:S(2)}) async-start(bf16[16,4,16,128]{3,2,1,0:T(8,128)(2,1)} %get-tuple-element.8), calls=%async_computation.1 | async-start | bytes 524288 | tf_op jit(solution)/shard_map/all_to_all | solution.py:139
  97.1 13.0 %collective-permute-start.11 = (f32[16,128]{1,0:T(8,128)S(1)}, f32[16,128]{1,0:T(8,128)S(1)}, u32[]{:S(2)}, u32[]{:S(2)}) collective-permute-start(f32[16,128]{1,0:T(8,128)S(1)} %get-tuple-element.10), channel_id=1, source_target_pairs={{0,1},{1,0},{2,3},{3,2},{4,5},{5,4},{6,7},{7,6},{8,9},{9,8},{10,11... | collective-permute-start | bytes 24584 | tf_op jit(solution)/shard_map/ppermute | solution.py:138

commit v2 on v0

v2 whole, which is shorter than its diff:
```python
import functools
import math

import jax
import jax.numpy as jnp
from jax import lax
from jax.experimental import pallas as pl
from jax.experimental.pallas import tpu as pltpu
from jax.sharding import Mesh
from jax.sharding import PartitionSpec as P

SIZES = {"y": 8, "zl": 4, "core": 2, "x": 4, "zh": 2}
ROW = 8
FAR = 4
EACH = 8
VMEM = pl.BlockSpec(memory_space=pltpu.VMEM)
SMEM = pl.BlockSpec(memory_space=pltpu.SMEM)
PARAMS = pltpu.CompilerParams(vmem_limit_bytes=32 * 1024 * 1024)


def ahead(block, by):
    return lax.ppermute(block, "y", [(i, (i - by) % SIZES["y"]) for i in range(SIZES["y"])])


def across(block, flip):
    return lax.ppermute(block, "zl", [(i, i ^ flip) for i in range(SIZES["zl"])])


def swapped(block):
    return lax.ppermute(block, "core", [(0, 1), (1, 0)])


def product(left_rows, right_rows):
    return lax.dot_general(
        left_rows, right_rows, (((1,), (1,)), ((), ())), preferred_element_type=jnp.float32
    )


def tiles_kernel(place_ref, *refs):
    lefts, rights, out_ref, left_all, right_all, dots = refs[:4], refs[4:14], *refs[14:]
    rows = rights[0].shape[0]
    share = rows // SIZES["x"]
    zl, core = place_ref[0], place_ref[1]
    for n in range(4):
        left_all[n * rows : (n + 1) * rows] = lefts[n][...]
    for n in range(10):
        right_all[n * rows : (n + 1) * rows] = rights[n][...]
    dots[...] = product(left_all[...], right_all[...])
    for flip in range(4):
        target = jnp.bitwise_xor(zl, flip)
        for other in range(2):
            side = jnp.bitwise_xor(core, other)
            first = jnp.where(zl * 2 + side > target * 2 + core, 0, 1)
            for t in range(FAR):
                start = pl.multiple_of((other * (FAR + 1) + t + first) * rows, rows)
                tile = dots[flip * rows : (flip + 1) * rows, pl.ds(start, rows)]
                tile = tile.astype(jnp.bfloat16)
                for x in range(SIZES["x"]):
                    out_ref[x, target * EACH + side * FAR + t] = tile[
                        x * share : (x + 1) * share
                    ]


def first_sum_kernel(parts_ref, out_ref):
    half = out_ref.shape[2]
    for target in range(4):
        for n in range(EACH):
            acc = parts_ref[0, target * EACH + n].astype(jnp.float32)
            for x in range(1, SIZES["x"]):
                acc = acc + parts_ref[x, target * EACH + n].astype(jnp.float32)
            acc = acc.astype(jnp.bfloat16)
            for h in range(SIZES["zh"]):
                out_ref[target * SIZES["zh"] + h, n] = acc[h * half : (h + 1) * half]


def last_sum_kernel(factor, place_ref, parts_ref, own_ref, out_ref):
    mine = place_ref[0] * 2 + place_ref[1]
    out_ref[0, 0] = own_ref[...] * factor
    for j in range(1, ROW + 1):
        source = lax.rem(mine + j, ROW)
        zl, core = lax.div(source, 2), lax.rem(source, 2)
        for t in range(FAR):
            a = parts_ref[zl * 2, core * FAR + t].astype(jnp.float32)
            b = parts_ref[zl * 2 + 1, core * FAR + t].astype(jnp.float32)
            out_ref[0, ROW * t + j] = (a + b) * factor


def on_device(snapshots, counts, weights):
    rows, points = snapshots.shape
    slot_index = lax.broadcasted_iota(jnp.int32, (rows, 1), 0)
    masked = jnp.where(slot_index < counts[0], snapshots, jnp.zeros_like(snapshots))
    weighted = (masked.astype(jnp.float32) * weights[None, :]).astype(jnp.bfloat16)
    place = jnp.stack([lax.axis_index("zl"), lax.axis_index("core")]).astype(jnp.int32)

    z2, z3, z1 = across(weighted, 2), across(weighted, 3), across(weighted, 1)
    r4, r1 = ahead(masked, 4), ahead(masked, 1)
    r3, r2 = ahead(r4, -1), ahead(r1, 1)
    lefts = [weighted, z1, z2, z3]
    rights = [masked, r1, r2, r3, r4]
    rights = rights + [swapped(b) for b in rights]
    own = lax.psum_scatter(
        product(weighted, masked), ("x", "zh"), scatter_dimension=0, tiled=True
    )

    share, half = rows // SIZES["x"], rows // (SIZES["x"] * SIZES["zh"])
    tiles = pl.pallas_call(
        tiles_kernel,
        out_shape=jax.ShapeDtypeStruct((SIZES["x"], 4 * EACH, share, rows), jnp.bfloat16),
        in_specs=[SMEM] + [VMEM] * 14,
        out_specs=VMEM,
        scratch_shapes=[
            pltpu.VMEM((4 * rows, points), jnp.bfloat16),
            pltpu.VMEM((10 * rows, points), jnp.bfloat16),
            pltpu.VMEM((4 * rows, 10 * rows), jnp.float32),
        ],
        compiler_params=PARAMS,
    )(place, *lefts, *rights)
    parts = lax.all_to_all(tiles, "x", 0, 0, tiled=True)
    sums = pl.pallas_call(
        first_sum_kernel,
        out_shape=jax.ShapeDtypeStruct((4 * SIZES["zh"], EACH, half, rows), jnp.bfloat16),
        in_specs=[VMEM],
        out_specs=VMEM,
        compiler_params=PARAMS,
    )(parts)
    shares = lax.all_to_all(sums, ("zl", "zh"), 0, 0, tiled=True)
    factor = 1.0 / math.sqrt(points * SIZES["x"] * SIZES["zh"])
    return pl.pallas_call(
        functools.partial(last_sum_kernel, factor),
        out_shape=jax.ShapeDtypeStruct((1, ROW * FAR + 1, half, rows), jnp.float32),
        in_specs=[SMEM, VMEM, VMEM],
        out_specs=VMEM,
        compiler_params=PARAMS,
    )(place, shares, own)


def solution(mesh):
    fine = Mesh(mesh.devices.reshape(tuple(SIZES.values())), tuple(SIZES))
    snap, space = ("y", "zl", "core"), ("x", "zh")
    return jax.shard_map(
        on_device,
        mesh=fine,
        in_specs=(P(snap, space), P(snap), P(space)),
        out_specs=P(snap, None, space, None),
        check_vma=False,
    )
```

time: 646 us -> 200 us (0.31)
  waiting for transfers between devices: 405 us -> 103 us
  starting transfers between devices: 210 us -> 52.4 us
  blocking collectives: 0 us -> 19.7 us
  matrix products: 8.56 us -> 0.9 us
    psum x1 -> x0, waiting for transfers between devices: 245 us -> none  [on_device(): summed = lax.psum(tile_set, 'space')]
    ppermute x32 -> x12, starting transfers between devices: 210 us -> 39.7 us  [the longest x3 18.3 us: across(): lax.ppermute(block, 'zl', [(i, i ^ flip) for i in range(SIZES['zl'])])]
    ppermute x32 -> x12, waiting for transfers between devices: 160 us -> 13.3 us  [the longest x4 12 us: ahead(): lax.ppermute(block, 'y', [(i, (i - by) % SIZES['y']) for i in range(SIZES...]
    reduce_scatter x0 -> x1, waiting for transfers between devices: none -> 89.8 us  [on_device(): lax.psum_scatter(product(weighted, masked), ('x', 'zh'), scatter_dimensio...]
    all_to_all x0 -> x1, blocking collectives: none -> 19.7 us  [on_device(): parts = lax.all_to_all(tiles, 'x', 0, 0, tiled=True)]
    all_to_all x0 -> x1, starting transfers between devices: none -> 12.6 us  [on_device(): shares = lax.all_to_all(sums, ('zl', 'zh'), 0, 0, tiled=True)]
    dot_general x33 -> x1, matrix products: 8.56 us -> 0.9 us  [product(): lax.dot_general(left_rows, right_rows, (((1,), (1,)), ((), ())), preferre...]
  transfers between devices with their start and end apart: 33 -> 14, of which waited for: 33 -> 5; matrix products, arithmetic and copies ran while one was open for 1% -> 0% of each run, Pallas kernels for 0% -> 0%
where the time goes in v2:
time: 200 us; the launch traced here: 199 us
  waiting for transfers between devices  103 us (52%)
  starting transfers between devices  52.4 us (26%)
  blocking collectives  19.7 us (10%)
  between operations  14.2 us (7%)
  Pallas kernels  6.09 us (3%)
    reduce_scatter x1, waiting for transfers between devices, on_device(): lax.psum_scatter(product(weighted, masked), ('x', 'zh'), scatter_dimensio...  89.8 us
    all_to_all x1, blocking collectives, on_device(): parts = lax.all_to_all(tiles, 'x', 0, 0, tiled=True)  19.7 us
    ppermute x3, starting transfers between devices, across(): lax.ppermute(block, 'zl', [(i, i ^ flip) for i in range(SIZES['zl'])])  18.3 us
    all_to_all x1, starting transfers between devices, on_device(): shares = lax.all_to_all(sums, ('zl', 'zh'), 0, 0, tiled=True)  12.6 us
    ppermute x4, waiting for transfers between devices, ahead(): lax.ppermute(block, 'y', [(i, (i - by) % SIZES['y']) for i in range(SIZES...  12 us
    ppermute x4, starting transfers between devices, ahead(): lax.ppermute(block, 'y', [(i, (i - by) % SIZES['y']) for i in range(SIZES...  10.9 us
    ppermute x5, starting transfers between devices, swapped(): return lax.ppermute(block, 'core', [(0, 1), (1, 0)])  10.6 us
  transfers between devices with their start and end apart: 14, of which 5 were waited for; matrix products, arithmetic and copies ran while one was open for 0% of the time, Pallas kernels for 0%

profile of v2, /device:TPU:56, one launch (start us, length us, event | category | flops | bytes accessed | tf_op | source)
XLA Modules:
  0.0 198.5 jit_solution(15533764896398518998)
XLA Ops:
  7.2 1.2 multiply_convert_fusion
  8.4 4.7 %collective-permute-start.5 = (bf16[128,1536]{1,0:T(8,128)(2,1)S(1)}, bf16[128,1536]{1,0:T(8,128)(2,1)S(1)}, u32[]{:S(2)}, u32[]{:S(2)}) collective-permute-start(bf16[128,1536]{1,0:T(8,128)(2,1)S(1)} %get-tuple-element.6.refs_4_), channel_id=1, source_target_pairs={{0,256},{64,320},{128,384},{192,448},{256,0},{320,64},{384,128},{4... | collective-permute-start | bytes 1179656 | tf_op jit(solution)/shard_map/ppermute | solution.py:22
  13.1 2.4 %collective-permute-start.3 = (bf16[128,1536]{1,0:T(8,128)(2,1)S(1)}, bf16[128,1536]{1,0:T(8,128)(2,1)S(1)}, u32[]{:S(2)}, u32[]{:S(2)}) collective-permute-start(bf16[128,1536]{1,0:T(8,128)(2,1)S(1)} %get-tuple-element.6.refs_4_), channel_id=1, source_target_pairs={{0,448},{64,0},{128,64},{192,128},{256,192},{320,256},{384,320},{4... | collective-permute-start | bytes 1179656 | tf_op jit(solution)/shard_map/ppermute | solution.py:22
  15.5 1.9 collective-permute-start.7
  17.4 4.3 %collective-permute-start = (bf16[128,1536]{1,0:T(8,128)(2,1)S(1)}, bf16[128,1536]{1,0:T(8,128)(2,1)S(1)}, u32[]{:S(2)}, u32[]{:S(2)}) collective-permute-start(bf16[128,1536]{1,0:T(8,128)(2,1)S(1)} %get-tuple-element.5.refs_0_), channel_id=1, source_target_pairs={{0,16},{16,0},{32,48},{48,32},{1,17},{17,1},{33,49},{49,33},{2,18}... | collective-permute-start | bytes 1179656 | tf_op jit(solution)/shard_map/ppermute | solution.py:26
  21.7 6.1 %collective-permute-start.1 = (bf16[128,1536]{1,0:T(8,128)(2,1)S(1)}, bf16[128,1536]{1,0:T(8,128)(2,1)S(1)}, u32[]{:S(2)}, u32[]{:S(2)}) collective-permute-start(bf16[128,1536]{1,0:T(8,128)(2,1)S(1)} %get-tuple-element.5.refs_0_), channel_id=1, source_target_pairs={{0,32},{16,48},{32,0},{48,16},{1,33},{17,49},{33,1},{49,17},{2,34}... | collective-permute-start | bytes 1179656 | tf_op jit(solution)/shard_map/ppermute | solution.py:26
  27.8 6.0 %collective-permute-done.5.refs_8_ = bf16[128,1536]{1,0:T(8,128)(2,1)S(1)} collective-permute-done((bf16[128,1536]{1,0:T(8,128)(2,1)S(1)}, bf16[128,1536]{1,0:T(8,128)(2,1)S(1)}, u32[]{:S(2)}, u32[]{:S(2)}) %collective-permute-start.5) | collective-permute-done | bytes 393248 | tf_op jit(solution)/shard_map/ppermute | solution.py:22
  33.8 1.9 collective-permute-start.6
  35.7 5.9 %collective-permute-done.3.refs_5_ = bf16[128,1536]{1,0:T(8,128)(2,1)S(1)} collective-permute-done((bf16[128,1536]{1,0:T(8,128)(2,1)S(1)}, bf16[128,1536]{1,0:T(8,128)(2,1)S(1)}, u32[]{:S(2)}, u32[]{:S(2)}) %collective-permute-start.3) | collective-permute-done | bytes 393248 | tf_op jit(solution)/shard_map/ppermute | solution.py:22
  41.7 1.9 collective-permute-start.4
  43.6 0.0 collective-permute-done.7.refs_9_
  43.6 7.9 %collective-permute-start.2 = (bf16[128,1536]{1,0:T(8,128)(2,1)S(1)}, bf16[128,1536]{1,0:T(8,128)(2,1)}, u32[]{:S(2)}, u32[]{:S(2)}) collective-permute-start(bf16[128,1536]{1,0:T(8,128)(2,1)S(1)} %get-tuple-element.5.refs_0_), channel_id=1, source_target_pairs={{0,48},{16,32},{32,16},{48,0},{1,49},{17,33},{33,17},{49,1},{2,50}... | collective-permute-start | bytes 1179656 | tf_op jit(solution)/shard_map/ppermute | solution.py:26
  51.5 0.0 collective-permute-done.refs_1_
  51.5 1.9 collective-permute-start.11
  53.4 0.0 collective-permute-done.1.refs_2_
  53.5 2.4 %collective-permute-start.8 = (bf16[128,1536]{1,0:T(8,128)(2,1)S(1)}, bf16[128,1536]{1,0:T(8,128)(2,1)}, u32[]{:S(2)}, u32[]{:S(2)}) collective-permute-start(bf16[128,1536]{1,0:T(8,128)(2,1)S(1)} %collective-permute-done.3.refs_5_), channel_id=1, source_target_pairs={{0,8},{8,0},{1,9},{9,1},{2,10},{10,2},{3,11},{11,3},{4,12},{12,4},... | collective-permute-start | bytes 1179656 | tf_op jit(solution)/shard_map/ppermute | solution.py:30
  55.9 0.0 collective-permute-done.6.refs_7_
  55.9 1.9 collective-permute-start.10
  57.8 0.0 collective-permute-done.4.refs_6_
  57.8 2.4 %collective-permute-start.9 = (bf16[128,1536]{1,0:T(8,128)(2,1)S(1)}, bf16[128,1536]{1,0:T(8,128)(2,1)}, u32[]{:S(2)}, u32[]{:S(2)}) collective-permute-start(bf16[128,1536]{1,0:T(8,128)(2,1)S(1)} %collective-permute-done.4.refs_6_), channel_id=1, source_target_pairs={{0,8},{8,0},{1,9},{9,1},{2,10},{10,2},{3,11},{11,3},{4,12},{12,4},... | collective-permute-start | bytes 1179656 | tf_op jit(solution)/shard_map/ppermute | solution.py:30
  60.2 0.1 pad_add_fusion.place_ref
  60.3 0.7 collective-permute-done.2.refs_3_
  61.0 0.0 collective-permute-done.11.refs_13_
  61.0 0.0 collective-permute-done.8.refs_10_
  61.0 0.0 collective-permute-done.10.refs_12_
  61.0 0.7 collective-permute-done.9.refs_11_
  61.7 4.0 %shard_map.37 = bf16[4,32,32,128]{3,2,1,0:T(8,128)(2,1)S(1)} custom-call(s32[2]{0:T(128)S(1)} %pad_add_fusion.place_ref, bf16[128,1536]{1,0:T(8,128)(2,1)S(1)} %get-tuple-element.5.refs_0_, bf16[128,1536]{1,0:T(8,128)(2,1)S(1)} %collective-permute-done.refs_1_, bf16[128,1536]{1,0:T(8,128)(2,1)S(1)} %collective-permute-done.1.refs_2_, ...), custom_call_target="tpu_custom_call" | custom-call | tf_op jit(solution)/shard_map/pallas_call | solution.py:106
  65.7 19.7 %all_to_all.10.parts_ref = bf16[4,32,32,128]{3,2,1,0:T(8,128)(2,1)S(1)} all-to-all(bf16[4,32,32,128]{3,2,1,0:T(8,128)(2,1)S(1)} %shard_map.37), channel_id=1, replica_groups=mesh['y'=8,'zl'=4,'core'=2,'x'=4,'zh'=2] {'x'}, dimensions={0} | all-to-all | bytes 2097152 | tf_op jit(solution)/shard_map/all_to_all | solution.py:118
  85.4 0.8 shard_map.38
  86.2 0.0 copy-start.1
  86.2 12.6 %all-to-all-start.1 = ((bf16[8,8,16,128]{3,2,1,0:T(8,128)(2,1)}), bf16[8,8,16,128]{3,2,1,0:T(8,128)(2,1)S(1)}, u32[]{:S(2)}, u32[]{:S(2)}) async-start(bf16[8,8,16,128]{3,2,1,0:T(8,128)(2,1)} %shard_map.38), calls=%async_computation.1 | async-start | bytes 524288 | tf_op jit(solution)/shard_map/all_to_all | solution.py:126
  98.9 0.0 reduce-scatter.2.cloned.1.call-start
  98.9 0.0 copy-done.1
  98.9 0.9 fusion
  99.8 0.0 reduce-scatter.2.cloned.1.call-update
  99.8 89.8 %reduce-scatter.2.cloned.1.call-done.own_ref = f32[16,128]{1,0:T(8,128)} async-done(((f32[128,128]{1,0:T(8,128)}), f32[16,128]{1,0:T(8,128)}) %reduce-scatter.2.cloned.1.call-update) | async-done | bytes 8208 | tf_op jit(solution)/shard_map/reduce_scatter | solution.py:101
  189.7 0.0 all-to-all-done.1.parts_ref
  189.7 0.0 copy-start
  189.7 0.7 copy-done
  190.4 1.3 shard_map.39
  (1 shorter events, 0.0 us)
Async XLA Ops:
  8.4 25.4 %collective-permute-start.5 = (bf16[128,1536]{1,0:T(8,128)(2,1)S(1)}, bf16[128,1536]{1,0:T(8,128)(2,1)S(1)}, u32[]{:S(2)}, u32[]{:S(2)}) collective-permute-start(bf16[128,1536]{1,0:T(8,128)(2,1)S(1)} %get-tuple-element.6.refs_4_), channel_id=1, source_target_pairs={{0,256},{64,320},{128,384},{192,448},{256,0},{320,64},{384,128},{4... | collective-permute-start | bytes 1179656 | tf_op jit(solution)/shard_map/ppermute | solution.py:22
  13.1 28.6 %collective-permute-start.3 = (bf16[128,1536]{1,0:T(8,128)(2,1)S(1)}, bf16[128,1536]{1,0:T(8,128)(2,1)S(1)}, u32[]{:S(2)}, u32[]{:S(2)}) collective-permute-start(bf16[128,1536]{1,0:T(8,128)(2,1)S(1)} %get-tuple-element.6.refs_4_), channel_id=1, source_target_pairs={{0,448},{64,0},{128,64},{192,128},{256,192},{320,256},{384,320},{4... | collective-permute-start | bytes 1179656 | tf_op jit(solution)/shard_map/ppermute | solution.py:22
  15.5 28.1 %collective-permute-start.7 = (bf16[128,1536]{1,0:T(8,128)(2,1)S(1)}, bf16[128,1536]{1,0:T(8,128)(2,1)S(1)}, u32[]{:S(2)}, u32[]{:S(2)}) collective-permute-start(bf16[128,1536]{1,0:T(8,128)(2,1)S(1)} %get-tuple-element.6.refs_4_), channel_id=1, source_target_pairs={{0,8},{8,0},{1,9},{9,1},{2,10},{10,2},{3,11},{11,3},{4,12},{12,4},... | collective-permute-start | bytes 1179656 | tf_op jit(solution)/shard_map/ppermute | solution.py:30
  17.4 34.1 %collective-permute-start = (bf16[128,1536]{1,0:T(8,128)(2,1)S(1)}, bf16[128,1536]{1,0:T(8,128)(2,1)S(1)}, u32[]{:S(2)}, u32[]{:S(2)}) collective-permute-start(bf16[128,1536]{1,0:T(8,128)(2,1)S(1)} %get-tuple-element.5.refs_0_), channel_id=1, source_target_pairs={{0,16},{16,0},{32,48},{48,32},{1,17},{17,1},{33,49},{49,33},{2,18}... | collective-permute-start | bytes 1179656 | tf_op jit(solution)/shard_map/ppermute | solution.py:26
  21.7 31.8 %collective-permute-start.1 = (bf16[128,1536]{1,0:T(8,128)(2,1)S(1)}, bf16[128,1536]{1,0:T(8,128)(2,1)S(1)}, u32[]{:S(2)}, u32[]{:S(2)}) collective-permute-start(bf16[128,1536]{1,0:T(8,128)(2,1)S(1)} %get-tuple-element.5.refs_0_), channel_id=1, source_target_pairs={{0,32},{16,48},{32,0},{48,16},{1,33},{17,49},{33,1},{49,17},{2,34}... | collective-permute-start | bytes 1179656 | tf_op jit(solution)/shard_map/ppermute | solution.py:26
  33.8 22.1 %collective-permute-start.6 = (bf16[128,1536]{1,0:T(8,128)(2,1)S(1)}, bf16[128,1536]{1,0:T(8,128)(2,1)S(1)}, u32[]{:S(2)}, u32[]{:S(2)}) collective-permute-start(bf16[128,1536]{1,0:T(8,128)(2,1)S(1)} %collective-permute-done.5.refs_8_), channel_id=1, source_target_pairs={{0,64},{64,128},{128,192},{192,256},{256,320},{320,384},{384,448},... | collective-permute-start | bytes 1179656 | tf_op jit(solution)/shard_map/ppermute | solution.py:22
  41.7 16.1 %collective-permute-start.4 = (bf16[128,1536]{1,0:T(8,128)(2,1)S(1)}, bf16[128,1536]{1,0:T(8,128)(2,1)S(1)}, u32[]{:S(2)}, u32[]{:S(2)}) collective-permute-start(bf16[128,1536]{1,0:T(8,128)(2,1)S(1)} %collective-permute-done.3.refs_5_), channel_id=1, source_target_pairs={{0,448},{64,0},{128,64},{192,128},{256,192},{320,256},{384,320},{4... | collective-permute-start | bytes 1179656 | tf_op jit(solution)/shard_map/ppermute | solution.py:22
  43.6 17.4 %collective-permute-start.2 = (bf16[128,1536]{1,0:T(8,128)(2,1)S(1)}, bf16[128,1536]{1,0:T(8,128)(2,1)}, u32[]{:S(2)}, u32[]{:S(2)}) collective-permute-start(bf16[128,1536]{1,0:T(8,128)(2,1)S(1)} %get-tuple-element.5.refs_0_), channel_id=1, source_target_pairs={{0,48},{16,32},{32,16},{48,0},{1,49},{17,33},{33,17},{49,1},{2,50}... | collective-permute-start | bytes 1179656 | tf_op jit(solution)/shard_map/ppermute | solution.py:26
  51.5 9.5 %collective-permute-start.11 = (bf16[128,1536]{1,0:T(8,128)(2,1)S(1)}, bf16[128,1536]{1,0:T(8,128)(2,1)}, u32[]{:S(2)}, u32[]{:S(2)}) collective-permute-start(bf16[128,1536]{1,0:T(8,128)(2,1)S(1)} %collective-permute-done.5.refs_8_), channel_id=1, source_target_pairs={{0,8},{8,0},{1,9},{9,1},{2,10},{10,2},{3,11},{11,3},{4,12},{12,4},... | collective-permute-start | bytes 1179656 | tf_op jit(solution)/shard_map/ppermute | solution.py:30
  53.5 7.5 %collective-permute-start.8 = (bf16[128,1536]{1,0:T(8,128)(2,1)S(1)}, bf16[128,1536]{1,0:T(8,128)(2,1)}, u32[]{:S(2)}, u32[]{:S(2)}) collective-permute-start(bf16[128,1536]{1,0:T(8,128)(2,1)S(1)} %collective-permute-done.3.refs_5_), channel_id=1, source_target_pairs={{0,8},{8,0},{1,9},{9,1},{2,10},{10,2},{3,11},{11,3},{4,12},{12,4},... | collective-permute-start | bytes 1179656 | tf_op jit(solution)/shard_map/ppermute | solution.py:30
  55.9 5.1 %collective-permute-start.10 = (bf16[128,1536]{1,0:T(8,128)(2,1)S(1)}, bf16[128,1536]{1,0:T(8,128)(2,1)}, u32[]{:S(2)}, u32[]{:S(2)}) collective-permute-start(bf16[128,1536]{1,0:T(8,128)(2,1)S(1)} %collective-permute-done.6.refs_7_), channel_id=1, source_target_pairs={{0,8},{8,0},{1,9},{9,1},{2,10},{10,2},{3,11},{11,3},{4,12},{12,4},... | collective-permute-start | bytes 1179656 | tf_op jit(solution)/shard_map/ppermute | solution.py:30
  57.8 3.9 %collective-permute-start.9 = (bf16[128,1536]{1,0:T(8,128)(2,1)S(1)}, bf16[128,1536]{1,0:T(8,128)(2,1)}, u32[]{:S(2)}, u32[]{:S(2)}) collective-permute-start(bf16[128,1536]{1,0:T(8,128)(2,1)S(1)} %collective-permute-done.4.refs_6_), channel_id=1, source_target_pairs={{0,8},{8,0},{1,9},{9,1},{2,10},{10,2},{3,11},{11,3},{4,12},{12,4},... | collective-permute-start | bytes 1179656 | tf_op jit(solution)/shard_map/ppermute | solution.py:30
  86.2 12.7 %copy-start.1 = (f32[1536]{0:T(1024)S(1)}, f32[1536]{0:T(1024)}, u32[]{:S(2)}) copy-start(f32[1536]{0:T(1024)} %param.5) | copy-start | bytes 18436
  86.2 103.4 %all-to-all-start.1 = ((bf16[8,8,16,128]{3,2,1,0:T(8,128)(2,1)}), bf16[8,8,16,128]{3,2,1,0:T(8,128)(2,1)S(1)}, u32[]{:S(2)}, u32[]{:S(2)}) async-start(bf16[8,8,16,128]{3,2,1,0:T(8,128)(2,1)} %shard_map.38), calls=%async_computation.1 | async-start | bytes 524288 | tf_op jit(solution)/shard_map/all_to_all | solution.py:126
  98.9 90.8 %reduce-scatter.2.cloned.1.call-start = ((), (), s32[]{:S(2)}) async-start(), calls=%async_computation.3 | async-start | bytes 73728 | tf_op jit(solution)/shard_map/reduce_scatter | solution.py:101
  189.7 0.7 copy-start
Sparse Core Ops, SparseCore 0:
  104.1 85.5 reduce-scatter.1

commit v3 on v2

--- a/solution.py
+++ b/solution.py
@@ -37,15 +37,25 @@
 
 
 def tiles_kernel(place_ref, *refs):
-    lefts, rights, out_ref, left_all, right_all, dots = refs[:4], refs[4:14], *refs[14:]
-    rows = rights[0].shape[0]
+    ins, (out_ref, left_all, right_all, dots) = refs[:-4], refs[-4:]
+    rows = ins[0].shape[0]
     share = rows // SIZES["x"]
     zl, core = place_ref[0], place_ref[1]
-    for n in range(4):
-        left_all[n * rows : (n + 1) * rows] = lefts[n][...]
-    for n in range(10):
-        right_all[n * rows : (n + 1) * rows] = rights[n][...]
+    at = 0
+    for ref in ins[:4]:
+        left_all[at : at + ref.shape[0]] = ref[...]
+        at += ref.shape[0]
+    at = 0
+    for ref in ins[4:]:
+        right_all[at : at + ref.shape[0]] = ref[...]
+        at += ref.shape[0]
     dots[...] = product(left_all[...], right_all[...])
+    own = dots[:rows, :rows]
+    high = own.astype(jnp.bfloat16)
+    low = (own - high.astype(jnp.float32)).astype(jnp.bfloat16)
+    for x in range(SIZES["x"]):
+        out_ref[x, 4 * EACH] = high[x * share : (x + 1) * share]
+        out_ref[x, 4 * EACH + 1] = low[x * share : (x + 1) * share]
     for flip in range(4):
         target = jnp.bitwise_xor(zl, flip)
         for other in range(2):
@@ -63,19 +73,33 @@
 
 def first_sum_kernel(parts_ref, out_ref):
     half = out_ref.shape[2]
+
+    def total(tile):
+        acc = parts_ref[0, tile].astype(jnp.float32)
+        for x in range(1, SIZES["x"]):
+            acc = acc + parts_ref[x, tile].astype(jnp.float32)
+        return acc
+
+    own = total(4 * EACH) + total(4 * EACH + 1)
+    high = own.astype(jnp.bfloat16)
+    low = (own - high.astype(jnp.float32)).astype(jnp.bfloat16)
     for target in range(4):
-        for n in range(EACH):
-            acc = parts_ref[0, target * EACH + n].astype(jnp.float32)
-            for x in range(1, SIZES["x"]):
-                acc = acc + parts_ref[x, target * EACH + n].astype(jnp.float32)
-            acc = acc.astype(jnp.bfloat16)
+        for n in range(EACH + 2):
+            if n < EACH:
+                tile = total(target * EACH + n).astype(jnp.bfloat16)
+            else:
+                tile = high if n == EACH else low
             for h in range(SIZES["zh"]):
-                out_ref[target * SIZES["zh"] + h, n] = acc[h * half : (h + 1) * half]
+                out_ref[target * SIZES["zh"] + h, n] = tile[h * half : (h + 1) * half]
 
 
-def last_sum_kernel(factor, place_ref, parts_ref, own_ref, out_ref):
+def last_sum_kernel(factor, place_ref, parts_ref, out_ref):
     mine = place_ref[0] * 2 + place_ref[1]
-    out_ref[0, 0] = own_ref[...] * factor
+    own = jnp.zeros(out_ref.shape[2:], jnp.float32)
+    for h in range(SIZES["zh"]):
+        for n in (EACH, EACH + 1):
+            own = own + parts_ref[place_ref[0] * 2 + h, n].astype(jnp.float32)
+    out_ref[0, 0] = own * factor
     for j in range(1, ROW + 1):
         source = lax.rem(mine + j, ROW)
         zl, core = lax.div(source, 2), lax.rem(source, 2)
@@ -92,20 +116,18 @@
     weighted = (masked.astype(jnp.float32) * weights[None, :]).astype(jnp.bfloat16)
     place = jnp.stack([lax.axis_index("zl"), lax.axis_index("core")]).astype(jnp.int32)
 
-    z2, z3, z1 = across(weighted, 2), across(weighted, 3), across(weighted, 1)
+    z2, z1 = across(weighted, 2), across(weighted, 1)
+    z3 = across(z2, 1)
     r4, r1 = ahead(masked, 4), ahead(masked, 1)
     r3, r2 = ahead(r4, -1), ahead(r1, 1)
     lefts = [weighted, z1, z2, z3]
     rights = [masked, r1, r2, r3, r4]
     rights = rights + [swapped(b) for b in rights]
-    own = lax.psum_scatter(
-        product(weighted, masked), ("x", "zh"), scatter_dimension=0, tiled=True
-    )
 
     share, half = rows // SIZES["x"], rows // (SIZES["x"] * SIZES["zh"])
     tiles = pl.pallas_call(
         tiles_kernel,
-        out_shape=jax.ShapeDtypeStruct((SIZES["x"], 4 * EACH, share, rows), jnp.bfloat16),
+        out_shape=jax.ShapeDtypeStruct((SIZES["x"], 4 * EACH + 2, share, rows), jnp.bfloat16),
         in_specs=[SMEM] + [VMEM] * 14,
         out_specs=VMEM,
         scratch_shapes=[
@@ -118,7 +140,7 @@
     parts = lax.all_to_all(tiles, "x", 0, 0, tiled=True)
     sums = pl.pallas_call(
         first_sum_kernel,
-        out_shape=jax.ShapeDtypeStruct((4 * SIZES["zh"], EACH, half, rows), jnp.bfloat16),
+        out_shape=jax.ShapeDtypeStruct((4 * SIZES["zh"], EACH + 2, half, rows), jnp.bfloat16),
         in_specs=[VMEM],
         out_specs=VMEM,
         compiler_params=PARAMS,
@@ -128,10 +150,10 @@
     return pl.pallas_call(
         functools.partial(last_sum_kernel, factor),
         out_shape=jax.ShapeDtypeStruct((1, ROW * FAR + 1, half, rows), jnp.float32),
-        in_specs=[SMEM, VMEM, VMEM],
+        in_specs=[SMEM, VMEM],
         out_specs=VMEM,
         compiler_params=PARAMS,
-    )(place, shares, own)
+    )(place, shares)
 
 
 def solution(mesh):

time: 200 us -> 103 us (0.52)
  the two profiles are of different devices: /device:TPU:56 before, /device:TPU:64 now
where the time goes in v3:
time: 103 us; the launch traced here: 102 us
  starting transfers between devices  43.3 us (42%)
  blocking collectives  38.7 us (38%)
  waiting for transfers between devices  12.6 us (12%)
  Pallas kernels  5.4 us (5%)
  other arithmetic  1.27 us (1%)
    ppermute x4, starting transfers between devices, ahead(): lax.ppermute(block, 'y', [(i, (i - by) % SIZES['y']) for i in range(SIZES...  23 us
    all_to_all x1, blocking collectives, on_device(): shares = lax.all_to_all(sums, ('zl', 'zh'), 0, 0, tiled=True)  19.5 us
    all_to_all x1, blocking collectives, on_device(): parts = lax.all_to_all(tiles, 'x', 0, 0, tiled=True)  19.2 us
    ppermute x5, starting transfers between devices, swapped(): return lax.ppermute(block, 'core', [(0, 1), (1, 0)])  10.3 us
    ppermute x3, starting transfers between devices, across(): lax.ppermute(block, 'zl', [(i, i ^ flip) for i in range(SIZES['zl'])])  9.93 us
    ppermute x3, waiting for transfers between devices, across(): lax.ppermute(block, 'zl', [(i, i ^ flip) for i in range(SIZES['zl'])])  6.66 us
    ppermute x4, waiting for transfers between devices, ahead(): lax.ppermute(block, 'y', [(i, (i - by) % SIZES['y']) for i in range(SIZES...  5.94 us
    pallas_call x1, Pallas kernels, on_device(): pl.pallas_call(tiles_kernel, out_shape=jax.ShapeDtypeStruct((SIZES['x'],...  3.95 us
  transfers between devices with their start and end apart: 12, of which 4 were waited for; matrix products, arithmetic and copies ran while one was open for 0% of the time, Pallas kernels for 0%

profile of v3, /device:TPU:64, one launch (start us, length us, event | category | flops | bytes accessed | tf_op | source)
XLA Modules:
  0.0 102.0 jit_solution(12250174345493987289)
XLA Ops:
  0.7 1.2 %multiply_convert_fusion = (bf16[128,1536]{1,0:T(8,128)(2,1)S(1)}, bf16[128,1536]{1,0:T(8,128)(2,1)S(1)}) fusion(f32[1536]{0:T(1024)} %param.5, bf16[128,1536]{1,0:T(8,128)(2,1)} %param.3, pred[128]{0:T(512)(128)(4,1)S(1)} %iota_compare_fusion), kind=kLoop, calls=%fused_computation | loop fusion | flops 786432 | bytes 1185920 | tf_op jit(solution)/shard_map/convert_element_type | solution.py:116
  1.9 7.7 %collective-permute-start.5 = (bf16[128,1536]{1,0:T(8,128)(2,1)S(1)}, bf16[128,1536]{1,0:T(8,128)(2,1)S(1)}, u32[]{:S(2)}, u32[]{:S(2)}) collective-permute-start(bf16[128,1536]{1,0:T(8,128)(2,1)S(1)} %get-tuple-element.6.refs_4_), channel_id=1, source_target_pairs={{0,256},{64,320},{128,384},{192,448},{256,0},{320,64},{384,128},{4... | collective-permute-start | bytes 1179656 | tf_op jit(solution)/shard_map/ppermute | solution.py:22
  9.6 2.4 %collective-permute-start.3 = (bf16[128,1536]{1,0:T(8,128)(2,1)S(1)}, bf16[128,1536]{1,0:T(8,128)(2,1)S(1)}, u32[]{:S(2)}, u32[]{:S(2)}) collective-permute-start(bf16[128,1536]{1,0:T(8,128)(2,1)S(1)} %get-tuple-element.6.refs_4_), channel_id=1, source_target_pairs={{0,448},{64,0},{128,64},{192,128},{256,192},{320,256},{384,320},{4... | collective-permute-start | bytes 1179656 | tf_op jit(solution)/shard_map/ppermute | solution.py:22
  12.0 6.1 %collective-permute-start.1 = (bf16[128,1536]{1,0:T(8,128)(2,1)S(1)}, bf16[128,1536]{1,0:T(8,128)(2,1)S(1)}, u32[]{:S(2)}, u32[]{:S(2)}) collective-permute-start(bf16[128,1536]{1,0:T(8,128)(2,1)S(1)} %get-tuple-element.5.refs_0_), channel_id=1, source_target_pairs={{0,32},{16,48},{32,0},{48,16},{1,33},{17,49},{33,1},{49,17},{2,34}... | collective-permute-start | bytes 1179656 | tf_op jit(solution)/shard_map/ppermute | solution.py:26
  18.1 1.9 %collective-permute-start = (bf16[128,1536]{1,0:T(8,128)(2,1)S(1)}, bf16[128,1536]{1,0:T(8,128)(2,1)S(1)}, u32[]{:S(2)}, u32[]{:S(2)}) collective-permute-start(bf16[128,1536]{1,0:T(8,128)(2,1)S(1)} %get-tuple-element.5.refs_0_), channel_id=1, source_target_pairs={{0,16},{16,0},{32,48},{48,32},{1,17},{17,1},{33,49},{49,33},{2,18}... | collective-permute-start | bytes 1179656 | tf_op jit(solution)/shard_map/ppermute | solution.py:26
  20.0 1.9 %collective-permute-start.7 = (bf16[128,1536]{1,0:T(8,128)(2,1)S(1)}, bf16[128,1536]{1,0:T(8,128)(2,1)S(1)}, u32[]{:S(2)}, u32[]{:S(2)}) collective-permute-start(bf16[128,1536]{1,0:T(8,128)(2,1)S(1)} %get-tuple-element.6.refs_4_), channel_id=1, source_target_pairs={{0,8},{8,0},{1,9},{9,1},{2,10},{10,2},{3,11},{11,3},{4,12},{12,4},... | collective-permute-start | bytes 1179656 | tf_op jit(solution)/shard_map/ppermute | solution.py:30
  21.9 0.4 collective-permute-done.5.refs_8_
  22.4 8.4 %collective-permute-start.6 = (bf16[128,1536]{1,0:T(8,128)(2,1)S(1)}, bf16[128,1536]{1,0:T(8,128)(2,1)S(1)}, u32[]{:S(2)}, u32[]{:S(2)}) collective-permute-start(bf16[128,1536]{1,0:T(8,128)(2,1)S(1)} %collective-permute-done.5.refs_8_), channel_id=1, source_target_pairs={{0,64},{64,128},{128,192},{192,256},{256,320},{320,384},{384,448},... | collective-permute-start | bytes 1179656 | tf_op jit(solution)/shard_map/ppermute | solution.py:22
  30.8 5.2 %collective-permute-done.3.refs_5_ = bf16[128,1536]{1,0:T(8,128)(2,1)S(1)} collective-permute-done((bf16[128,1536]{1,0:T(8,128)(2,1)S(1)}, bf16[128,1536]{1,0:T(8,128)(2,1)S(1)}, u32[]{:S(2)}, u32[]{:S(2)}) %collective-permute-start.3) | collective-permute-done | bytes 393248 | tf_op jit(solution)/shard_map/ppermute | solution.py:22
  36.0 4.5 %collective-permute-start.4 = (bf16[128,1536]{1,0:T(8,128)(2,1)S(1)}, bf16[128,1536]{1,0:T(8,128)(2,1)S(1)}, u32[]{:S(2)}, u32[]{:S(2)}) collective-permute-start(bf16[128,1536]{1,0:T(8,128)(2,1)S(1)} %collective-permute-done.3.refs_5_), channel_id=1, source_target_pairs={{0,448},{64,0},{128,64},{192,128},{256,192},{320,256},{384,320},{4... | collective-permute-start | bytes 1179656 | tf_op jit(solution)/shard_map/ppermute | solution.py:22
  40.5 0.0 collective-permute-done.1.refs_2_
  40.5 1.9 %collective-permute-start.11 = (bf16[128,1536]{1,0:T(8,128)(2,1)S(1)}, bf16[128,1536]{1,0:T(8,128)(2,1)}, u32[]{:S(2)}, u32[]{:S(2)}) collective-permute-start(bf16[128,1536]{1,0:T(8,128)(2,1)S(1)} %collective-permute-done.5.refs_8_), channel_id=1, source_target_pairs={{0,8},{8,0},{1,9},{9,1},{2,10},{10,2},{3,11},{11,3},{4,12},{12,4},... | collective-permute-start | bytes 1179656 | tf_op jit(solution)/shard_map/ppermute | solution.py:30
  42.5 0.0 collective-permute-done.refs_1_
  42.5 2.4 %collective-permute-start.8 = (bf16[128,1536]{1,0:T(8,128)(2,1)S(1)}, bf16[128,1536]{1,0:T(8,128)(2,1)}, u32[]{:S(2)}, u32[]{:S(2)}) collective-permute-start(bf16[128,1536]{1,0:T(8,128)(2,1)S(1)} %collective-permute-done.3.refs_5_), channel_id=1, source_target_pairs={{0,8},{8,0},{1,9},{9,1},{2,10},{10,2},{3,11},{11,3},{4,12},{12,4},... | collective-permute-start | bytes 1179656 | tf_op jit(solution)/shard_map/ppermute | solution.py:30
  44.9 0.0 collective-permute-done.7.refs_9_
  44.9 1.9 %collective-permute-start.2 = (bf16[128,1536]{1,0:T(8,128)(2,1)S(1)}, bf16[128,1536]{1,0:T(8,128)(2,1)}, u32[]{:S(2)}, u32[]{:S(2)}) collective-permute-start(bf16[128,1536]{1,0:T(8,128)(2,1)S(1)} %collective-permute-done.1.refs_2_), channel_id=1, source_target_pairs={{0,16},{16,0},{32,48},{48,32},{1,17},{17,1},{33,49},{49,33},{2,18}... | collective-permute-start | bytes 1179656 | tf_op jit(solution)/shard_map/ppermute | solution.py:26
  46.8 0.0 collective-permute-done.6.refs_7_
  46.8 1.9 %collective-permute-start.10 = (bf16[128,1536]{1,0:T(8,128)(2,1)S(1)}, bf16[128,1536]{1,0:T(8,128)(2,1)}, u32[]{:S(2)}, u32[]{:S(2)}) collective-permute-start(bf16[128,1536]{1,0:T(8,128)(2,1)S(1)} %collective-permute-done.6.refs_7_), channel_id=1, source_target_pairs={{0,8},{8,0},{1,9},{9,1},{2,10},{10,2},{3,11},{11,3},{4,12},{12,4},... | collective-permute-start | bytes 1179656 | tf_op jit(solution)/shard_map/ppermute | solution.py:30
  48.8 0.3 collective-permute-done.4.refs_6_
  49.0 2.1 %collective-permute-start.9 = (bf16[128,1536]{1,0:T(8,128)(2,1)S(1)}, bf16[128,1536]{1,0:T(8,128)(2,1)}, u32[]{:S(2)}, u32[]{:S(2)}) collective-permute-start(bf16[128,1536]{1,0:T(8,128)(2,1)S(1)} %collective-permute-done.4.refs_6_), channel_id=1, source_target_pairs={{0,8},{8,0},{1,9},{9,1},{2,10},{10,2},{3,11},{11,3},{4,12},{12,4},... | collective-permute-start | bytes 1179656 | tf_op jit(solution)/shard_map/ppermute | solution.py:30
  51.2 0.1 pad_add_fusion.place_ref
  51.3 6.7 %collective-permute-done.2.refs_3_ = bf16[128,1536]{1,0:T(8,128)(2,1)} collective-permute-done((bf16[128,1536]{1,0:T(8,128)(2,1)S(1)}, bf16[128,1536]{1,0:T(8,128)(2,1)}, u32[]{:S(2)}, u32[]{:S(2)}) %collective-permute-start.2) | collective-permute-done | bytes 393248 | tf_op jit(solution)/shard_map/ppermute | solution.py:26
  57.9 0.0 collective-permute-done.11.refs_13_
  57.9 0.0 collective-permute-done.8.refs_10_
  57.9 0.0 collective-permute-done.10.refs_12_
  57.9 0.0 collective-permute-done.9.refs_11_
  57.9 4.0 %shard_map.37 = bf16[4,34,32,128]{3,2,1,0:T(8,128)(2,1)S(1)} custom-call(s32[2]{0:T(128)S(1)} %pad_add_fusion.place_ref, bf16[128,1536]{1,0:T(8,128)(2,1)S(1)} %get-tuple-element.5.refs_0_, bf16[128,1536]{1,0:T(8,128)(2,1)S(1)} %collective-permute-done.refs_1_, bf16[128,1536]{1,0:T(8,128)(2,1)S(1)} %collective-permute-done.1.refs_2_, ...), custom_call_target="tpu_custom_call" | custom-call | tf_op jit(solution)/shard_map/pallas_call | solution.py:128
  61.9 19.2 %all_to_all.10.parts_ref = bf16[4,34,32,128]{3,2,1,0:T(8,128)(2,1)S(1)} all-to-all(bf16[4,34,32,128]{3,2,1,0:T(8,128)(2,1)S(1)} %shard_map.37), channel_id=1, replica_groups=mesh['y'=8,'zl'=4,'core'=2,'x'=4,'zh'=2] {'x'}, dimensions={0} | all-to-all | bytes 2228224 | tf_op jit(solution)/shard_map/all_to_all | solution.py:140
  81.1 0.1 shard_map.38
  81.3 19.5 %all_to_all.11.parts_ref = bf16[8,10,16,128]{3,2,1,0:T(8,128)(2,1)S(1)} all-to-all(bf16[8,10,16,128]{3,2,1,0:T(8,128)(2,1)S(1)} %shard_map.38), channel_id=1, replica_groups=mesh['y'=8,'zl'=4,'core'=2,'x'=4,'zh'=2] {'zl','zh'}, dimensions={0} | all-to-all | bytes 655360 | tf_op jit(solution)/shard_map/all_to_all | solution.py:148
  100.7 1.3 %shard_map.39 = f32[1,33,16,128]{3,2,1,0:T(8,128)} custom-call(s32[2]{0:T(128)S(1)} %pad_add_fusion.place_ref, bf16[8,10,16,128]{3,2,1,0:T(8,128)(2,1)S(1)} %all_to_all.11.parts_ref), custom_call_target="tpu_custom_call" | custom-call | tf_op jit(solution)/shard_map/pallas_call | solution.py:150
  (1 shorter events, 0.0 us)
Async XLA Ops:
  1.9 20.5 %collective-permute-start.5 = (bf16[128,1536]{1,0:T(8,128)(2,1)S(1)}, bf16[128,1536]{1,0:T(8,128)(2,1)S(1)}, u32[]{:S(2)}, u32[]{:S(2)}) collective-permute-start(bf16[128,1536]{1,0:T(8,128)(2,1)S(1)} %get-tuple-element.6.refs_4_), channel_id=1, source_target_pairs={{0,256},{64,320},{128,384},{192,448},{256,0},{320,64},{384,128},{4... | collective-permute-start | bytes 1179656 | tf_op jit(solution)/shard_map/ppermute | solution.py:22
  9.6 26.4 %collective-permute-start.3 = (bf16[128,1536]{1,0:T(8,128)(2,1)S(1)}, bf16[128,1536]{1,0:T(8,128)(2,1)S(1)}, u32[]{:S(2)}, u32[]{:S(2)}) collective-permute-start(bf16[128,1536]{1,0:T(8,128)(2,1)S(1)} %get-tuple-element.6.refs_4_), channel_id=1, source_target_pairs={{0,448},{64,0},{128,64},{192,128},{256,192},{320,256},{384,320},{4... | collective-permute-start | bytes 1179656 | tf_op jit(solution)/shard_map/ppermute | solution.py:22
  12.0 28.6 %collective-permute-start.1 = (bf16[128,1536]{1,0:T(8,128)(2,1)S(1)}, bf16[128,1536]{1,0:T(8,128)(2,1)S(1)}, u32[]{:S(2)}, u32[]{:S(2)}) collective-permute-start(bf16[128,1536]{1,0:T(8,128)(2,1)S(1)} %get-tuple-element.5.refs_0_), channel_id=1, source_target_pairs={{0,32},{16,48},{32,0},{48,16},{1,33},{17,49},{33,1},{49,17},{2,34}... | collective-permute-start | bytes 1179656 | tf_op jit(solution)/shard_map/ppermute | solution.py:26
  18.1 24.4 %collective-permute-start = (bf16[128,1536]{1,0:T(8,128)(2,1)S(1)}, bf16[128,1536]{1,0:T(8,128)(2,1)S(1)}, u32[]{:S(2)}, u32[]{:S(2)}) collective-permute-start(bf16[128,1536]{1,0:T(8,128)(2,1)S(1)} %get-tuple-element.5.refs_0_), channel_id=1, source_target_pairs={{0,16},{16,0},{32,48},{48,32},{1,17},{17,1},{33,49},{49,33},{2,18}... | collective-permute-start | bytes 1179656 | tf_op jit(solution)/shard_map/ppermute | solution.py:26
  20.0 24.9 %collective-permute-start.7 = (bf16[128,1536]{1,0:T(8,128)(2,1)S(1)}, bf16[128,1536]{1,0:T(8,128)(2,1)S(1)}, u32[]{:S(2)}, u32[]{:S(2)}) collective-permute-start(bf16[128,1536]{1,0:T(8,128)(2,1)S(1)} %get-tuple-element.6.refs_4_), channel_id=1, source_target_pairs={{0,8},{8,0},{1,9},{9,1},{2,10},{10,2},{3,11},{11,3},{4,12},{12,4},... | collective-permute-start | bytes 1179656 | tf_op jit(solution)/shard_map/ppermute | solution.py:30
  22.4 24.5 %collective-permute-start.6 = (bf16[128,1536]{1,0:T(8,128)(2,1)S(1)}, bf16[128,1536]{1,0:T(8,128)(2,1)S(1)}, u32[]{:S(2)}, u32[]{:S(2)}) collective-permute-start(bf16[128,1536]{1,0:T(8,128)(2,1)S(1)} %collective-permute-done.5.refs_8_), channel_id=1, source_target_pairs={{0,64},{64,128},{128,192},{192,256},{256,320},{320,384},{384,448},... | collective-permute-start | bytes 1179656 | tf_op jit(solution)/shard_map/ppermute | solution.py:22
  36.0 13.1 %collective-permute-start.4 = (bf16[128,1536]{1,0:T(8,128)(2,1)S(1)}, bf16[128,1536]{1,0:T(8,128)(2,1)S(1)}, u32[]{:S(2)}, u32[]{:S(2)}) collective-permute-start(bf16[128,1536]{1,0:T(8,128)(2,1)S(1)} %collective-permute-done.3.refs_5_), channel_id=1, source_target_pairs={{0,448},{64,0},{128,64},{192,128},{256,192},{320,256},{384,320},{4... | collective-permute-start | bytes 1179656 | tf_op jit(solution)/shard_map/ppermute | solution.py:22
  40.5 17.4 %collective-permute-start.11 = (bf16[128,1536]{1,0:T(8,128)(2,1)S(1)}, bf16[128,1536]{1,0:T(8,128)(2,1)}, u32[]{:S(2)}, u32[]{:S(2)}) collective-permute-start(bf16[128,1536]{1,0:T(8,128)(2,1)S(1)} %collective-permute-done.5.refs_8_), channel_id=1, source_target_pairs={{0,8},{8,0},{1,9},{9,1},{2,10},{10,2},{3,11},{11,3},{4,12},{12,4},... | collective-permute-start | bytes 1179656 | tf_op jit(solution)/shard_map/ppermute | solution.py:30
  42.5 15.5 %collective-permute-start.8 = (bf16[128,1536]{1,0:T(8,128)(2,1)S(1)}, bf16[128,1536]{1,0:T(8,128)(2,1)}, u32[]{:S(2)}, u32[]{:S(2)}) collective-permute-start(bf16[128,1536]{1,0:T(8,128)(2,1)S(1)} %collective-permute-done.3.refs_5_), channel_id=1, source_target_pairs={{0,8},{8,0},{1,9},{9,1},{2,10},{10,2},{3,11},{11,3},{4,12},{12,4},... | collective-permute-start | bytes 1179656 | tf_op jit(solution)/shard_map/ppermute | solution.py:30
  44.9 13.0 %collective-permute-start.2 = (bf16[128,1536]{1,0:T(8,128)(2,1)S(1)}, bf16[128,1536]{1,0:T(8,128)(2,1)}, u32[]{:S(2)}, u32[]{:S(2)}) collective-permute-start(bf16[128,1536]{1,0:T(8,128)(2,1)S(1)} %collective-permute-done.1.refs_2_), channel_id=1, source_target_pairs={{0,16},{16,0},{32,48},{48,32},{1,17},{17,1},{33,49},{49,33},{2,18}... | collective-permute-start | bytes 1179656 | tf_op jit(solution)/shard_map/ppermute | solution.py:26
  46.8 11.1 %collective-permute-start.10 = (bf16[128,1536]{1,0:T(8,128)(2,1)S(1)}, bf16[128,1536]{1,0:T(8,128)(2,1)}, u32[]{:S(2)}, u32[]{:S(2)}) collective-permute-start(bf16[128,1536]{1,0:T(8,128)(2,1)S(1)} %collective-permute-done.6.refs_7_), channel_id=1, source_target_pairs={{0,8},{8,0},{1,9},{9,1},{2,10},{10,2},{3,11},{11,3},{4,12},{12,4},... | collective-permute-start | bytes 1179656 | tf_op jit(solution)/shard_map/ppermute | solution.py:30
  49.0 8.9 %collective-permute-start.9 = (bf16[128,1536]{1,0:T(8,128)(2,1)S(1)}, bf16[128,1536]{1,0:T(8,128)(2,1)}, u32[]{:S(2)}, u32[]{:S(2)}) collective-permute-start(bf16[128,1536]{1,0:T(8,128)(2,1)S(1)} %collective-permute-done.4.refs_6_), channel_id=1, source_target_pairs={{0,8},{8,0},{1,9},{9,1},{2,10},{10,2},{3,11},{11,3},{4,12},{12,4},... | collective-permute-start | bytes 1179656 | tf_op jit(solution)/shard_map/ppermute | solution.py:30

commit v4 on v3

--- a/solution.py
+++ b/solution.py
@@ -116,19 +116,21 @@
     weighted = (masked.astype(jnp.float32) * weights[None, :]).astype(jnp.bfloat16)
     place = jnp.stack([lax.axis_index("zl"), lax.axis_index("core")]).astype(jnp.int32)
 
+    tie = lax.optimization_barrier
+    r1, r4 = ahead(masked, 1), ahead(masked, 4)
     z2, z1 = across(weighted, 2), across(weighted, 1)
+    r2, r3 = ahead(r1, 1), ahead(r4, -1)
+    r4, z2 = tie((r4, z2))
     z3 = across(z2, 1)
-    r4, r1 = ahead(masked, 4), ahead(masked, 1)
-    r3, r2 = ahead(r4, -1), ahead(r1, 1)
+    pair = jnp.concatenate([masked, r1])
     lefts = [weighted, z1, z2, z3]
-    rights = [masked, r1, r2, r3, r4]
-    rights = rights + [swapped(b) for b in rights]
+    rights = [pair, r2, r3, r4, swapped(pair), swapped(r2), swapped(r3), swapped(r4)]
 
     share, half = rows // SIZES["x"], rows // (SIZES["x"] * SIZES["zh"])
     tiles = pl.pallas_call(
         tiles_kernel,
         out_shape=jax.ShapeDtypeStruct((SIZES["x"], 4 * EACH + 2, share, rows), jnp.bfloat16),
-        in_specs=[SMEM] + [VMEM] * 14,
+        in_specs=[SMEM] + [VMEM] * 12,
         out_specs=VMEM,
         scratch_shapes=[
             pltpu.VMEM((4 * rows, points), jnp.bfloat16),

time: 103 us -> 102 us (level)
  the two profiles are of different devices: /device:TPU:64 before, /device:TPU:56 now
where the time goes in v4:
time: 102 us; the launch traced here: 101 us
  starting transfers between devices  39.9 us (39%)
  blocking collectives  39.8 us (39%)
  waiting for transfers between devices  13.9 us (14%)
  Pallas kernels  5.41 us (5%)
  other arithmetic  1.33 us (1%)
    all_to_all x1, blocking collectives, on_device(): parts = lax.all_to_all(tiles, 'x', 0, 0, tiled=True)  20 us
    all_to_all x1, blocking collectives, on_device(): shares = lax.all_to_all(sums, ('zl', 'zh'), 0, 0, tiled=True)  19.8 us
    ppermute x3, starting transfers between devices, across(): lax.ppermute(block, 'zl', [(i, i ^ flip) for i in range(SIZES['zl'])])  17.4 us
    ppermute x4, starting transfers between devices, ahead(): lax.ppermute(block, 'y', [(i, (i - by) % SIZES['y']) for i in range(SIZES...  14.1 us
    ppermute x4, waiting for transfers between devices, ahead(): lax.ppermute(block, 'y', [(i, (i - by) % SIZES['y']) for i in range(SIZES...  10.6 us
    ppermute x4, starting transfers between devices, swapped(): return lax.ppermute(block, 'core', [(0, 1), (1, 0)])  8.38 us
    pallas_call x1, Pallas kernels, on_device(): pl.pallas_call(tiles_kernel, out_shape=jax.ShapeDtypeStruct((SIZES['x'],...  3.97 us
    ppermute x3, waiting for transfers between devices, across(): lax.ppermute(block, 'zl', [(i, i ^ flip) for i in range(SIZES['zl'])])  3.28 us
  transfers between devices with their start and end apart: 11, of which 2 were waited for; matrix products, arithmetic and copies ran while one was open for 0% of the time, Pallas kernels for 0%

profile of v4, /device:TPU:56, one launch (start us, length us, event | category | flops | bytes accessed | tf_op | source)
XLA Modules:
  0.0 101.1 jit_solution(3476543875834384176)
XLA Ops:
  0.7 1.2 %multiply_convert_fusion = (bf16[128,1536]{1,0:T(8,128)(2,1)S(1)}, bf16[128,1536]{1,0:T(8,128)(2,1)S(1)}) fusion(f32[1536]{0:T(1024)} %param.5, bf16[128,1536]{1,0:T(8,128)(2,1)} %param.3, pred[128]{0:T(512)(128)(4,1)S(1)} %iota_compare_fusion), kind=kLoop, calls=%fused_computation.1 | loop fusion | flops 786432 | bytes 1185920 | tf_op jit(solution)/shard_map/convert_element_type | solution.py:116
  1.9 3.3 %collective-permute-start.4 = (bf16[128,1536]{1,0:T(8,128)(2,1)S(1)}, bf16[128,1536]{1,0:T(8,128)(2,1)S(1)}, u32[]{:S(2)}, u32[]{:S(2)}) collective-permute-start(bf16[128,1536]{1,0:T(8,128)(2,1)S(1)} %get-tuple-element.10), channel_id=1, source_target_pairs={{0,448},{64,0},{128,64},{192,128},{256,192},{320,256},{384,320},{4... | collective-permute-start | bytes 1179656 | tf_op jit(solution)/shard_map/ppermute | solution.py:22
  5.1 3.8 %collective-permute-start.1 = (bf16[128,1536]{1,0:T(8,128)(2,1)S(1)}, bf16[128,1536]{1,0:T(8,128)(2,1)S(1)}, u32[]{:S(2)}, u32[]{:S(2)}) collective-permute-start(bf16[128,1536]{1,0:T(8,128)(2,1)S(1)} %get-tuple-element.10), channel_id=1, source_target_pairs={{0,256},{64,320},{128,384},{192,448},{256,0},{320,64},{384,128},{4... | collective-permute-start | bytes 1179656 | tf_op jit(solution)/shard_map/ppermute | solution.py:22
  8.9 6.1 %collective-permute-start.2 = (bf16[128,1536]{1,0:T(8,128)(2,1)S(1)}, bf16[128,1536]{1,0:T(8,128)(2,1)S(1)}, u32[]{:S(2)}, u32[]{:S(2)}) collective-permute-start(bf16[128,1536]{1,0:T(8,128)(2,1)S(1)} %get-tuple-element.9.refs_0_), channel_id=1, source_target_pairs={{0,32},{16,48},{32,0},{48,16},{1,33},{17,49},{33,1},{49,17},{2,34}... | collective-permute-start | bytes 1179656 | tf_op jit(solution)/shard_map/ppermute | solution.py:26
  15.0 4.3 %collective-permute-start = (bf16[128,1536]{1,0:T(8,128)(2,1)S(1)}, bf16[128,1536]{1,0:T(8,128)(2,1)S(1)}, u32[]{:S(2)}, u32[]{:S(2)}) collective-permute-start(bf16[128,1536]{1,0:T(8,128)(2,1)S(1)} %get-tuple-element.9.refs_0_), channel_id=1, source_target_pairs={{0,16},{16,0},{32,48},{48,32},{1,17},{17,1},{33,49},{49,33},{2,18}... | collective-permute-start | bytes 1179656 | tf_op jit(solution)/shard_map/ppermute | solution.py:26
  19.3 10.6 %collective-permute-done.4 = bf16[128,1536]{1,0:T(8,128)(2,1)S(1)} collective-permute-done((bf16[128,1536]{1,0:T(8,128)(2,1)S(1)}, bf16[128,1536]{1,0:T(8,128)(2,1)S(1)}, u32[]{:S(2)}, u32[]{:S(2)}) %collective-permute-start.4) | collective-permute-done | bytes 393248 | tf_op jit(solution)/shard_map/ppermute | solution.py:22
  29.9 1.9 %collective-permute-start.5 = (bf16[128,1536]{1,0:T(8,128)(2,1)S(1)}, bf16[128,1536]{1,0:T(8,128)(2,1)S(1)}, u32[]{:S(2)}, u32[]{:S(2)}) collective-permute-start(bf16[128,1536]{1,0:T(8,128)(2,1)S(1)} %collective-permute-done.4), channel_id=1, source_target_pairs={{0,448},{64,0},{128,64},{192,128},{256,192},{320,256},{384,320},{4... | collective-permute-start | bytes 1179656 | tf_op jit(solution)/shard_map/ppermute | solution.py:22
  31.8 0.0 collective-permute-done.1.refs_7_
  31.8 5.1 %collective-permute-start.6 = (bf16[128,1536]{1,0:T(8,128)(2,1)S(1)}, bf16[128,1536]{1,0:T(8,128)(2,1)}, u32[]{:S(2)}, u32[]{:S(2)}) collective-permute-start(bf16[128,1536]{1,0:T(8,128)(2,1)S(1)} %collective-permute-done.1.refs_7_), channel_id=1, source_target_pairs={{0,64},{64,128},{128,192},{192,256},{256,320},{320,384},{384,448},... | collective-permute-start | bytes 1179656 | tf_op jit(solution)/shard_map/ppermute | solution.py:22
  37.0 0.1 pad_maximum_fusion.refs_4_
  37.0 1.9 %collective-permute-start.7 = (bf16[256,1536]{1,0:T(8,128)(2,1)S(1)}, bf16[256,1536]{1,0:T(8,128)(2,1)S(1)}, u32[]{:S(2)}, u32[]{:S(2)}) collective-permute-start(bf16[256,1536]{1,0:T(8,128)(2,1)S(1)} %pad_maximum_fusion.refs_4_), channel_id=1, source_target_pairs={{0,8},{8,0},{1,9},{9,1},{2,10},{10,2},{3,11},{11,3},{4,12},{12,4},... | collective-permute-start | bytes 2359304 | tf_op jit(solution)/shard_map/ppermute | solution.py:30
  39.0 0.0 collective-permute-done.2.refs_2_
  39.0 7.0 %collective-permute-start.3 = (bf16[128,1536]{1,0:T(8,128)(2,1)S(1)}, bf16[128,1536]{1,0:T(8,128)(2,1)}, u32[]{:S(2)}, u32[]{:S(2)}) collective-permute-start(bf16[128,1536]{1,0:T(8,128)(2,1)S(1)} %collective-permute-done.2.refs_2_), channel_id=1, source_target_pairs={{0,16},{16,0},{32,48},{48,32},{1,17},{17,1},{33,49},{49,33},{2,18}... | collective-permute-start | bytes 1179656 | tf_op jit(solution)/shard_map/ppermute | solution.py:26
  46.0 0.0 collective-permute-done.refs_1_
  46.0 2.1 %collective-permute-start.10 = (bf16[128,1536]{1,0:T(8,128)(2,1)S(1)}, bf16[128,1536]{1,0:T(8,128)(2,1)}, u32[]{:S(2)}, u32[]{:S(2)}) collective-permute-start(bf16[128,1536]{1,0:T(8,128)(2,1)S(1)} %collective-permute-done.1.refs_7_), channel_id=1, source_target_pairs={{0,8},{8,0},{1,9},{9,1},{2,10},{10,2},{3,11},{11,3},{4,12},{12,4},... | collective-permute-start | bytes 1179656 | tf_op jit(solution)/shard_map/ppermute | solution.py:30
  48.2 0.0 collective-permute-done.5.refs_5_
  48.2 2.2 %collective-permute-start.8 = (bf16[128,1536]{1,0:T(8,128)(2,1)S(1)}, bf16[128,1536]{1,0:T(8,128)(2,1)}, u32[]{:S(2)}, u32[]{:S(2)}) collective-permute-start(bf16[128,1536]{1,0:T(8,128)(2,1)S(1)} %collective-permute-done.5.refs_5_), channel_id=1, source_target_pairs={{0,8},{8,0},{1,9},{9,1},{2,10},{10,2},{3,11},{11,3},{4,12},{12,4},... | collective-permute-start | bytes 1179656 | tf_op jit(solution)/shard_map/ppermute | solution.py:30
  50.4 0.0 collective-permute-done.6.refs_6_
  50.4 2.1 %collective-permute-start.9 = (bf16[128,1536]{1,0:T(8,128)(2,1)}, bf16[128,1536]{1,0:T(8,128)(2,1)}, u32[]{:S(2)}, u32[]{:S(2)}) collective-permute-start(bf16[128,1536]{1,0:T(8,128)(2,1)} %collective-permute-done.6.refs_6_), channel_id=1, source_target_pairs={{0,8},{8,0},{1,9},{9,1},{2,10},{10,2},{3,11},{11,3},{4,12},{12,4},... | collective-permute-start | bytes 1179656 | tf_op jit(solution)/shard_map/ppermute | solution.py:30
  52.5 0.1 pad_add_fusion.place_ref
  52.6 3.3 %collective-permute-done.3.refs_3_ = bf16[128,1536]{1,0:T(8,128)(2,1)} collective-permute-done((bf16[128,1536]{1,0:T(8,128)(2,1)S(1)}, bf16[128,1536]{1,0:T(8,128)(2,1)}, u32[]{:S(2)}, u32[]{:S(2)}) %collective-permute-start.3) | collective-permute-done | bytes 393248 | tf_op jit(solution)/shard_map/ppermute | solution.py:26
  55.9 0.0 collective-permute-done.10.refs_11_
  55.9 0.0 collective-permute-done.8.refs_9_
  55.9 0.0 collective-permute-done.9.refs_10_
  55.9 0.0 collective-permute-done.7.refs_8_
  55.9 4.0 %shard_map.37 = bf16[4,34,32,128]{3,2,1,0:T(8,128)(2,1)S(1)} custom-call(s32[2]{0:T(128)S(1)} %pad_add_fusion.place_ref, bf16[128,1536]{1,0:T(8,128)(2,1)S(1)} %get-tuple-element.9.refs_0_, bf16[128,1536]{1,0:T(8,128)(2,1)S(1)} %collective-permute-done.refs_1_, bf16[128,1536]{1,0:T(8,128)(2,1)S(1)} %collective-permute-done.2.refs_2_, ...), custom_call_target="tpu_custom_call" | custom-call | tf_op jit(solution)/shard_map/pallas_call | solution.py:130
  59.9 20.0 %all_to_all.10.parts_ref = bf16[4,34,32,128]{3,2,1,0:T(8,128)(2,1)S(1)} all-to-all(bf16[4,34,32,128]{3,2,1,0:T(8,128)(2,1)S(1)} %shard_map.37), channel_id=1, replica_groups=mesh['y'=8,'zl'=4,'core'=2,'x'=4,'zh'=2] {'x'}, dimensions={0} | all-to-all | bytes 2228224 | tf_op jit(solution)/shard_map/all_to_all | solution.py:142
  79.9 0.1 shard_map.38
  80.0 19.8 %all_to_all.11.parts_ref = bf16[8,10,16,128]{3,2,1,0:T(8,128)(2,1)S(1)} all-to-all(bf16[8,10,16,128]{3,2,1,0:T(8,128)(2,1)S(1)} %shard_map.38), channel_id=1, replica_groups=mesh['y'=8,'zl'=4,'core'=2,'x'=4,'zh'=2] {'zl','zh'}, dimensions={0} | all-to-all | bytes 655360 | tf_op jit(solution)/shard_map/all_to_all | solution.py:150
  99.8 1.3 %shard_map.39 = f32[1,33,16,128]{3,2,1,0:T(8,128)} custom-call(s32[2]{0:T(128)S(1)} %pad_add_fusion.place_ref, bf16[8,10,16,128]{3,2,1,0:T(8,128)(2,1)S(1)} %all_to_all.11.parts_ref), custom_call_target="tpu_custom_call" | custom-call | tf_op jit(solution)/shard_map/pallas_call | solution.py:152
  (1 shorter events, 0.0 us)
Async XLA Ops:
  1.9 28.1 %collective-permute-start.4 = (bf16[128,1536]{1,0:T(8,128)(2,1)S(1)}, bf16[128,1536]{1,0:T(8,128)(2,1)S(1)}, u32[]{:S(2)}, u32[]{:S(2)}) collective-permute-start(bf16[128,1536]{1,0:T(8,128)(2,1)S(1)} %get-tuple-element.10), channel_id=1, source_target_pairs={{0,448},{64,0},{128,64},{192,128},{256,192},{320,256},{384,320},{4... | collective-permute-start | bytes 1179656 | tf_op jit(solution)/shard_map/ppermute | solution.py:22
  5.1 26.7 %collective-permute-start.1 = (bf16[128,1536]{1,0:T(8,128)(2,1)S(1)}, bf16[128,1536]{1,0:T(8,128)(2,1)S(1)}, u32[]{:S(2)}, u32[]{:S(2)}) collective-permute-start(bf16[128,1536]{1,0:T(8,128)(2,1)S(1)} %get-tuple-element.10), channel_id=1, source_target_pairs={{0,256},{64,320},{128,384},{192,448},{256,0},{320,64},{384,128},{4... | collective-permute-start | bytes 1179656 | tf_op jit(solution)/shard_map/ppermute | solution.py:22
  8.9 30.0 %collective-permute-start.2 = (bf16[128,1536]{1,0:T(8,128)(2,1)S(1)}, bf16[128,1536]{1,0:T(8,128)(2,1)S(1)}, u32[]{:S(2)}, u32[]{:S(2)}) collective-permute-start(bf16[128,1536]{1,0:T(8,128)(2,1)S(1)} %get-tuple-element.9.refs_0_), channel_id=1, source_target_pairs={{0,32},{16,48},{32,0},{48,16},{1,33},{17,49},{33,1},{49,17},{2,34}... | collective-permute-start | bytes 1179656 | tf_op jit(solution)/shard_map/ppermute | solution.py:26
  15.0 31.0 %collective-permute-start = (bf16[128,1536]{1,0:T(8,128)(2,1)S(1)}, bf16[128,1536]{1,0:T(8,128)(2,1)S(1)}, u32[]{:S(2)}, u32[]{:S(2)}) collective-permute-start(bf16[128,1536]{1,0:T(8,128)(2,1)S(1)} %get-tuple-element.9.refs_0_), channel_id=1, source_target_pairs={{0,16},{16,0},{32,48},{48,32},{1,17},{17,1},{33,49},{49,33},{2,18}... | collective-permute-start | bytes 1179656 | tf_op jit(solution)/shard_map/ppermute | solution.py:26
  29.9 18.3 %collective-permute-start.5 = (bf16[128,1536]{1,0:T(8,128)(2,1)S(1)}, bf16[128,1536]{1,0:T(8,128)(2,1)S(1)}, u32[]{:S(2)}, u32[]{:S(2)}) collective-permute-start(bf16[128,1536]{1,0:T(8,128)(2,1)S(1)} %collective-permute-done.4), channel_id=1, source_target_pairs={{0,448},{64,0},{128,64},{192,128},{256,192},{320,256},{384,320},{4... | collective-permute-start | bytes 1179656 | tf_op jit(solution)/shard_map/ppermute | solution.py:22
  31.8 18.6 %collective-permute-start.6 = (bf16[128,1536]{1,0:T(8,128)(2,1)S(1)}, bf16[128,1536]{1,0:T(8,128)(2,1)}, u32[]{:S(2)}, u32[]{:S(2)}) collective-permute-start(bf16[128,1536]{1,0:T(8,128)(2,1)S(1)} %collective-permute-done.1.refs_7_), channel_id=1, source_target_pairs={{0,64},{64,128},{128,192},{192,256},{256,320},{320,384},{384,448},... | collective-permute-start | bytes 1179656 | tf_op jit(solution)/shard_map/ppermute | solution.py:22
  37.0 18.9 %collective-permute-start.7 = (bf16[256,1536]{1,0:T(8,128)(2,1)S(1)}, bf16[256,1536]{1,0:T(8,128)(2,1)S(1)}, u32[]{:S(2)}, u32[]{:S(2)}) collective-permute-start(bf16[256,1536]{1,0:T(8,128)(2,1)S(1)} %pad_maximum_fusion.refs_4_), channel_id=1, source_target_pairs={{0,8},{8,0},{1,9},{9,1},{2,10},{10,2},{3,11},{11,3},{4,12},{12,4},... | collective-permute-start | bytes 2359304 | tf_op jit(solution)/shard_map/ppermute | solution.py:30
  39.0 16.9 %collective-permute-start.3 = (bf16[128,1536]{1,0:T(8,128)(2,1)S(1)}, bf16[128,1536]{1,0:T(8,128)(2,1)}, u32[]{:S(2)}, u32[]{:S(2)}) collective-permute-start(bf16[128,1536]{1,0:T(8,128)(2,1)S(1)} %collective-permute-done.2.refs_2_), channel_id=1, source_target_pairs={{0,16},{16,0},{32,48},{48,32},{1,17},{17,1},{33,49},{49,33},{2,18}... | collective-permute-start | bytes 1179656 | tf_op jit(solution)/shard_map/ppermute | solution.py:26
  46.0 9.9 %collective-permute-start.10 = (bf16[128,1536]{1,0:T(8,128)(2,1)S(1)}, bf16[128,1536]{1,0:T(8,128)(2,1)}, u32[]{:S(2)}, u32[]{:S(2)}) collective-permute-start(bf16[128,1536]{1,0:T(8,128)(2,1)S(1)} %collective-permute-done.1.refs_7_), channel_id=1, source_target_pairs={{0,8},{8,0},{1,9},{9,1},{2,10},{10,2},{3,11},{11,3},{4,12},{12,4},... | collective-permute-start | bytes 1179656 | tf_op jit(solution)/shard_map/ppermute | solution.py:30
  48.2 7.7 %collective-permute-start.8 = (bf16[128,1536]{1,0:T(8,128)(2,1)S(1)}, bf16[128,1536]{1,0:T(8,128)(2,1)}, u32[]{:S(2)}, u32[]{:S(2)}) collective-permute-start(bf16[128,1536]{1,0:T(8,128)(2,1)S(1)} %collective-permute-done.5.refs_5_), channel_id=1, source_target_pairs={{0,8},{8,0},{1,9},{9,1},{2,10},{10,2},{3,11},{11,3},{4,12},{12,4},... | collective-permute-start | bytes 1179656 | tf_op jit(solution)/shard_map/ppermute | solution.py:30
  50.4 5.5 %collective-permute-start.9 = (bf16[128,1536]{1,0:T(8,128)(2,1)}, bf16[128,1536]{1,0:T(8,128)(2,1)}, u32[]{:S(2)}, u32[]{:S(2)}) collective-permute-start(bf16[128,1536]{1,0:T(8,128)(2,1)} %collective-permute-done.6.refs_6_), channel_id=1, source_target_pairs={{0,8},{8,0},{1,9},{9,1},{2,10},{10,2},{3,11},{11,3},{4,12},{12,4},... | collective-permute-start | bytes 1179656 | tf_op jit(solution)/shard_map/ppermute | solution.py:30

commit v5 on v3

--- a/solution.py
+++ b/solution.py
@@ -116,13 +116,17 @@
     weighted = (masked.astype(jnp.float32) * weights[None, :]).astype(jnp.bfloat16)
     place = jnp.stack([lax.axis_index("zl"), lax.axis_index("core")]).astype(jnp.int32)
 
+    tie = lax.optimization_barrier
+    r1, r4 = ahead(masked, 1), ahead(masked, 4)
     z2, z1 = across(weighted, 2), across(weighted, 1)
+    r2 = ahead(r1, 1)
+    r4t, z1 = tie((r4, z1))
+    r3 = ahead(r4, -1)
+    r1t, z2 = tie((r1, z2))
     z3 = across(z2, 1)
-    r4, r1 = ahead(masked, 4), ahead(masked, 1)
-    r3, r2 = ahead(r4, -1), ahead(r1, 1)
     lefts = [weighted, z1, z2, z3]
     rights = [masked, r1, r2, r3, r4]
-    rights = rights + [swapped(b) for b in rights]
+    rights = rights + [swapped(b) for b in (masked, r1t, r2, r3, r4t)]
 
     share, half = rows // SIZES["x"], rows // (SIZES["x"] * SIZES["zh"])
     tiles = pl.pallas_call(

time: 103 us -> 102 us (level)
  the two profiles are of different devices: /device:TPU:64 before, /device:TPU:56 now
where the time goes in v5:
time: 102 us; the launch traced here: 101 us
  starting transfers between devices  44.5 us (44%)
  blocking collectives  39.8 us (39%)
  waiting for transfers between devices  9.26 us (9%)
  Pallas kernels  5.41 us (5%)
  other arithmetic  1.27 us (1%)
    ppermute x3, starting transfers between devices, across(): lax.ppermute(block, 'zl', [(i, i ^ flip) for i in range(SIZES['zl'])])  20.1 us
    all_to_all x1, blocking collectives, on_device(): parts = lax.all_to_all(tiles, 'x', 0, 0, tiled=True)  20 us
    all_to_all x1, blocking collectives, on_device(): shares = lax.all_to_all(sums, ('zl', 'zh'), 0, 0, tiled=True)  19.8 us
    ppermute x4, starting transfers between devices, ahead(): lax.ppermute(block, 'y', [(i, (i - by) % SIZES['y']) for i in range(SIZES...  14.1 us
    ppermute x5, starting transfers between devices, swapped(): return lax.ppermute(block, 'core', [(0, 1), (1, 0)])  10.3 us
    ppermute x4, waiting for transfers between devices, ahead(): lax.ppermute(block, 'y', [(i, (i - by) % SIZES['y']) for i in range(SIZES...  5.97 us
    pallas_call x1, Pallas kernels, on_device(): pl.pallas_call(tiles_kernel, out_shape=jax.ShapeDtypeStruct((SIZES['x'],...  3.97 us
    ppermute x3, waiting for transfers between devices, across(): lax.ppermute(block, 'zl', [(i, i ^ flip) for i in range(SIZES['zl'])])  3.28 us
  transfers between devices with their start and end apart: 12, of which 2 were waited for; matrix products, arithmetic and copies ran while one was open for 0% of the time, Pallas kernels for 0%

profile of v5, /device:TPU:56, one launch (start us, length us, event | category | flops | bytes accessed | tf_op | source)
XLA Modules:
  0.0 101.1 jit_solution(18203848173001759396)
XLA Ops:
  0.7 1.2 %multiply_convert_fusion = (bf16[128,1536]{1,0:T(8,128)(2,1)S(1)}, bf16[128,1536]{1,0:T(8,128)(2,1)S(1)}) fusion(f32[1536]{0:T(1024)} %param.5, bf16[128,1536]{1,0:T(8,128)(2,1)} %param.3, pred[128]{0:T(512)(128)(4,1)S(1)} %iota_compare_fusion), kind=kLoop, calls=%fused_computation | loop fusion | flops 786432 | bytes 1185920 | tf_op jit(solution)/shard_map/convert_element_type | solution.py:116
  1.9 3.3 %collective-permute-start.2 = (bf16[128,1536]{1,0:T(8,128)(2,1)S(1)}, bf16[128,1536]{1,0:T(8,128)(2,1)S(1)}, u32[]{:S(2)}, u32[]{:S(2)}) collective-permute-start(bf16[128,1536]{1,0:T(8,128)(2,1)S(1)} %get-tuple-element.14.refs_4_), channel_id=1, source_target_pairs={{0,448},{64,0},{128,64},{192,128},{256,192},{320,256},{384,320},{4... | collective-permute-start | bytes 1179656 | tf_op jit(solution)/shard_map/ppermute | solution.py:22
  5.1 3.8 %collective-permute-start = (bf16[128,1536]{1,0:T(8,128)(2,1)S(1)}, bf16[128,1536]{1,0:T(8,128)(2,1)S(1)}, u32[]{:S(2)}, u32[]{:S(2)}) collective-permute-start(bf16[128,1536]{1,0:T(8,128)(2,1)S(1)} %get-tuple-element.14.refs_4_), channel_id=1, source_target_pairs={{0,256},{64,320},{128,384},{192,448},{256,0},{320,64},{384,128},{4... | collective-permute-start | bytes 1179656 | tf_op jit(solution)/shard_map/ppermute | solution.py:22
  8.9 6.1 %collective-permute-start.3 = (bf16[128,1536]{1,0:T(8,128)(2,1)S(1)}, bf16[128,1536]{1,0:T(8,128)(2,1)S(1)}, u32[]{:S(2)}, u32[]{:S(2)}) collective-permute-start(bf16[128,1536]{1,0:T(8,128)(2,1)S(1)} %get-tuple-element.13.refs_0_), channel_id=1, source_target_pairs={{0,32},{16,48},{32,0},{48,16},{1,33},{17,49},{33,1},{49,17},{2,34}... | collective-permute-start | bytes 1179656 | tf_op jit(solution)/shard_map/ppermute | solution.py:26
  15.0 4.3 %collective-permute-start.1 = (bf16[128,1536]{1,0:T(8,128)(2,1)S(1)}, bf16[128,1536]{1,0:T(8,128)(2,1)S(1)}, u32[]{:S(2)}, u32[]{:S(2)}) collective-permute-start(bf16[128,1536]{1,0:T(8,128)(2,1)S(1)} %get-tuple-element.13.refs_0_), channel_id=1, source_target_pairs={{0,16},{16,0},{32,48},{48,32},{1,17},{17,1},{33,49},{49,33},{2,18}... | collective-permute-start | bytes 1179656 | tf_op jit(solution)/shard_map/ppermute | solution.py:26
  19.3 1.9 %collective-permute-start.7 = (bf16[128,1536]{1,0:T(8,128)(2,1)S(1)}, bf16[128,1536]{1,0:T(8,128)(2,1)S(1)}, u32[]{:S(2)}, u32[]{:S(2)}) collective-permute-start(bf16[128,1536]{1,0:T(8,128)(2,1)S(1)} %get-tuple-element.14.refs_4_), channel_id=1, source_target_pairs={{0,8},{8,0},{1,9},{9,1},{2,10},{10,2},{3,11},{11,3},{4,12},{12,4},... | collective-permute-start | bytes 1179656 | tf_op jit(solution)/shard_map/ppermute | solution.py:30
  21.3 6.0 %collective-permute-done.2.refs_5_ = bf16[128,1536]{1,0:T(8,128)(2,1)S(1)} collective-permute-done((bf16[128,1536]{1,0:T(8,128)(2,1)S(1)}, bf16[128,1536]{1,0:T(8,128)(2,1)S(1)}, u32[]{:S(2)}, u32[]{:S(2)}) %collective-permute-start.2) | collective-permute-done | bytes 393248 | tf_op jit(solution)/shard_map/ppermute | solution.py:22
  27.2 1.9 %collective-permute-start.5 = (bf16[128,1536]{1,0:T(8,128)(2,1)S(1)}, bf16[128,1536]{1,0:T(8,128)(2,1)S(1)}, u32[]{:S(2)}, u32[]{:S(2)}) collective-permute-start(bf16[128,1536]{1,0:T(8,128)(2,1)S(1)} %collective-permute-done.2.refs_5_), channel_id=1, source_target_pairs={{0,448},{64,0},{128,64},{192,128},{256,192},{320,256},{384,320},{4... | collective-permute-start | bytes 1179656 | tf_op jit(solution)/shard_map/ppermute | solution.py:22
  29.1 0.0 collective-permute-done.refs_8_
  29.2 5.1 %collective-permute-start.6 = (bf16[128,1536]{1,0:T(8,128)(2,1)S(1)}, bf16[128,1536]{1,0:T(8,128)(2,1)S(1)}, u32[]{:S(2)}, u32[]{:S(2)}) collective-permute-start(bf16[128,1536]{1,0:T(8,128)(2,1)S(1)} %collective-permute-done.refs_8_), channel_id=1, source_target_pairs={{0,64},{64,128},{128,192},{192,256},{256,320},{320,384},{384,448},... | collective-permute-start | bytes 1179656 | tf_op jit(solution)/shard_map/ppermute | solution.py:22
  34.3 0.0 collective-permute-done.3.refs_2_
  34.3 1.9 %collective-permute-start.8 = (bf16[128,1536]{1,0:T(8,128)(2,1)S(1)}, bf16[128,1536]{1,0:T(8,128)(2,1)}, u32[]{:S(2)}, u32[]{:S(2)}) collective-permute-start(bf16[128,1536]{1,0:T(8,128)(2,1)S(1)} %collective-permute-done.2.refs_5_), channel_id=1, source_target_pairs={{0,8},{8,0},{1,9},{9,1},{2,10},{10,2},{3,11},{11,3},{4,12},{12,4},... | collective-permute-start | bytes 1179656 | tf_op jit(solution)/shard_map/ppermute | solution.py:30
  36.2 0.0 collective-permute-done.1.refs_1_
  36.2 9.7 %collective-permute-start.4 = (bf16[128,1536]{1,0:T(8,128)(2,1)S(1)}, bf16[128,1536]{1,0:T(8,128)(2,1)}, u32[]{:S(2)}, u32[]{:S(2)}) collective-permute-start(bf16[128,1536]{1,0:T(8,128)(2,1)S(1)} %collective-permute-done.3.refs_2_), channel_id=1, source_target_pairs={{0,16},{16,0},{32,48},{48,32},{1,17},{17,1},{33,49},{49,33},{2,18}... | collective-permute-start | bytes 1179656 | tf_op jit(solution)/shard_map/ppermute | solution.py:26
  46.0 0.0 collective-permute-done.7.refs_9_
  46.0 2.1 %collective-permute-start.11 = (bf16[128,1536]{1,0:T(8,128)(2,1)S(1)}, bf16[128,1536]{1,0:T(8,128)(2,1)}, u32[]{:S(2)}, u32[]{:S(2)}) collective-permute-start(bf16[128,1536]{1,0:T(8,128)(2,1)S(1)} %collective-permute-done.refs_8_), channel_id=1, source_target_pairs={{0,8},{8,0},{1,9},{9,1},{2,10},{10,2},{3,11},{11,3},{4,12},{12,4},... | collective-permute-start | bytes 1179656 | tf_op jit(solution)/shard_map/ppermute | solution.py:30
  48.1 0.0 collective-permute-done.5.refs_6_
  48.1 2.2 %collective-permute-start.9 = (bf16[128,1536]{1,0:T(8,128)(2,1)S(1)}, bf16[128,1536]{1,0:T(8,128)(2,1)}, u32[]{:S(2)}, u32[]{:S(2)}) collective-permute-start(bf16[128,1536]{1,0:T(8,128)(2,1)S(1)} %collective-permute-done.5.refs_6_), channel_id=1, source_target_pairs={{0,8},{8,0},{1,9},{9,1},{2,10},{10,2},{3,11},{11,3},{4,12},{12,4},... | collective-permute-start | bytes 1179656 | tf_op jit(solution)/shard_map/ppermute | solution.py:30
  50.3 0.0 collective-permute-done.6.refs_7_
  50.4 2.1 %collective-permute-start.10 = (bf16[128,1536]{1,0:T(8,128)(2,1)S(1)}, bf16[128,1536]{1,0:T(8,128)(2,1)}, u32[]{:S(2)}, u32[]{:S(2)}) collective-permute-start(bf16[128,1536]{1,0:T(8,128)(2,1)S(1)} %collective-permute-done.6.refs_7_), channel_id=1, source_target_pairs={{0,8},{8,0},{1,9},{9,1},{2,10},{10,2},{3,11},{11,3},{4,12},{12,4},... | collective-permute-start | bytes 1179656 | tf_op jit(solution)/shard_map/ppermute | solution.py:30
  52.5 0.1 pad_add_fusion.place_ref
  52.6 0.0 collective-permute-done.8.refs_10_
  52.6 3.3 %collective-permute-done.4.refs_3_ = bf16[128,1536]{1,0:T(8,128)(2,1)} collective-permute-done((bf16[128,1536]{1,0:T(8,128)(2,1)S(1)}, bf16[128,1536]{1,0:T(8,128)(2,1)}, u32[]{:S(2)}, u32[]{:S(2)}) %collective-permute-start.4) | collective-permute-done | bytes 393248 | tf_op jit(solution)/shard_map/ppermute | solution.py:26
  55.8 0.0 collective-permute-done.11.refs_13_
  55.9 0.0 collective-permute-done.9.refs_11_
  55.9 0.0 collective-permute-done.10.refs_12_
  55.9 4.0 %shard_map.37 = bf16[4,34,32,128]{3,2,1,0:T(8,128)(2,1)S(1)} custom-call(s32[2]{0:T(128)S(1)} %pad_add_fusion.place_ref, bf16[128,1536]{1,0:T(8,128)(2,1)S(1)} %get-tuple-element.13.refs_0_, bf16[128,1536]{1,0:T(8,128)(2,1)S(1)} %collective-permute-done.1.refs_1_, bf16[128,1536]{1,0:T(8,128)(2,1)S(1)} %collective-permute-done.3.refs_2_, ...), custom_call_target="tpu_custom_call" | custom-call | tf_op jit(solution)/shard_map/pallas_call | solution.py:132
  59.8 20.0 %all_to_all.10.parts_ref = bf16[4,34,32,128]{3,2,1,0:T(8,128)(2,1)S(1)} all-to-all(bf16[4,34,32,128]{3,2,1,0:T(8,128)(2,1)S(1)} %shard_map.37), channel_id=1, replica_groups=mesh['y'=8,'zl'=4,'core'=2,'x'=4,'zh'=2] {'x'}, dimensions={0} | all-to-all | bytes 2228224 | tf_op jit(solution)/shard_map/all_to_all | solution.py:144
  79.8 0.1 shard_map.38
  80.0 19.8 %all_to_all.11.parts_ref = bf16[8,10,16,128]{3,2,1,0:T(8,128)(2,1)S(1)} all-to-all(bf16[8,10,16,128]{3,2,1,0:T(8,128)(2,1)S(1)} %shard_map.38), channel_id=1, replica_groups=mesh['y'=8,'zl'=4,'core'=2,'x'=4,'zh'=2] {'zl','zh'}, dimensions={0} | all-to-all | bytes 655360 | tf_op jit(solution)/shard_map/all_to_all | solution.py:152
  99.8 1.3 %shard_map.39 = f32[1,33,16,128]{3,2,1,0:T(8,128)} custom-call(s32[2]{0:T(128)S(1)} %pad_add_fusion.place_ref, bf16[8,10,16,128]{3,2,1,0:T(8,128)(2,1)S(1)} %all_to_all.11.parts_ref), custom_call_target="tpu_custom_call" | custom-call | tf_op jit(solution)/shard_map/pallas_call | solution.py:154
  (1 shorter events, 0.0 us)
Async XLA Ops:
  1.9 25.4 %collective-permute-start.2 = (bf16[128,1536]{1,0:T(8,128)(2,1)S(1)}, bf16[128,1536]{1,0:T(8,128)(2,1)S(1)}, u32[]{:S(2)}, u32[]{:S(2)}) collective-permute-start(bf16[128,1536]{1,0:T(8,128)(2,1)S(1)} %get-tuple-element.14.refs_4_), channel_id=1, source_target_pairs={{0,448},{64,0},{128,64},{192,128},{256,192},{320,256},{384,320},{4... | collective-permute-start | bytes 1179656 | tf_op jit(solution)/shard_map/ppermute | solution.py:22
  5.1 24.0 %collective-permute-start = (bf16[128,1536]{1,0:T(8,128)(2,1)S(1)}, bf16[128,1536]{1,0:T(8,128)(2,1)S(1)}, u32[]{:S(2)}, u32[]{:S(2)}) collective-permute-start(bf16[128,1536]{1,0:T(8,128)(2,1)S(1)} %get-tuple-element.14.refs_4_), channel_id=1, source_target_pairs={{0,256},{64,320},{128,384},{192,448},{256,0},{320,64},{384,128},{4... | collective-permute-start | bytes 1179656 | tf_op jit(solution)/shard_map/ppermute | solution.py:22
  8.9 25.3 %collective-permute-start.3 = (bf16[128,1536]{1,0:T(8,128)(2,1)S(1)}, bf16[128,1536]{1,0:T(8,128)(2,1)S(1)}, u32[]{:S(2)}, u32[]{:S(2)}) collective-permute-start(bf16[128,1536]{1,0:T(8,128)(2,1)S(1)} %get-tuple-element.13.refs_0_), channel_id=1, source_target_pairs={{0,32},{16,48},{32,0},{48,16},{1,33},{17,49},{33,1},{49,17},{2,34}... | collective-permute-start | bytes 1179656 | tf_op jit(solution)/shard_map/ppermute | solution.py:26
  15.0 21.2 %collective-permute-start.1 = (bf16[128,1536]{1,0:T(8,128)(2,1)S(1)}, bf16[128,1536]{1,0:T(8,128)(2,1)S(1)}, u32[]{:S(2)}, u32[]{:S(2)}) collective-permute-start(bf16[128,1536]{1,0:T(8,128)(2,1)S(1)} %get-tuple-element.13.refs_0_), channel_id=1, source_target_pairs={{0,16},{16,0},{32,48},{48,32},{1,17},{17,1},{33,49},{49,33},{2,18}... | collective-permute-start | bytes 1179656 | tf_op jit(solution)/shard_map/ppermute | solution.py:26
  19.3 26.7 %collective-permute-start.7 = (bf16[128,1536]{1,0:T(8,128)(2,1)S(1)}, bf16[128,1536]{1,0:T(8,128)(2,1)S(1)}, u32[]{:S(2)}, u32[]{:S(2)}) collective-permute-start(bf16[128,1536]{1,0:T(8,128)(2,1)S(1)} %get-tuple-element.14.refs_4_), channel_id=1, source_target_pairs={{0,8},{8,0},{1,9},{9,1},{2,10},{10,2},{3,11},{11,3},{4,12},{12,4},... | collective-permute-start | bytes 1179656 | tf_op jit(solution)/shard_map/ppermute | solution.py:30
  27.2 20.9 %collective-permute-start.5 = (bf16[128,1536]{1,0:T(8,128)(2,1)S(1)}, bf16[128,1536]{1,0:T(8,128)(2,1)S(1)}, u32[]{:S(2)}, u32[]{:S(2)}) collective-permute-start(bf16[128,1536]{1,0:T(8,128)(2,1)S(1)} %collective-permute-done.2.refs_5_), channel_id=1, source_target_pairs={{0,448},{64,0},{128,64},{192,128},{256,192},{320,256},{384,320},{4... | collective-permute-start | bytes 1179656 | tf_op jit(solution)/shard_map/ppermute | solution.py:22
  29.2 21.2 %collective-permute-start.6 = (bf16[128,1536]{1,0:T(8,128)(2,1)S(1)}, bf16[128,1536]{1,0:T(8,128)(2,1)S(1)}, u32[]{:S(2)}, u32[]{:S(2)}) collective-permute-start(bf16[128,1536]{1,0:T(8,128)(2,1)S(1)} %collective-permute-done.refs_8_), channel_id=1, source_target_pairs={{0,64},{64,128},{128,192},{192,256},{256,320},{320,384},{384,448},... | collective-permute-start | bytes 1179656 | tf_op jit(solution)/shard_map/ppermute | solution.py:22
  34.3 18.3 %collective-permute-start.8 = (bf16[128,1536]{1,0:T(8,128)(2,1)S(1)}, bf16[128,1536]{1,0:T(8,128)(2,1)}, u32[]{:S(2)}, u32[]{:S(2)}) collective-permute-start(bf16[128,1536]{1,0:T(8,128)(2,1)S(1)} %collective-permute-done.2.refs_5_), channel_id=1, source_target_pairs={{0,8},{8,0},{1,9},{9,1},{2,10},{10,2},{3,11},{11,3},{4,12},{12,4},... | collective-permute-start | bytes 1179656 | tf_op jit(solution)/shard_map/ppermute | solution.py:30
  36.2 19.6 %collective-permute-start.4 = (bf16[128,1536]{1,0:T(8,128)(2,1)S(1)}, bf16[128,1536]{1,0:T(8,128)(2,1)}, u32[]{:S(2)}, u32[]{:S(2)}) collective-permute-start(bf16[128,1536]{1,0:T(8,128)(2,1)S(1)} %collective-permute-done.3.refs_2_), channel_id=1, source_target_pairs={{0,16},{16,0},{32,48},{48,32},{1,17},{17,1},{33,49},{49,33},{2,18}... | collective-permute-start | bytes 1179656 | tf_op jit(solution)/shard_map/ppermute | solution.py:26
  46.0 9.9 %collective-permute-start.11 = (bf16[128,1536]{1,0:T(8,128)(2,1)S(1)}, bf16[128,1536]{1,0:T(8,128)(2,1)}, u32[]{:S(2)}, u32[]{:S(2)}) collective-permute-start(bf16[128,1536]{1,0:T(8,128)(2,1)S(1)} %collective-permute-done.refs_8_), channel_id=1, source_target_pairs={{0,8},{8,0},{1,9},{9,1},{2,10},{10,2},{3,11},{11,3},{4,12},{12,4},... | collective-permute-start | bytes 1179656 | tf_op jit(solution)/shard_map/ppermute | solution.py:30
  48.1 7.7 %collective-permute-start.9 = (bf16[128,1536]{1,0:T(8,128)(2,1)S(1)}, bf16[128,1536]{1,0:T(8,128)(2,1)}, u32[]{:S(2)}, u32[]{:S(2)}) collective-permute-start(bf16[128,1536]{1,0:T(8,128)(2,1)S(1)} %collective-permute-done.5.refs_6_), channel_id=1, source_target_pairs={{0,8},{8,0},{1,9},{9,1},{2,10},{10,2},{3,11},{11,3},{4,12},{12,4},... | collective-permute-start | bytes 1179656 | tf_op jit(solution)/shard_map/ppermute | solution.py:30
  50.4 5.5 %collective-permute-start.10 = (bf16[128,1536]{1,0:T(8,128)(2,1)S(1)}, bf16[128,1536]{1,0:T(8,128)(2,1)}, u32[]{:S(2)}, u32[]{:S(2)}) collective-permute-start(bf16[128,1536]{1,0:T(8,128)(2,1)S(1)} %collective-permute-done.6.refs_7_), channel_id=1, source_target_pairs={{0,8},{8,0},{1,9},{9,1},{2,10},{10,2},{3,11},{11,3},{4,12},{12,4},... | collective-permute-start | bytes 1179656 | tf_op jit(solution)/shard_map/ppermute | solution.py:30

commit v6 on v5

--- a/solution.py
+++ b/solution.py
@@ -120,9 +120,9 @@
     r1, r4 = ahead(masked, 1), ahead(masked, 4)
     z2, z1 = across(weighted, 2), across(weighted, 1)
     r2 = ahead(r1, 1)
-    r4t, z1 = tie((r4, z1))
+    r1t, z1 = tie((r1, z1))
     r3 = ahead(r4, -1)
-    r1t, z2 = tie((r1, z2))
+    r4t, z2 = tie((r4, z2))
     z3 = across(z2, 1)
     lefts = [weighted, z1, z2, z3]
     rights = [masked, r1, r2, r3, r4]

time: 102 us -> 102 us (level); the launches traced: 101 us -> 100 us
  starting transfers between devices: 44.5 us -> 35.6 us
  waiting for transfers between devices: 9.26 us -> 15.5 us
  blocking collectives: 39.8 us -> 41.4 us
    ppermute x4, waiting for transfers between devices: 5.97 us -> 13.6 us  [ahead(): lax.ppermute(block, 'y', [(i, (i - by) % SIZES['y']) for i in range(SIZES...]
    ppermute x3, starting transfers between devices: 20.1 us -> 14.7 us  [across(): lax.ppermute(block, 'zl', [(i, i ^ flip) for i in range(SIZES['zl'])])]
    ppermute x4, starting transfers between devices: 14.1 us -> 10.9 us  [ahead(): lax.ppermute(block, 'y', [(i, (i - by) % SIZES['y']) for i in range(SIZES...]
    all_to_all x1, blocking collectives: 19.8 us -> 21.4 us  [on_device(): shares = lax.all_to_all(sums, ('zl', 'zh'), 0, 0, tiled=True)]
    ppermute x3, waiting for transfers between devices: 3.28 us -> 1.9 us  [across(): lax.ppermute(block, 'zl', [(i, i ^ flip) for i in range(SIZES['zl'])])]
  transfers between devices with their start and end apart: 12 -> 12, of which waited for: 2 -> 4; matrix products, arithmetic and copies ran while one was open for 0% -> 0% of each run, Pallas kernels for 0% -> 0%
where the time goes in v6:
time: 102 us; the launch traced here: 100 us
  blocking collectives  41.4 us (41%)
  starting transfers between devices  35.6 us (35%)
  waiting for transfers between devices  15.5 us (15%)
  Pallas kernels  5.41 us (5%)
  other arithmetic  1.27 us (1%)
    all_to_all x1, blocking collectives, on_device(): shares = lax.all_to_all(sums, ('zl', 'zh'), 0, 0, tiled=True)  21.4 us
    all_to_all x1, blocking collectives, on_device(): parts = lax.all_to_all(tiles, 'x', 0, 0, tiled=True)  20 us
    ppermute x3, starting transfers between devices, across(): lax.ppermute(block, 'zl', [(i, i ^ flip) for i in range(SIZES['zl'])])  14.7 us
    ppermute x4, waiting for transfers between devices, ahead(): lax.ppermute(block, 'y', [(i, (i - by) % SIZES['y']) for i in range(SIZES...  13.6 us
    ppermute x4, starting transfers between devices, ahead(): lax.ppermute(block, 'y', [(i, (i - by) % SIZES['y']) for i in range(SIZES...  10.9 us
    ppermute x5, starting transfers between devices, swapped(): return lax.ppermute(block, 'core', [(0, 1), (1, 0)])  10.1 us
    pallas_call x1, Pallas kernels, on_device(): pl.pallas_call(tiles_kernel, out_shape=jax.ShapeDtypeStruct((SIZES['x'],...  3.96 us
  transfers between devices with their start and end apart: 12, of which 4 were waited for; matrix products, arithmetic and copies ran while one was open for 0% of the time, Pallas kernels for 0%

profile of v6, /device:TPU:56, one launch (start us, length us, event | category | flops | bytes accessed | tf_op | source)
XLA Modules:
  0.0 100.0 jit_solution(820601868468608474)
XLA Ops:
  0.7 1.2 %multiply_convert_fusion = (bf16[128,1536]{1,0:T(8,128)(2,1)S(1)}, bf16[128,1536]{1,0:T(8,128)(2,1)S(1)}) fusion(f32[1536]{0:T(1024)} %param.5, bf16[128,1536]{1,0:T(8,128)(2,1)} %param.3, pred[128]{0:T(512)(128)(4,1)S(1)} %iota_compare_fusion), kind=kLoop, calls=%fused_computation | loop fusion | flops 786432 | bytes 1185920 | tf_op jit(solution)/shard_map/convert_element_type | solution.py:116
  1.9 4.7 %collective-permute-start.2 = (bf16[128,1536]{1,0:T(8,128)(2,1)S(1)}, bf16[128,1536]{1,0:T(8,128)(2,1)S(1)}, u32[]{:S(2)}, u32[]{:S(2)}) collective-permute-start(bf16[128,1536]{1,0:T(8,128)(2,1)S(1)} %get-tuple-element.14.refs_4_), channel_id=1, source_target_pairs={{0,256},{64,320},{128,384},{192,448},{256,0},{320,64},{384,128},{4... | collective-permute-start | bytes 1179656 | tf_op jit(solution)/shard_map/ppermute | solution.py:22
  6.6 2.4 %collective-permute-start = (bf16[128,1536]{1,0:T(8,128)(2,1)S(1)}, bf16[128,1536]{1,0:T(8,128)(2,1)S(1)}, u32[]{:S(2)}, u32[]{:S(2)}) collective-permute-start(bf16[128,1536]{1,0:T(8,128)(2,1)S(1)} %get-tuple-element.14.refs_4_), channel_id=1, source_target_pairs={{0,448},{64,0},{128,64},{192,128},{256,192},{320,256},{384,320},{4... | collective-permute-start | bytes 1179656 | tf_op jit(solution)/shard_map/ppermute | solution.py:22
  8.9 6.1 %collective-permute-start.3 = (bf16[128,1536]{1,0:T(8,128)(2,1)S(1)}, bf16[128,1536]{1,0:T(8,128)(2,1)S(1)}, u32[]{:S(2)}, u32[]{:S(2)}) collective-permute-start(bf16[128,1536]{1,0:T(8,128)(2,1)S(1)} %get-tuple-element.13.refs_0_), channel_id=1, source_target_pairs={{0,32},{16,48},{32,0},{48,16},{1,33},{17,49},{33,1},{49,17},{2,34}... | collective-permute-start | bytes 1179656 | tf_op jit(solution)/shard_map/ppermute | solution.py:26
  15.0 4.3 %collective-permute-start.1 = (bf16[128,1536]{1,0:T(8,128)(2,1)S(1)}, bf16[128,1536]{1,0:T(8,128)(2,1)S(1)}, u32[]{:S(2)}, u32[]{:S(2)}) collective-permute-start(bf16[128,1536]{1,0:T(8,128)(2,1)S(1)} %get-tuple-element.13.refs_0_), channel_id=1, source_target_pairs={{0,16},{16,0},{32,48},{48,32},{1,17},{17,1},{33,49},{49,33},{2,18}... | collective-permute-start | bytes 1179656 | tf_op jit(solution)/shard_map/ppermute | solution.py:26
  19.3 1.9 %collective-permute-start.7 = (bf16[128,1536]{1,0:T(8,128)(2,1)S(1)}, bf16[128,1536]{1,0:T(8,128)(2,1)S(1)}, u32[]{:S(2)}, u32[]{:S(2)}) collective-permute-start(bf16[128,1536]{1,0:T(8,128)(2,1)S(1)} %get-tuple-element.14.refs_4_), channel_id=1, source_target_pairs={{0,8},{8,0},{1,9},{9,1},{2,10},{10,2},{3,11},{11,3},{4,12},{12,4},... | collective-permute-start | bytes 1179656 | tf_op jit(solution)/shard_map/ppermute | solution.py:30
  21.3 6.0 %collective-permute-done.2.refs_8_ = bf16[128,1536]{1,0:T(8,128)(2,1)S(1)} collective-permute-done((bf16[128,1536]{1,0:T(8,128)(2,1)S(1)}, bf16[128,1536]{1,0:T(8,128)(2,1)S(1)}, u32[]{:S(2)}, u32[]{:S(2)}) %collective-permute-start.2) | collective-permute-done | bytes 393248 | tf_op jit(solution)/shard_map/ppermute | solution.py:22
  27.3 1.9 %collective-permute-start.6 = (bf16[128,1536]{1,0:T(8,128)(2,1)S(1)}, bf16[128,1536]{1,0:T(8,128)(2,1)S(1)}, u32[]{:S(2)}, u32[]{:S(2)}) collective-permute-start(bf16[128,1536]{1,0:T(8,128)(2,1)S(1)} %collective-permute-done.2.refs_8_), channel_id=1, source_target_pairs={{0,64},{64,128},{128,192},{192,256},{256,320},{320,384},{384,448},... | collective-permute-start | bytes 1179656 | tf_op jit(solution)/shard_map/ppermute | solution.py:22
  29.2 5.9 %collective-permute-done.refs_5_ = bf16[128,1536]{1,0:T(8,128)(2,1)S(1)} collective-permute-done((bf16[128,1536]{1,0:T(8,128)(2,1)S(1)}, bf16[128,1536]{1,0:T(8,128)(2,1)S(1)}, u32[]{:S(2)}, u32[]{:S(2)}) %collective-permute-start) | collective-permute-done | bytes 393248 | tf_op jit(solution)/shard_map/ppermute | solution.py:22
  35.1 1.9 %collective-permute-start.5 = (bf16[128,1536]{1,0:T(8,128)(2,1)S(1)}, bf16[128,1536]{1,0:T(8,128)(2,1)S(1)}, u32[]{:S(2)}, u32[]{:S(2)}) collective-permute-start(bf16[128,1536]{1,0:T(8,128)(2,1)S(1)} %collective-permute-done.refs_5_), channel_id=1, source_target_pairs={{0,448},{64,0},{128,64},{192,128},{256,192},{320,256},{384,320},{4... | collective-permute-start | bytes 1179656 | tf_op jit(solution)/shard_map/ppermute | solution.py:22
  37.1 0.0 collective-permute-done.3.refs_2_
  37.1 1.9 %collective-permute-start.11 = (bf16[128,1536]{1,0:T(8,128)(2,1)S(1)}, bf16[128,1536]{1,0:T(8,128)(2,1)}, u32[]{:S(2)}, u32[]{:S(2)}) collective-permute-start(bf16[128,1536]{1,0:T(8,128)(2,1)S(1)} %collective-permute-done.2.refs_8_), channel_id=1, source_target_pairs={{0,8},{8,0},{1,9},{9,1},{2,10},{10,2},{3,11},{11,3},{4,12},{12,4},... | collective-permute-start | bytes 1179656 | tf_op jit(solution)/shard_map/ppermute | solution.py:30
  39.0 0.0 collective-permute-done.1.refs_1_
  39.0 4.3 %collective-permute-start.4 = (bf16[128,1536]{1,0:T(8,128)(2,1)S(1)}, bf16[128,1536]{1,0:T(8,128)(2,1)}, u32[]{:S(2)}, u32[]{:S(2)}) collective-permute-start(bf16[128,1536]{1,0:T(8,128)(2,1)S(1)} %collective-permute-done.3.refs_2_), channel_id=1, source_target_pairs={{0,16},{16,0},{32,48},{48,32},{1,17},{17,1},{33,49},{49,33},{2,18}... | collective-permute-start | bytes 1179656 | tf_op jit(solution)/shard_map/ppermute | solution.py:26
  43.3 0.0 collective-permute-done.7.refs_9_
  43.3 2.1 %collective-permute-start.8 = (bf16[128,1536]{1,0:T(8,128)(2,1)S(1)}, bf16[128,1536]{1,0:T(8,128)(2,1)}, u32[]{:S(2)}, u32[]{:S(2)}) collective-permute-start(bf16[128,1536]{1,0:T(8,128)(2,1)S(1)} %collective-permute-done.refs_5_), channel_id=1, source_target_pairs={{0,8},{8,0},{1,9},{9,1},{2,10},{10,2},{3,11},{11,3},{4,12},{12,4},... | collective-permute-start | bytes 1179656 | tf_op jit(solution)/shard_map/ppermute | solution.py:30
  45.4 0.0 collective-permute-done.6.refs_7_
  45.5 2.2 %collective-permute-start.10 = (bf16[128,1536]{1,0:T(8,128)(2,1)S(1)}, bf16[128,1536]{1,0:T(8,128)(2,1)}, u32[]{:S(2)}, u32[]{:S(2)}) collective-permute-start(bf16[128,1536]{1,0:T(8,128)(2,1)S(1)} %collective-permute-done.6.refs_7_), channel_id=1, source_target_pairs={{0,8},{8,0},{1,9},{9,1},{2,10},{10,2},{3,11},{11,3},{4,12},{12,4},... | collective-permute-start | bytes 1179656 | tf_op jit(solution)/shard_map/ppermute | solution.py:30
  47.7 1.6 %collective-permute-done.5.refs_6_ = bf16[128,1536]{1,0:T(8,128)(2,1)S(1)} collective-permute-done((bf16[128,1536]{1,0:T(8,128)(2,1)S(1)}, bf16[128,1536]{1,0:T(8,128)(2,1)S(1)}, u32[]{:S(2)}, u32[]{:S(2)}) %collective-permute-start.5) | collective-permute-done | bytes 393248 | tf_op jit(solution)/shard_map/ppermute | solution.py:22
  49.3 1.9 %collective-permute-start.9 = (bf16[128,1536]{1,0:T(8,128)(2,1)S(1)}, bf16[128,1536]{1,0:T(8,128)(2,1)}, u32[]{:S(2)}, u32[]{:S(2)}) collective-permute-start(bf16[128,1536]{1,0:T(8,128)(2,1)S(1)} %collective-permute-done.5.refs_6_), channel_id=1, source_target_pairs={{0,8},{8,0},{1,9},{9,1},{2,10},{10,2},{3,11},{11,3},{4,12},{12,4},... | collective-permute-start | bytes 1179656 | tf_op jit(solution)/shard_map/ppermute | solution.py:30
  51.2 0.1 pad_add_fusion.place_ref
  51.3 0.0 collective-permute-done.11.refs_13_
  51.3 1.9 %collective-permute-done.4.refs_3_ = bf16[128,1536]{1,0:T(8,128)(2,1)} collective-permute-done((bf16[128,1536]{1,0:T(8,128)(2,1)S(1)}, bf16[128,1536]{1,0:T(8,128)(2,1)}, u32[]{:S(2)}, u32[]{:S(2)}) %collective-permute-start.4) | collective-permute-done | bytes 393248 | tf_op jit(solution)/shard_map/ppermute | solution.py:26
  53.2 0.0 collective-permute-done.8.refs_10_
  53.2 0.0 collective-permute-done.10.refs_12_
  53.2 0.0 collective-permute-done.9.refs_11_
  53.2 4.0 %shard_map.37 = bf16[4,34,32,128]{3,2,1,0:T(8,128)(2,1)S(1)} custom-call(s32[2]{0:T(128)S(1)} %pad_add_fusion.place_ref, bf16[128,1536]{1,0:T(8,128)(2,1)S(1)} %get-tuple-element.13.refs_0_, bf16[128,1536]{1,0:T(8,128)(2,1)S(1)} %collective-permute-done.1.refs_1_, bf16[128,1536]{1,0:T(8,128)(2,1)S(1)} %collective-permute-done.3.refs_2_, ...), custom_call_target="tpu_custom_call" | custom-call | tf_op jit(solution)/shard_map/pallas_call | solution.py:132
  57.1 20.0 %all_to_all.10.parts_ref = bf16[4,34,32,128]{3,2,1,0:T(8,128)(2,1)S(1)} all-to-all(bf16[4,34,32,128]{3,2,1,0:T(8,128)(2,1)S(1)} %shard_map.37), channel_id=1, replica_groups=mesh['y'=8,'zl'=4,'core'=2,'x'=4,'zh'=2] {'x'}, dimensions={0} | all-to-all | bytes 2228224 | tf_op jit(solution)/shard_map/all_to_all | solution.py:144
  77.2 0.1 shard_map.38
  77.3 21.4 %all_to_all.11.parts_ref = bf16[8,10,16,128]{3,2,1,0:T(8,128)(2,1)S(1)} all-to-all(bf16[8,10,16,128]{3,2,1,0:T(8,128)(2,1)S(1)} %shard_map.38), channel_id=1, replica_groups=mesh['y'=8,'zl'=4,'core'=2,'x'=4,'zh'=2] {'zl','zh'}, dimensions={0} | all-to-all | bytes 655360 | tf_op jit(solution)/shard_map/all_to_all | solution.py:152
  98.7 1.3 %shard_map.39 = f32[1,33,16,128]{3,2,1,0:T(8,128)} custom-call(s32[2]{0:T(128)S(1)} %pad_add_fusion.place_ref, bf16[8,10,16,128]{3,2,1,0:T(8,128)(2,1)S(1)} %all_to_all.11.parts_ref), custom_call_target="tpu_custom_call" | custom-call | tf_op jit(solution)/shard_map/pallas_call | solution.py:154
  (1 shorter events, 0.0 us)
Async XLA Ops:
  1.9 25.4 %collective-permute-start.2 = (bf16[128,1536]{1,0:T(8,128)(2,1)S(1)}, bf16[128,1536]{1,0:T(8,128)(2,1)S(1)}, u32[]{:S(2)}, u32[]{:S(2)}) collective-permute-start(bf16[128,1536]{1,0:T(8,128)(2,1)S(1)} %get-tuple-element.14.refs_4_), channel_id=1, source_target_pairs={{0,256},{64,320},{128,384},{192,448},{256,0},{320,64},{384,128},{4... | collective-permute-start | bytes 1179656 | tf_op jit(solution)/shard_map/ppermute | solution.py:22
  6.6 28.6 %collective-permute-start = (bf16[128,1536]{1,0:T(8,128)(2,1)S(1)}, bf16[128,1536]{1,0:T(8,128)(2,1)S(1)}, u32[]{:S(2)}, u32[]{:S(2)}) collective-permute-start(bf16[128,1536]{1,0:T(8,128)(2,1)S(1)} %get-tuple-element.14.refs_4_), channel_id=1, source_target_pairs={{0,448},{64,0},{128,64},{192,128},{256,192},{320,256},{384,320},{4... | collective-permute-start | bytes 1179656 | tf_op jit(solution)/shard_map/ppermute | solution.py:22
  8.9 28.1 %collective-permute-start.3 = (bf16[128,1536]{1,0:T(8,128)(2,1)S(1)}, bf16[128,1536]{1,0:T(8,128)(2,1)S(1)}, u32[]{:S(2)}, u32[]{:S(2)}) collective-permute-start(bf16[128,1536]{1,0:T(8,128)(2,1)S(1)} %get-tuple-element.13.refs_0_), channel_id=1, source_target_pairs={{0,32},{16,48},{32,0},{48,16},{1,33},{17,49},{33,1},{49,17},{2,34}... | collective-permute-start | bytes 1179656 | tf_op jit(solution)/shard_map/ppermute | solution.py:26
  15.0 24.0 %collective-permute-start.1 = (bf16[128,1536]{1,0:T(8,128)(2,1)S(1)}, bf16[128,1536]{1,0:T(8,128)(2,1)S(1)}, u32[]{:S(2)}, u32[]{:S(2)}) collective-permute-start(bf16[128,1536]{1,0:T(8,128)(2,1)S(1)} %get-tuple-element.13.refs_0_), channel_id=1, source_target_pairs={{0,16},{16,0},{32,48},{48,32},{1,17},{17,1},{33,49},{49,33},{2,18}... | collective-permute-start | bytes 1179656 | tf_op jit(solution)/shard_map/ppermute | solution.py:26
  19.3 24.0 %collective-permute-start.7 = (bf16[128,1536]{1,0:T(8,128)(2,1)S(1)}, bf16[128,1536]{1,0:T(8,128)(2,1)S(1)}, u32[]{:S(2)}, u32[]{:S(2)}) collective-permute-start(bf16[128,1536]{1,0:T(8,128)(2,1)S(1)} %get-tuple-element.14.refs_4_), channel_id=1, source_target_pairs={{0,8},{8,0},{1,9},{9,1},{2,10},{10,2},{3,11},{11,3},{4,12},{12,4},... | collective-permute-start | bytes 1179656 | tf_op jit(solution)/shard_map/ppermute | solution.py:30
  27.3 18.2 %collective-permute-start.6 = (bf16[128,1536]{1,0:T(8,128)(2,1)S(1)}, bf16[128,1536]{1,0:T(8,128)(2,1)S(1)}, u32[]{:S(2)}, u32[]{:S(2)}) collective-permute-start(bf16[128,1536]{1,0:T(8,128)(2,1)S(1)} %collective-permute-done.2.refs_8_), channel_id=1, source_target_pairs={{0,64},{64,128},{128,192},{192,256},{256,320},{320,384},{384,448},... | collective-permute-start | bytes 1179656 | tf_op jit(solution)/shard_map/ppermute | solution.py:22
  35.1 14.1 %collective-permute-start.5 = (bf16[128,1536]{1,0:T(8,128)(2,1)S(1)}, bf16[128,1536]{1,0:T(8,128)(2,1)S(1)}, u32[]{:S(2)}, u32[]{:S(2)}) collective-permute-start(bf16[128,1536]{1,0:T(8,128)(2,1)S(1)} %collective-permute-done.refs_5_), channel_id=1, source_target_pairs={{0,448},{64,0},{128,64},{192,128},{256,192},{320,256},{384,320},{4... | collective-permute-start | bytes 1179656 | tf_op jit(solution)/shard_map/ppermute | solution.py:22
  37.1 14.2 %collective-permute-start.11 = (bf16[128,1536]{1,0:T(8,128)(2,1)S(1)}, bf16[128,1536]{1,0:T(8,128)(2,1)}, u32[]{:S(2)}, u32[]{:S(2)}) collective-permute-start(bf16[128,1536]{1,0:T(8,128)(2,1)S(1)} %collective-permute-done.2.refs_8_), channel_id=1, source_target_pairs={{0,8},{8,0},{1,9},{9,1},{2,10},{10,2},{3,11},{11,3},{4,12},{12,4},... | collective-permute-start | bytes 1179656 | tf_op jit(solution)/shard_map/ppermute | solution.py:30
  39.0 14.2 %collective-permute-start.4 = (bf16[128,1536]{1,0:T(8,128)(2,1)S(1)}, bf16[128,1536]{1,0:T(8,128)(2,1)}, u32[]{:S(2)}, u32[]{:S(2)}) collective-permute-start(bf16[128,1536]{1,0:T(8,128)(2,1)S(1)} %collective-permute-done.3.refs_2_), channel_id=1, source_target_pairs={{0,16},{16,0},{32,48},{48,32},{1,17},{17,1},{33,49},{49,33},{2,18}... | collective-permute-start | bytes 1179656 | tf_op jit(solution)/shard_map/ppermute | solution.py:26
  43.3 9.9 %collective-permute-start.8 = (bf16[128,1536]{1,0:T(8,128)(2,1)S(1)}, bf16[128,1536]{1,0:T(8,128)(2,1)}, u32[]{:S(2)}, u32[]{:S(2)}) collective-permute-start(bf16[128,1536]{1,0:T(8,128)(2,1)S(1)} %collective-permute-done.refs_5_), channel_id=1, source_target_pairs={{0,8},{8,0},{1,9},{9,1},{2,10},{10,2},{3,11},{11,3},{4,12},{12,4},... | collective-permute-start | bytes 1179656 | tf_op jit(solution)/shard_map/ppermute | solution.py:30
  45.5 7.7 %collective-permute-start.10 = (bf16[128,1536]{1,0:T(8,128)(2,1)S(1)}, bf16[128,1536]{1,0:T(8,128)(2,1)}, u32[]{:S(2)}, u32[]{:S(2)}) collective-permute-start(bf16[128,1536]{1,0:T(8,128)(2,1)S(1)} %collective-permute-done.6.refs_7_), channel_id=1, source_target_pairs={{0,8},{8,0},{1,9},{9,1},{2,10},{10,2},{3,11},{11,3},{4,12},{12,4},... | collective-permute-start | bytes 1179656 | tf_op jit(solution)/shard_map/ppermute | solution.py:30
  49.3 3.9 %collective-permute-start.9 = (bf16[128,1536]{1,0:T(8,128)(2,1)S(1)}, bf16[128,1536]{1,0:T(8,128)(2,1)}, u32[]{:S(2)}, u32[]{:S(2)}) collective-permute-start(bf16[128,1536]{1,0:T(8,128)(2,1)S(1)} %collective-permute-done.5.refs_6_), channel_id=1, source_target_pairs={{0,8},{8,0},{1,9},{9,1},{2,10},{10,2},{3,11},{11,3},{4,12},{12,4},... | collective-permute-start | bytes 1179656 | tf_op jit(solution)/shard_map/ppermute | solution.py:30

commit v7 on v5

--- a/solution.py
+++ b/solution.py
@@ -49,7 +49,9 @@
     for ref in ins[4:]:
         right_all[at : at + ref.shape[0]] = ref[...]
         at += ref.shape[0]
-    dots[...] = product(left_all[...], right_all[...])
+    half = (FAR + 1) * rows
+    dots[:, :half] = product(left_all[...], right_all[:half])
+    dots[:, half:] = product(left_all[...], right_all[half:])
     own = dots[:rows, :rows]
     high = own.astype(jnp.bfloat16)
     low = (own - high.astype(jnp.float32)).astype(jnp.bfloat16)

time: 102 us -> 102 us (level)
  no operation moved by 1% of the time
where the time goes in v7:
time: 102 us; the launch traced here: 101 us
  starting transfers between devices  44.5 us (44%)
  blocking collectives  39.8 us (39%)
  waiting for transfers between devices  9.26 us (9%)
  Pallas kernels  5.8 us (6%)
  other arithmetic  1.27 us (1%)
    ppermute x3, starting transfers between devices, across(): lax.ppermute(block, 'zl', [(i, i ^ flip) for i in range(SIZES['zl'])])  20.1 us
    all_to_all x1, blocking collectives, on_device(): parts = lax.all_to_all(tiles, 'x', 0, 0, tiled=True)  20 us
    all_to_all x1, blocking collectives, on_device(): shares = lax.all_to_all(sums, ('zl', 'zh'), 0, 0, tiled=True)  19.8 us
    ppermute x4, starting transfers between devices, ahead(): lax.ppermute(block, 'y', [(i, (i - by) % SIZES['y']) for i in range(SIZES...  14.1 us
    ppermute x5, starting transfers between devices, swapped(): return lax.ppermute(block, 'core', [(0, 1), (1, 0)])  10.3 us
    ppermute x4, waiting for transfers between devices, ahead(): lax.ppermute(block, 'y', [(i, (i - by) % SIZES['y']) for i in range(SIZES...  5.97 us
    pallas_call x1, Pallas kernels, on_device(): pl.pallas_call(tiles_kernel, out_shape=jax.ShapeDtypeStruct((SIZES['x'],...  4.36 us
    ppermute x3, waiting for transfers between devices, across(): lax.ppermute(block, 'zl', [(i, i ^ flip) for i in range(SIZES['zl'])])  3.28 us
  transfers between devices with their start and end apart: 12, of which 2 were waited for; matrix products, arithmetic and copies ran while one was open for 0% of the time, Pallas kernels for 0%

profile of v7, /device:TPU:56, one launch (start us, length us, event | category | flops | bytes accessed | tf_op | source)
XLA Modules:
  0.0 101.4 jit_solution(14531174290991575930)
XLA Ops:
  0.7 1.2 %multiply_convert_fusion = (bf16[128,1536]{1,0:T(8,128)(2,1)S(1)}, bf16[128,1536]{1,0:T(8,128)(2,1)S(1)}) fusion(f32[1536]{0:T(1024)} %param.5, bf16[128,1536]{1,0:T(8,128)(2,1)} %param.3, pred[128]{0:T(512)(128)(4,1)S(1)} %iota_compare_fusion), kind=kLoop, calls=%fused_computation | loop fusion | flops 786432 | bytes 1185920 | tf_op jit(solution)/shard_map/convert_element_type | solution.py:118
  1.9 3.3 %collective-permute-start.2 = (bf16[128,1536]{1,0:T(8,128)(2,1)S(1)}, bf16[128,1536]{1,0:T(8,128)(2,1)S(1)}, u32[]{:S(2)}, u32[]{:S(2)}) collective-permute-start(bf16[128,1536]{1,0:T(8,128)(2,1)S(1)} %get-tuple-element.14.refs_4_), channel_id=1, source_target_pairs={{0,448},{64,0},{128,64},{192,128},{256,192},{320,256},{384,320},{4... | collective-permute-start | bytes 1179656 | tf_op jit(solution)/shard_map/ppermute | solution.py:22
  5.1 3.8 %collective-permute-start = (bf16[128,1536]{1,0:T(8,128)(2,1)S(1)}, bf16[128,1536]{1,0:T(8,128)(2,1)S(1)}, u32[]{:S(2)}, u32[]{:S(2)}) collective-permute-start(bf16[128,1536]{1,0:T(8,128)(2,1)S(1)} %get-tuple-element.14.refs_4_), channel_id=1, source_target_pairs={{0,256},{64,320},{128,384},{192,448},{256,0},{320,64},{384,128},{4... | collective-permute-start | bytes 1179656 | tf_op jit(solution)/shard_map/ppermute | solution.py:22
  8.9 6.1 %collective-permute-start.3 = (bf16[128,1536]{1,0:T(8,128)(2,1)S(1)}, bf16[128,1536]{1,0:T(8,128)(2,1)S(1)}, u32[]{:S(2)}, u32[]{:S(2)}) collective-permute-start(bf16[128,1536]{1,0:T(8,128)(2,1)S(1)} %get-tuple-element.13.refs_0_), channel_id=1, source_target_pairs={{0,32},{16,48},{32,0},{48,16},{1,33},{17,49},{33,1},{49,17},{2,34}... | collective-permute-start | bytes 1179656 | tf_op jit(solution)/shard_map/ppermute | solution.py:26
  15.0 4.3 %collective-permute-start.1 = (bf16[128,1536]{1,0:T(8,128)(2,1)S(1)}, bf16[128,1536]{1,0:T(8,128)(2,1)S(1)}, u32[]{:S(2)}, u32[]{:S(2)}) collective-permute-start(bf16[128,1536]{1,0:T(8,128)(2,1)S(1)} %get-tuple-element.13.refs_0_), channel_id=1, source_target_pairs={{0,16},{16,0},{32,48},{48,32},{1,17},{17,1},{33,49},{49,33},{2,18}... | collective-permute-start | bytes 1179656 | tf_op jit(solution)/shard_map/ppermute | solution.py:26
  19.3 1.9 %collective-permute-start.7 = (bf16[128,1536]{1,0:T(8,128)(2,1)S(1)}, bf16[128,1536]{1,0:T(8,128)(2,1)S(1)}, u32[]{:S(2)}, u32[]{:S(2)}) collective-permute-start(bf16[128,1536]{1,0:T(8,128)(2,1)S(1)} %get-tuple-element.14.refs_4_), channel_id=1, source_target_pairs={{0,8},{8,0},{1,9},{9,1},{2,10},{10,2},{3,11},{11,3},{4,12},{12,4},... | collective-permute-start | bytes 1179656 | tf_op jit(solution)/shard_map/ppermute | solution.py:30
  21.3 6.0 %collective-permute-done.2.refs_5_ = bf16[128,1536]{1,0:T(8,128)(2,1)S(1)} collective-permute-done((bf16[128,1536]{1,0:T(8,128)(2,1)S(1)}, bf16[128,1536]{1,0:T(8,128)(2,1)S(1)}, u32[]{:S(2)}, u32[]{:S(2)}) %collective-permute-start.2) | collective-permute-done | bytes 393248 | tf_op jit(solution)/shard_map/ppermute | solution.py:22
  27.2 1.9 %collective-permute-start.5 = (bf16[128,1536]{1,0:T(8,128)(2,1)S(1)}, bf16[128,1536]{1,0:T(8,128)(2,1)S(1)}, u32[]{:S(2)}, u32[]{:S(2)}) collective-permute-start(bf16[128,1536]{1,0:T(8,128)(2,1)S(1)} %collective-permute-done.2.refs_5_), channel_id=1, source_target_pairs={{0,448},{64,0},{128,64},{192,128},{256,192},{320,256},{384,320},{4... | collective-permute-start | bytes 1179656 | tf_op jit(solution)/shard_map/ppermute | solution.py:22
  29.1 0.0 collective-permute-done.refs_8_
  29.2 5.1 %collective-permute-start.6 = (bf16[128,1536]{1,0:T(8,128)(2,1)S(1)}, bf16[128,1536]{1,0:T(8,128)(2,1)S(1)}, u32[]{:S(2)}, u32[]{:S(2)}) collective-permute-start(bf16[128,1536]{1,0:T(8,128)(2,1)S(1)} %collective-permute-done.refs_8_), channel_id=1, source_target_pairs={{0,64},{64,128},{128,192},{192,256},{256,320},{320,384},{384,448},... | collective-permute-start | bytes 1179656 | tf_op jit(solution)/shard_map/ppermute | solution.py:22
  34.3 0.0 collective-permute-done.3.refs_2_
  34.3 1.9 %collective-permute-start.8 = (bf16[128,1536]{1,0:T(8,128)(2,1)S(1)}, bf16[128,1536]{1,0:T(8,128)(2,1)}, u32[]{:S(2)}, u32[]{:S(2)}) collective-permute-start(bf16[128,1536]{1,0:T(8,128)(2,1)S(1)} %collective-permute-done.2.refs_5_), channel_id=1, source_target_pairs={{0,8},{8,0},{1,9},{9,1},{2,10},{10,2},{3,11},{11,3},{4,12},{12,4},... | collective-permute-start | bytes 1179656 | tf_op jit(solution)/shard_map/ppermute | solution.py:30
  36.2 0.0 collective-permute-done.1.refs_1_
  36.2 9.7 %collective-permute-start.4 = (bf16[128,1536]{1,0:T(8,128)(2,1)S(1)}, bf16[128,1536]{1,0:T(8,128)(2,1)}, u32[]{:S(2)}, u32[]{:S(2)}) collective-permute-start(bf16[128,1536]{1,0:T(8,128)(2,1)S(1)} %collective-permute-done.3.refs_2_), channel_id=1, source_target_pairs={{0,16},{16,0},{32,48},{48,32},{1,17},{17,1},{33,49},{49,33},{2,18}... | collective-permute-start | bytes 1179656 | tf_op jit(solution)/shard_map/ppermute | solution.py:26
  46.0 0.0 collective-permute-done.7.refs_9_
  46.0 2.1 %collective-permute-start.11 = (bf16[128,1536]{1,0:T(8,128)(2,1)S(1)}, bf16[128,1536]{1,0:T(8,128)(2,1)}, u32[]{:S(2)}, u32[]{:S(2)}) collective-permute-start(bf16[128,1536]{1,0:T(8,128)(2,1)S(1)} %collective-permute-done.refs_8_), channel_id=1, source_target_pairs={{0,8},{8,0},{1,9},{9,1},{2,10},{10,2},{3,11},{11,3},{4,12},{12,4},... | collective-permute-start | bytes 1179656 | tf_op jit(solution)/shard_map/ppermute | solution.py:30
  48.1 0.0 collective-permute-done.5.refs_6_
  48.1 2.2 %collective-permute-start.9 = (bf16[128,1536]{1,0:T(8,128)(2,1)S(1)}, bf16[128,1536]{1,0:T(8,128)(2,1)}, u32[]{:S(2)}, u32[]{:S(2)}) collective-permute-start(bf16[128,1536]{1,0:T(8,128)(2,1)S(1)} %collective-permute-done.5.refs_6_), channel_id=1, source_target_pairs={{0,8},{8,0},{1,9},{9,1},{2,10},{10,2},{3,11},{11,3},{4,12},{12,4},... | collective-permute-start | bytes 1179656 | tf_op jit(solution)/shard_map/ppermute | solution.py:30
  50.3 0.0 collective-permute-done.6.refs_7_
  50.4 2.1 %collective-permute-start.10 = (bf16[128,1536]{1,0:T(8,128)(2,1)S(1)}, bf16[128,1536]{1,0:T(8,128)(2,1)}, u32[]{:S(2)}, u32[]{:S(2)}) collective-permute-start(bf16[128,1536]{1,0:T(8,128)(2,1)S(1)} %collective-permute-done.6.refs_7_), channel_id=1, source_target_pairs={{0,8},{8,0},{1,9},{9,1},{2,10},{10,2},{3,11},{11,3},{4,12},{12,4},... | collective-permute-start | bytes 1179656 | tf_op jit(solution)/shard_map/ppermute | solution.py:30
  52.5 0.1 pad_add_fusion.place_ref
  52.6 0.0 collective-permute-done.8.refs_10_
  52.6 3.3 %collective-permute-done.4.refs_3_ = bf16[128,1536]{1,0:T(8,128)(2,1)} collective-permute-done((bf16[128,1536]{1,0:T(8,128)(2,1)S(1)}, bf16[128,1536]{1,0:T(8,128)(2,1)}, u32[]{:S(2)}, u32[]{:S(2)}) %collective-permute-start.4) | collective-permute-done | bytes 393248 | tf_op jit(solution)/shard_map/ppermute | solution.py:26
  55.8 0.0 collective-permute-done.11.refs_13_
  55.9 0.0 collective-permute-done.9.refs_11_
  55.9 0.0 collective-permute-done.10.refs_12_
  55.9 4.4 %shard_map.37 = bf16[4,34,32,128]{3,2,1,0:T(8,128)(2,1)S(1)} custom-call(s32[2]{0:T(128)S(1)} %pad_add_fusion.place_ref, bf16[128,1536]{1,0:T(8,128)(2,1)S(1)} %get-tuple-element.13.refs_0_, bf16[128,1536]{1,0:T(8,128)(2,1)S(1)} %collective-permute-done.1.refs_1_, bf16[128,1536]{1,0:T(8,128)(2,1)S(1)} %collective-permute-done.3.refs_2_, ...), custom_call_target="tpu_custom_call" | custom-call | tf_op jit(solution)/shard_map/pallas_call | solution.py:134
  60.2 20.0 %all_to_all.10.parts_ref = bf16[4,34,32,128]{3,2,1,0:T(8,128)(2,1)S(1)} all-to-all(bf16[4,34,32,128]{3,2,1,0:T(8,128)(2,1)S(1)} %shard_map.37), channel_id=1, replica_groups=mesh['y'=8,'zl'=4,'core'=2,'x'=4,'zh'=2] {'x'}, dimensions={0} | all-to-all | bytes 2228224 | tf_op jit(solution)/shard_map/all_to_all | solution.py:146
  80.2 0.1 shard_map.38
  80.3 19.8 %all_to_all.11.parts_ref = bf16[8,10,16,128]{3,2,1,0:T(8,128)(2,1)S(1)} all-to-all(bf16[8,10,16,128]{3,2,1,0:T(8,128)(2,1)S(1)} %shard_map.38), channel_id=1, replica_groups=mesh['y'=8,'zl'=4,'core'=2,'x'=4,'zh'=2] {'zl','zh'}, dimensions={0} | all-to-all | bytes 655360 | tf_op jit(solution)/shard_map/all_to_all | solution.py:154
  100.1 1.3 %shard_map.39 = f32[1,33,16,128]{3,2,1,0:T(8,128)} custom-call(s32[2]{0:T(128)S(1)} %pad_add_fusion.place_ref, bf16[8,10,16,128]{3,2,1,0:T(8,128)(2,1)S(1)} %all_to_all.11.parts_ref), custom_call_target="tpu_custom_call" | custom-call | tf_op jit(solution)/shard_map/pallas_call | solution.py:156
  (1 shorter events, 0.0 us)
Async XLA Ops:
  1.9 25.4 %collective-permute-start.2 = (bf16[128,1536]{1,0:T(8,128)(2,1)S(1)}, bf16[128,1536]{1,0:T(8,128)(2,1)S(1)}, u32[]{:S(2)}, u32[]{:S(2)}) collective-permute-start(bf16[128,1536]{1,0:T(8,128)(2,1)S(1)} %get-tuple-element.14.refs_4_), channel_id=1, source_target_pairs={{0,448},{64,0},{128,64},{192,128},{256,192},{320,256},{384,320},{4... | collective-permute-start | bytes 1179656 | tf_op jit(solution)/shard_map/ppermute | solution.py:22
  5.1 24.0 %collective-permute-start = (bf16[128,1536]{1,0:T(8,128)(2,1)S(1)}, bf16[128,1536]{1,0:T(8,128)(2,1)S(1)}, u32[]{:S(2)}, u32[]{:S(2)}) collective-permute-start(bf16[128,1536]{1,0:T(8,128)(2,1)S(1)} %get-tuple-element.14.refs_4_), channel_id=1, source_target_pairs={{0,256},{64,320},{128,384},{192,448},{256,0},{320,64},{384,128},{4... | collective-permute-start | bytes 1179656 | tf_op jit(solution)/shard_map/ppermute | solution.py:22
  8.9 25.3 %collective-permute-start.3 = (bf16[128,1536]{1,0:T(8,128)(2,1)S(1)}, bf16[128,1536]{1,0:T(8,128)(2,1)S(1)}, u32[]{:S(2)}, u32[]{:S(2)}) collective-permute-start(bf16[128,1536]{1,0:T(8,128)(2,1)S(1)} %get-tuple-element.13.refs_0_), channel_id=1, source_target_pairs={{0,32},{16,48},{32,0},{48,16},{1,33},{17,49},{33,1},{49,17},{2,34}... | collective-permute-start | bytes 1179656 | tf_op jit(solution)/shard_map/ppermute | solution.py:26
  15.0 21.2 %collective-permute-start.1 = (bf16[128,1536]{1,0:T(8,128)(2,1)S(1)}, bf16[128,1536]{1,0:T(8,128)(2,1)S(1)}, u32[]{:S(2)}, u32[]{:S(2)}) collective-permute-start(bf16[128,1536]{1,0:T(8,128)(2,1)S(1)} %get-tuple-element.13.refs_0_), channel_id=1, source_target_pairs={{0,16},{16,0},{32,48},{48,32},{1,17},{17,1},{33,49},{49,33},{2,18}... | collective-permute-start | bytes 1179656 | tf_op jit(solution)/shard_map/ppermute | solution.py:26
  19.3 26.7 %collective-permute-start.7 = (bf16[128,1536]{1,0:T(8,128)(2,1)S(1)}, bf16[128,1536]{1,0:T(8,128)(2,1)S(1)}, u32[]{:S(2)}, u32[]{:S(2)}) collective-permute-start(bf16[128,1536]{1,0:T(8,128)(2,1)S(1)} %get-tuple-element.14.refs_4_), channel_id=1, source_target_pairs={{0,8},{8,0},{1,9},{9,1},{2,10},{10,2},{3,11},{11,3},{4,12},{12,4},... | collective-permute-start | bytes 1179656 | tf_op jit(solution)/shard_map/ppermute | solution.py:30
  27.2 20.9 %collective-permute-start.5 = (bf16[128,1536]{1,0:T(8,128)(2,1)S(1)}, bf16[128,1536]{1,0:T(8,128)(2,1)S(1)}, u32[]{:S(2)}, u32[]{:S(2)}) collective-permute-start(bf16[128,1536]{1,0:T(8,128)(2,1)S(1)} %collective-permute-done.2.refs_5_), channel_id=1, source_target_pairs={{0,448},{64,0},{128,64},{192,128},{256,192},{320,256},{384,320},{4... | collective-permute-start | bytes 1179656 | tf_op jit(solution)/shard_map/ppermute | solution.py:22
  29.2 21.2 %collective-permute-start.6 = (bf16[128,1536]{1,0:T(8,128)(2,1)S(1)}, bf16[128,1536]{1,0:T(8,128)(2,1)S(1)}, u32[]{:S(2)}, u32[]{:S(2)}) collective-permute-start(bf16[128,1536]{1,0:T(8,128)(2,1)S(1)} %collective-permute-done.refs_8_), channel_id=1, source_target_pairs={{0,64},{64,128},{128,192},{192,256},{256,320},{320,384},{384,448},... | collective-permute-start | bytes 1179656 | tf_op jit(solution)/shard_map/ppermute | solution.py:22
  34.3 18.3 %collective-permute-start.8 = (bf16[128,1536]{1,0:T(8,128)(2,1)S(1)}, bf16[128,1536]{1,0:T(8,128)(2,1)}, u32[]{:S(2)}, u32[]{:S(2)}) collective-permute-start(bf16[128,1536]{1,0:T(8,128)(2,1)S(1)} %collective-permute-done.2.refs_5_), channel_id=1, source_target_pairs={{0,8},{8,0},{1,9},{9,1},{2,10},{10,2},{3,11},{11,3},{4,12},{12,4},... | collective-permute-start | bytes 1179656 | tf_op jit(solution)/shard_map/ppermute | solution.py:30
  36.2 19.6 %collective-permute-start.4 = (bf16[128,1536]{1,0:T(8,128)(2,1)S(1)}, bf16[128,1536]{1,0:T(8,128)(2,1)}, u32[]{:S(2)}, u32[]{:S(2)}) collective-permute-start(bf16[128,1536]{1,0:T(8,128)(2,1)S(1)} %collective-permute-done.3.refs_2_), channel_id=1, source_target_pairs={{0,16},{16,0},{32,48},{48,32},{1,17},{17,1},{33,49},{49,33},{2,18}... | collective-permute-start | bytes 1179656 | tf_op jit(solution)/shard_map/ppermute | solution.py:26
  46.0 9.9 %collective-permute-start.11 = (bf16[128,1536]{1,0:T(8,128)(2,1)S(1)}, bf16[128,1536]{1,0:T(8,128)(2,1)}, u32[]{:S(2)}, u32[]{:S(2)}) collective-permute-start(bf16[128,1536]{1,0:T(8,128)(2,1)S(1)} %collective-permute-done.refs_8_), channel_id=1, source_target_pairs={{0,8},{8,0},{1,9},{9,1},{2,10},{10,2},{3,11},{11,3},{4,12},{12,4},... | collective-permute-start | bytes 1179656 | tf_op jit(solution)/shard_map/ppermute | solution.py:30
  48.1 7.7 %collective-permute-start.9 = (bf16[128,1536]{1,0:T(8,128)(2,1)S(1)}, bf16[128,1536]{1,0:T(8,128)(2,1)}, u32[]{:S(2)}, u32[]{:S(2)}) collective-permute-start(bf16[128,1536]{1,0:T(8,128)(2,1)S(1)} %collective-permute-done.5.refs_6_), channel_id=1, source_target_pairs={{0,8},{8,0},{1,9},{9,1},{2,10},{10,2},{3,11},{11,3},{4,12},{12,4},... | collective-permute-start | bytes 1179656 | tf_op jit(solution)/shard_map/ppermute | solution.py:30
  50.4 5.5 %collective-permute-start.10 = (bf16[128,1536]{1,0:T(8,128)(2,1)S(1)}, bf16[128,1536]{1,0:T(8,128)(2,1)}, u32[]{:S(2)}, u32[]{:S(2)}) collective-permute-start(bf16[128,1536]{1,0:T(8,128)(2,1)S(1)} %collective-permute-done.6.refs_7_), channel_id=1, source_target_pairs={{0,8},{8,0},{1,9},{9,1},{2,10},{10,2},{3,11},{11,3},{4,12},{12,4},... | collective-permute-start | bytes 1179656 | tf_op jit(solution)/shard_map/ppermute | solution.py:30
